TPU v7x, 32 devices: a whole 2x2x4 slice. The times are simulated.
32 devices in a mesh: shard: 8 (over y, x, core), ctx: 4 (over z).
Axes of the slice: x: 2, y: 2, z: 4, core: 2. Of those that a mesh axis runs over, the one named last changes fastest.
Arguments:
- tokens: bfloat16 [12288, 1600], P(('shard', 'ctx')), may hold values from -6 to 6
- cotangent: bfloat16 [12288, 1600], P(('shard', 'ctx')), may hold values from -12 to 12
- master_qkv: float32 [1600, 4800], P('shard', 'ctx'), may hold values from -0.15625 to 0.15625
- master_out: float32 [1600, 1600], P('shard', 'ctx'), may hold values from -2.5 to 2.5
- master_fc: float32 [1600, 6400], P('shard', 'ctx'), may hold values from -0.15625 to 0.15625
- master_proj: float32 [6400, 1600], P('shard', 'ctx'), may hold values from -0.078125 to 0.078125
- master_small: float32 [12, 1600], P(None, 'shard'), may hold values from -0.6 to 1.5, as said below
- first_qkv: float32 [1600, 4800], P('shard', 'ctx'), may hold values from -64 to 64
- first_out: float32 [1600, 1600], P('shard', 'ctx'), may hold values from -4 to 4
- first_fc: float32 [1600, 6400], P('shard', 'ctx'), may hold values from -28 to 28
- first_proj: float32 [6400, 1600], P('shard', 'ctx'), may hold values from -40 to 40
- first_small: float32 [12, 1600], P(None, 'shard'), may hold values from -64 to 64
- second_qkv: float32 [1600, 4800], P('shard', 'ctx'), may hold values from 12.288 to 49.152
- second_out: float32 [1600, 1600], P('shard', 'ctx'), may hold values from 0.0442368 to 0.1769472
- second_fc: float32 [1600, 6400], P('shard', 'ctx'), may hold values from 1.96608 to 7.86432
- second_proj: float32 [6400, 1600], P('shard', 'ctx'), may hold values from 4.42368 to 17.69472
- second_small: float32 [12, 1600], P(None, 'shard'), may hold values from 12.288 to 49.152
Outputs:
- output: bfloat16 [12288, 1600], P(('shard', 'ctx'))
- grad_input: float32 [12288, 1600], P(('shard', 'ctx'))
- master_qkv_new: float32 [1600, 4800], P('shard', 'ctx')
- master_out_new: float32 [1600, 1600], P('shard', 'ctx')
- master_fc_new: float32 [1600, 6400], P('shard', 'ctx')
- master_proj_new: float32 [6400, 1600], P('shard', 'ctx')
- master_small_new: float32 [12, 1600], P(None, 'shard')
- first_qkv_new: float32 [1600, 4800], P('shard', 'ctx')
- first_out_new: float32 [1600, 1600], P('shard', 'ctx')
- first_fc_new: float32 [1600, 6400], P('shard', 'ctx')
- first_proj_new: float32 [6400, 1600], P('shard', 'ctx')
- first_small_new: float32 [12, 1600], P(None, 'shard')
- second_qkv_new: float32 [1600, 4800], P('shard', 'ctx')
- second_out_new: float32 [1600, 1600], P('shard', 'ctx')
- second_fc_new: float32 [1600, 6400], P('shard', 'ctx')
- second_proj_new: float32 [6400, 1600], P('shard', 'ctx')
- second_small_new: float32 [12, 1600], P(None, 'shard')
- copy_qkv: bfloat16 [1600, 4800], P('shard', 'ctx')
- copy_out: bfloat16 [1600, 1600], P('shard', 'ctx')
- copy_fc: bfloat16 [1600, 6400], P('shard', 'ctx')
- copy_proj: bfloat16 [6400, 1600], P('shard', 'ctx')
- copy_small: bfloat16 [12, 1600], P(None, 'shard')
Inputs may be any that keep to these rules, and one draw needn't show every extreme that they name: `master_small`: rows 0 and 2 (norm gains) lie in 0.5 to 1.5, the other rows in -0.6 to 0.6.
All inputs are finite; a program needn't handle non-finite values.
Results may differ from a plain program's by a relative error of at most 0.009.
The roundings to bfloat16 on the way count: a program that leaves them out, or rounds other values in their place, can miss the bound.
Values may be sent and summed in bfloat16 or wider, within the bound.
A program may use at most 384 MiB of HBM per device.

v0:
```python
import math

import jax
import jax.numpy as jnp
from jax import lax
from jax.sharding import PartitionSpec as P

D = 1600
HD = 64
FF = 6400
BLK = 128
PROMPT = 1024
STEP = 10


NORM_EPS = 1e-05
BETA_ONE = 0.9
BETA_TWO = 0.999
ADAM_EPS = 1e-08
WEIGHT_DECAY = 0.1
SMALL_RATE = 0.2
MASKED = -1e30


def norm_rows(values, gain_row, shift_row):
    row_mean = jnp.mean(values, axis=-1, keepdims=True)
    centred = values - row_mean
    spread = jnp.mean(centred * centred, axis=-1, keepdims=True)
    return centred * lax.rsqrt(spread + NORM_EPS) * gain_row + shift_row


def gelu_tanh(values):
    inner_arg = 0.7978845608028654 * (values + 0.044715 * values * values * values)
    return 0.5 * values * (1.0 + jnp.tanh(inner_arg))


def contract_rows(left, right):
    return lax.dot_general(
        left, right, (((0,), (0,)), ((), ())), preferred_element_type=jnp.float32
    )


def through(left, weight):
    return lax.dot_general(
        left, weight, (((1,), (1,)), ((), ())), preferred_element_type=jnp.float32
    )


def forward_dot(left, weight):
    return jnp.dot(left, weight, preferred_element_type=jnp.float32)


def split_heads(matrix, groups):
    return matrix.reshape(matrix.shape[0], groups, -1).transpose(1, 0, 2)


def join_heads(stacked):
    return stacked.transpose(1, 0, 2).reshape(stacked.shape[1], -1)


def head_scores(queries, key_rows, allowed, head_dim):
    row_count = queries.shape[0]
    head_count = queries.shape[1] // head_dim
    query_heads = queries.reshape(row_count, head_count, head_dim)
    key_heads = key_rows.reshape(key_rows.shape[0], head_count, head_dim)
    raw_scores = jnp.einsum(
        "qhe,khe->hqk", query_heads, key_heads, preferred_element_type=jnp.float32
    ) * (1.0 / math.sqrt(head_dim))
    return jnp.where(allowed[None], raw_scores, MASKED)


def attend_forward(queries, key_rows, value_rows, allowed, head_dim):
    scores = head_scores(queries, key_rows, allowed, head_dim)
    peak_score = jnp.max(scores, axis=-1, keepdims=True)
    exp_scores = jnp.exp(scores - peak_score)
    score_total = jnp.sum(exp_scores, axis=-1, keepdims=True)
    softmax_probs = (exp_scores / score_total).astype(jnp.bfloat16)
    head_count = softmax_probs.shape[0]
    value_heads = value_rows.reshape(value_rows.shape[0], head_count, head_dim)
    attended = jnp.einsum(
        "hqk,khe->qhe", softmax_probs, value_heads, preferred_element_type=jnp.float32
    )
    return (attended.reshape(queries.shape[0], -1), (peak_score + jnp.log(score_total))[..., 0])


def attend_backward(queries, key_rows, value_rows, grad_attended, log_totals, allowed, head_dim):
    scores = head_scores(queries, key_rows, allowed, head_dim)
    softmax_probs = jnp.exp(scores - log_totals[..., None])
    head_count = softmax_probs.shape[0]
    row_count = queries.shape[0]
    query_heads = queries.reshape(row_count, head_count, head_dim)
    key_heads = key_rows.reshape(key_rows.shape[0], head_count, head_dim)
    value_heads = value_rows.reshape(value_rows.shape[0], head_count, head_dim)
    grad_heads = grad_attended.reshape(row_count, head_count, head_dim)
    grad_probs = jnp.einsum(
        "qhe,khe->hqk", grad_heads, value_heads, preferred_element_type=jnp.float32
    )
    centre = jnp.sum(softmax_probs * grad_probs, axis=-1, keepdims=True)
    grad_scores = (softmax_probs * (grad_probs - centre)).astype(jnp.bfloat16)
    score_scale = 1.0 / math.sqrt(head_dim)
    grad_query = (
        jnp.einsum("hqk,khe->qhe", grad_scores, key_heads, preferred_element_type=jnp.float32)
        * score_scale
    )
    grad_key = (
        jnp.einsum("hqk,qhe->khe", grad_scores, query_heads, preferred_element_type=jnp.float32)
        * score_scale
    )
    grad_value = jnp.einsum(
        "hqk,qhe->khe",
        softmax_probs.astype(jnp.bfloat16),
        grad_heads,
        preferred_element_type=jnp.float32,
    )
    return (
        grad_query.reshape(row_count, -1),
        grad_key.reshape(key_rows.shape[0], -1),
        grad_value.reshape(value_rows.shape[0], -1),
    )


def gather_weights(parts):
    small_turned = parts[4].T
    widened = (
        lax.all_gather(parts[0], "ctx", axis=1, tiled=True),
        lax.all_gather(parts[1], "ctx", axis=1, tiled=True),
        lax.all_gather(parts[2], "ctx", axis=1, tiled=True),
        lax.all_gather(parts[3], "ctx", axis=1, tiled=True),
    )
    tallest = (
        lax.all_gather(widened[0], "shard", axis=0, tiled=True),
        lax.all_gather(widened[1], "shard", axis=0, tiled=True),
        lax.all_gather(widened[2], "shard", axis=0, tiled=True),
        lax.all_gather(widened[3], "shard", axis=0, tiled=True),
        lax.all_gather(small_turned, "shard", axis=0, tiled=True),
    )
    return (tallest[0], tallest[1], tallest[2], tallest[3], tallest[4].T)


def reduce_gradients(matrices, small_grads):
    small_turned = small_grads.T
    row_parts = (
        lax.psum_scatter(matrices[0], "shard", scatter_dimension=0, tiled=True),
        lax.psum_scatter(matrices[1], "shard", scatter_dimension=0, tiled=True),
        lax.psum_scatter(matrices[2], "shard", scatter_dimension=0, tiled=True),
        lax.psum_scatter(matrices[3], "shard", scatter_dimension=0, tiled=True),
        lax.psum_scatter(small_turned, "shard", scatter_dimension=0, tiled=True),
    )
    column_parts = (
        lax.psum_scatter(row_parts[0], "ctx", scatter_dimension=1, tiled=True),
        lax.psum_scatter(row_parts[1], "ctx", scatter_dimension=1, tiled=True),
        lax.psum_scatter(row_parts[2], "ctx", scatter_dimension=1, tiled=True),
        lax.psum_scatter(row_parts[3], "ctx", scatter_dimension=1, tiled=True),
    )
    return (column_parts[0], column_parts[1], column_parts[2], column_parts[3], row_parts[4].T)


def adamw(master, first, second, gradient, rate, decay):
    first_new = BETA_ONE * first + (1.0 - BETA_ONE) * gradient
    second_new = BETA_TWO * second + (1.0 - BETA_TWO) * gradient * gradient
    fix_one = 1.0 - BETA_ONE**STEP
    fix_two = 1.0 - BETA_TWO**STEP
    update = first_new / fix_one / (jnp.sqrt(second_new / fix_two) + ADAM_EPS)
    master_new = master - rate * (update + decay * master)
    return (master_new, first_new, second_new, master_new.astype(jnp.bfloat16))


def local(
    tokens,
    cotangent,
    master_qkv,
    master_out,
    master_fc,
    master_proj,
    master_small,
    first_qkv,
    first_out,
    first_fc,
    first_proj,
    first_small,
    second_qkv,
    second_out,
    second_fc,
    second_proj,
    second_small,
):
    feat_width = tokens.shape[1]
    row_count = tokens.shape[0]
    ctx_count = lax.axis_size("ctx")
    ctx_here = lax.axis_index("ctx")
    prompt_rows = PROMPT // ctx_count
    fc_rows = FF // feat_width
    head_count = feat_width // HD
    per_pass = 5
    groups = head_count // per_pass
    lowered = (
        master_qkv.astype(jnp.bfloat16),
        master_out.astype(jnp.bfloat16),
        master_fc.astype(jnp.bfloat16),
        master_proj.astype(jnp.bfloat16),
        master_small.astype(jnp.bfloat16),
    )
    w_qkv, w_out, w_fc, w_proj, small_low = gather_weights(lowered)
    small_params = small_low.astype(jnp.float32)
    places = jnp.arange(row_count, dtype=jnp.int32)
    in_prompt = places < prompt_rows
    later = places - prompt_rows
    pos_query = jnp.where(in_prompt, ctx_here * prompt_rows + places, PROMPT + later % BLK)
    seq_query = jnp.where(in_prompt, -1, later // BLK)
    cont_keys = jnp.arange(row_count - prompt_rows, dtype=jnp.int32)
    pos_key = jnp.concatenate([jnp.arange(PROMPT, dtype=jnp.int32), PROMPT + cont_keys % BLK])
    seq_key = jnp.concatenate([jnp.full((PROMPT,), -1, jnp.int32), cont_keys // BLK])
    allowed = (pos_key[None, :] <= pos_query[:, None]) & (
        (seq_key[None, :] == -1) | (seq_key[None, :] == seq_query[:, None])
    )
    inputs = tokens.astype(jnp.float32)
    normed_one, norm_one_back = jax.vjp(norm_rows, inputs, small_params[0], small_params[1])
    act_one = normed_one.astype(jnp.bfloat16)
    qkv_bias = jnp.concatenate([small_params[4], jnp.zeros_like(small_params[4]), small_params[5]])
    qkv = (forward_dot(act_one, w_qkv) + qkv_bias).astype(jnp.bfloat16)
    queries = qkv[:, :feat_width]
    key_local = qkv[:, feat_width : 2 * feat_width]
    value_local = qkv[:, 2 * feat_width :]
    key_prompt, value_prompt = (
        lax.all_gather(key_local[:prompt_rows], "ctx", axis=0, tiled=True),
        lax.all_gather(value_local[:prompt_rows], "ctx", axis=0, tiled=True),
    )
    key_rows = jnp.concatenate([key_prompt, key_local[prompt_rows:]], axis=0)
    value_rows = jnp.concatenate([value_prompt, value_local[prompt_rows:]], axis=0)
    query_split = split_heads(queries, groups)
    key_split = split_heads(key_rows, groups)
    value_split = split_heads(value_rows, groups)
    attended, log_totals = lax.map(
        lambda element: attend_forward(element[0], element[1], element[2], allowed, HD),
        (query_split, key_split, value_split),
    )
    attended_low = join_heads(attended).astype(jnp.bfloat16)
    middle = inputs + forward_dot(attended_low, w_out) + small_params[6]
    normed_two, norm_two_back = jax.vjp(norm_rows, middle, small_params[2], small_params[3])
    act_two = normed_two.astype(jnp.bfloat16)
    hidden = forward_dot(act_two, w_fc) + small_params[7 : 7 + fc_rows].reshape(-1)
    activated, gelu_back = jax.vjp(gelu_tanh, hidden)
    act_three = activated.astype(jnp.bfloat16)
    output = middle + forward_dot(act_three, w_proj) + small_params[small_params.shape[0] - 1]
    grad_output = cotangent.astype(jnp.float32)
    grad_proj = contract_rows(act_three, cotangent)
    grad_proj_bias = jnp.sum(grad_output, axis=0)
    grad_hidden = gelu_back(through(cotangent, w_proj))[0].astype(jnp.bfloat16)
    grad_fc_bias = jnp.sum(grad_hidden, axis=0, dtype=jnp.float32)
    grad_fc = contract_rows(act_two, grad_hidden)
    grad_middle_norm, grad_gain_two, grad_shift_two = norm_two_back(through(grad_hidden, w_fc))
    grad_middle = grad_output + grad_middle_norm
    grad_branch = grad_middle.astype(jnp.bfloat16)
    grad_out_bias = jnp.sum(grad_branch, axis=0, dtype=jnp.float32)
    grad_wout = contract_rows(attended_low, grad_branch)
    grad_attended = through(grad_branch, w_out).astype(jnp.bfloat16)
    grad_query, grad_key, grad_value = lax.map(
        lambda element: attend_backward(
            element[0], element[1], element[2], element[3], element[4], allowed, HD
        ),
        (query_split, key_split, value_split, split_heads(grad_attended, groups), log_totals),
    )
    grad_query = join_heads(grad_query)
    grad_key = join_heads(grad_key)
    grad_value = join_heads(grad_value)
    key_prompt_grad, value_prompt_grad = (
        lax.psum_scatter(grad_key[:PROMPT], "ctx", scatter_dimension=0, tiled=True),
        lax.psum_scatter(grad_value[:PROMPT], "ctx", scatter_dimension=0, tiled=True),
    )
    grad_qkv = jnp.concatenate(
        [
            grad_query,
            jnp.concatenate([key_prompt_grad, grad_key[PROMPT:]], axis=0),
            jnp.concatenate([value_prompt_grad, grad_value[PROMPT:]], axis=0),
        ],
        axis=1,
    ).astype(jnp.bfloat16)
    grad_query_bias = jnp.sum(grad_qkv[:, :feat_width], axis=0, dtype=jnp.float32)
    grad_value_bias = jnp.sum(grad_qkv[:, 2 * feat_width :], axis=0, dtype=jnp.float32)
    grad_wqkv = contract_rows(act_one, grad_qkv)
    grad_in_norm, grad_gain_one, grad_shift_one = norm_one_back(through(grad_qkv, w_qkv))
    grad_input = grad_middle + grad_in_norm
    small_grads = jnp.concatenate(
        [
            jnp.stack(
                [
                    grad_gain_one,
                    grad_shift_one,
                    grad_gain_two,
                    grad_shift_two,
                    grad_query_bias,
                    grad_value_bias,
                    grad_out_bias,
                ]
            ),
            grad_fc_bias.reshape(fc_rows, feat_width),
            grad_proj_bias[None],
        ],
        axis=0,
    )
    small_grads = lax.psum(small_grads, "ctx")
    gradients = reduce_gradients((grad_wqkv, grad_wout, grad_fc, grad_proj), small_grads)
    masters = (master_qkv, master_out, master_fc, master_proj, master_small)
    firsts = (first_qkv, first_out, first_fc, first_proj, first_small)
    seconds = (second_qkv, second_out, second_fc, second_proj, second_small)
    rates = (D ** (-0.5), max(D // 256, 1) ** (-0.5), D ** (-0.5), FF ** (-0.5), SMALL_RATE)
    decays = (WEIGHT_DECAY, WEIGHT_DECAY, WEIGHT_DECAY, WEIGHT_DECAY, 0.0)
    results = [
        adamw(
            masters[index],
            firsts[index],
            seconds[index],
            gradients[index],
            rates[index],
            decays[index],
        )
        for index in range(5)
    ]
    return (
        output.astype(jnp.bfloat16),
        grad_input,
        results[0][0],
        results[1][0],
        results[2][0],
        results[3][0],
        results[4][0],
        results[0][1],
        results[1][1],
        results[2][1],
        results[3][1],
        results[4][1],
        results[0][2],
        results[1][2],
        results[2][2],
        results[3][2],
        results[4][2],
        results[0][3],
        results[1][3],
        results[2][3],
        results[3][3],
        results[4][3],
    )


def solution(mesh):
    placed = (
        P(("shard", "ctx"), None),
        P(("shard", "ctx"), None),
        P("shard", "ctx"),
        P("shard", "ctx"),
        P("shard", "ctx"),
        P("shard", "ctx"),
        P(None, "shard"),
        P("shard", "ctx"),
        P("shard", "ctx"),
        P("shard", "ctx"),
        P("shard", "ctx"),
        P(None, "shard"),
        P("shard", "ctx"),
        P("shard", "ctx"),
        P("shard", "ctx"),
        P("shard", "ctx"),
        P(None, "shard"),
    )
    return jax.shard_map(
        local,
        mesh=mesh,
        in_specs=placed,
        out_specs=(
            P(("shard", "ctx"), None),
            P(("shard", "ctx"), None),
            P("shard", "ctx"),
            P("shard", "ctx"),
            P("shard", "ctx"),
            P("shard", "ctx"),
            P(None, "shard"),
            P("shard", "ctx"),
            P("shard", "ctx"),
            P("shard", "ctx"),
            P("shard", "ctx"),
            P(None, "shard"),
            P("shard", "ctx"),
            P("shard", "ctx"),
            P("shard", "ctx"),
            P("shard", "ctx"),
            P(None, "shard"),
            P("shard", "ctx"),
            P("shard", "ctx"),
            P("shard", "ctx"),
            P("shard", "ctx"),
            P(None, "shard"),
        ),
        check_vma=False,
    )
```

profile of v0, /device:TPU:0, one launch (start us, length us, event | category | flops | bytes accessed | tf_op | source)
XLA Modules:
  0.0 2439.9 jit_solution(6329291306452716737)
XLA Ops:
  9.4 48.5 %all-gather.27.cloned.1.call-done = bf16[4,1200,200]{1,2,0:T(8,128)(2,1)} async-done(((bf16[1,1200,200]{1,2,0:T(8,128)(2,1)}), bf16[4,1200,200]{1,2,0:T(8,128)(2,1)}) %all-gather.27.cloned.1.call-update) | async-done | bytes 1920016 | tf_op jit(solution)/shard_map/all_gather | solution.py:125
  66.8 9.2 all-gather
  77.6 69.3 %all-gather.13.cloned.1.call-done = bf16[1600,4800]{1,0:T(8,128)(2,1)} async-done(((bf16[200,4800]{1,0:T(8,128)(2,1)}), bf16[1600,4800]{1,0:T(8,128)(2,1)}) %all-gather.13.cloned.1.call-update) | async-done | bytes 15360016 | tf_op jit(solution)/shard_map/all_gather | solution.py:131
  147.0 13.8 add_convert_fusion
  164.7 31.2 %all_gather.38 = bf16[200,1600]{0,1:T(8,128)(2,1)S(1)} all-gather(bf16[200,400]{0,1:T(8,128)(2,1)S(1)} %copy.87), channel_id=1, replica_groups=mesh['shard'=8,'ctx'=4] {'ctx'}, dimensions={1}, use_global_device_ids=true | all-gather | bytes 800000 | tf_op jit(solution)/shard_map/all_gather | solution.py:126
  197.2 23.9 all-gather.23.cloned.1.call-done
  226.7 50.5 %all-gather.29.cloned.1.call-done = bf16[4,1600,200]{1,2,0:T(8,128)(2,1)} async-done(((bf16[1,1600,200]{1,2,0:T(8,128)(2,1)}), bf16[4,1600,200]{1,2,0:T(8,128)(2,1)}) %all-gather.29.cloned.1.call-update) | async-done | bytes 2560016 | tf_op jit(solution)/shard_map/all_gather | solution.py:127
  288.6 55.0 %all-gather.15.cloned.1.call-done = bf16[1024,1600]{0,1:T(8,128)(2,1)} async-done(((bf16[256,1600]{0,1:T(8,128)(2,1)}), bf16[1024,1600]{0,1:T(8,128)(2,1)}) %all-gather.15.cloned.1.call-update) | async-done | bytes 3276816 | tf_op jit(solution)/shard_map/all_gather | solution.py:226
  347.8 61.6 %all-gather.17.cloned.1.call-done = bf16[1024,1600]{0,1:T(8,128)(2,1)} async-done(((bf16[256,1600]{0,1:T(8,128)(2,1)}), bf16[1024,1600]{0,1:T(8,128)(2,1)}) %all-gather.17.cloned.1.call-update) | async-done | bytes 3276816 | tf_op jit(solution)/shard_map/all_gather | solution.py:225
  414.9 51.5 %while.28 = (s32[]{:T(128)}, bf16[5,384,320]{1,2,0:T(8,128)(2,1)}, f32[5,5,384]{2,1,0:T(8,128)S(1)}, bf16[5,1152,320]{1,2,0:T(8,128)(2,1)}, bf16[5,384,320]{1,2,...) while((s32[]{:T(128)}, bf16[5,384,320]{1,2,0:T(8,128)(2,1)}, ...), condition=%wide.region_5.6_spmd.clone, body=%wide.region_2.5_spmd.clone.sunk | while | flops 594540672 | bytes 34298636 | solution.py:233
  466.4 6.7 fusion.75
  474.9 87.5 %all-gather.25.cloned.1.call-done = bf16[6400,1600]{1,0:T(8,128)(2,1)} async-done(((bf16[800,1600]{1,0:T(8,128)(2,1)}), bf16[6400,1600]{1,0:T(8,128)(2,1)}) %all-gather.25.cloned.1.call-update) | async-done | bytes 20480016 | tf_op jit(solution)/shard_map/all_gather | solution.py:134
  562.4 16.4 fusion.77
  578.9 91.0 %all-gather.21.cloned.1.call-done = bf16[1600,6400]{1,0:T(8,128)(2,1)} async-done(((bf16[200,6400]{1,0:T(8,128)(2,1)}), bf16[1600,6400]{1,0:T(8,128)(2,1)}) %all-gather.21.cloned.1.call-update) | async-done | bytes 20480016 | tf_op jit(solution)/shard_map/all_gather | solution.py:133
  669.9 26.7 %convert_reduce_fusion = (f32[6400]{0:T(1024)}, bf16[384,6400]{1,0:T(8,128)(2,1)}, f32[384,6400]{1,0:T(8,128)}) fusion(f32[384,6400]{1,0:T(8,128)} %fusion.77, f32[6400]{0:T(1024)S(1)} %add.297, bf16[1600,6400]{1,0:T(8,128)(2,1)} %all-gather.21.cloned.1.call-done, f32[384,1600]{0,1:T(8,128)S(1)} %copy-done.4, f32[1600]{0:T(1024)S(1)} %copy-done.43, ...), kind=kOutput, calls=%fused_computation.43 | convolution fusion | flops 7933741056 | bytes 47580672 | tf_op jit(solution)/shard_map/dot_general | solution.py:50
  696.6 19.6 multiply_reduce_fusion.1
  718.6 7.0 convolution_convert_fusion
  726.8 165.5 %while.29 = (s32[]{:T(128)}, bf16[5,384,320]{1,2,0:T(8,128)(2,1)}, f32[5,1152,320]{1,2,0:T(8,128)}, f32[5,1152,320]{1,2,0:T(8,128)}, bf16[5,1152,320]{1,2,0:T(8,...) while((s32[]{:T(128)}, bf16[5,384,320]{1,2,0:T(8,128)(2,1)}, ...), condition=%wide.region_12.13_spmd.clone, body=%wide.region_10.12_spmd.clone.sunk | while | flops 1437866112 | bytes 132664176 | solution.py:257
  732.5 6.4 multiply_reduce_fusion.5
  738.9 9.2 multiply_convert_fusion.2
  765.5 6.4 multiply_reduce_fusion.5
  771.9 9.2 multiply_convert_fusion.2
  798.5 6.4 multiply_reduce_fusion.5
  804.9 9.2 multiply_convert_fusion.2
  831.5 6.4 multiply_reduce_fusion.5
  837.9 9.2 multiply_convert_fusion.2
  864.6 6.4 multiply_reduce_fusion.5
  871.0 9.2 multiply_convert_fusion.2
  892.3 6.8 slice.114
  899.2 7.4 slice.112
  918.0 96.3 %reduce-scatter.26.cloned.1.call-done = f32[256,1600]{0,1:T(8,128)} async-done(((f32[1024,1600]{0,1:T(8,128)}), f32[256,1600]{0,1:T(8,128)}) %reduce-scatter.26.cloned.1.call-update) | async-done | bytes 1638416 | tf_op jit(solution)/shard_map/reduce_scatter | solution.py:268
  1015.8 116.3 %reduce-scatter.24.cloned.1.call-done = f32[256,1600]{0,1:T(8,128)} async-done(((f32[1024,1600]{0,1:T(8,128)}), f32[256,1600]{0,1:T(8,128)}) %reduce-scatter.24.cloned.1.call-update) | async-done | bytes 1638416 | tf_op jit(solution)/shard_map/reduce_scatter | solution.py:267
  1134.7 20.9 fusion.50
  1156.3 23.1 fusion.54
  1180.7 23.0 fusion.55
  1206.4 14.8 fusion.58
  1232.8 189.6 %reduce-scatter.28.cloned.1.call-done = f32[200,4800]{1,0:T(8,128)} async-done(((f32[1600,4800]{1,0:T(8,128)}), f32[200,4800]{1,0:T(8,128)}) %reduce-scatter.28.cloned.1.call-update) | async-done | bytes 3840016 | tf_op jit(solution)/shard_map/reduce_scatter | solution.py:143
  1428.1 309.9 %reduce-scatter.42.cloned.1.call-done = f32[200,6400]{1,0:T(8,128)} async-done(((f32[1600,6400]{1,0:T(8,128)}), f32[200,6400]{1,0:T(8,128)}) %reduce-scatter.42.cloned.1.call-update) | async-done | bytes 5120016
  1738.0 6.5 copy.103
  1745.0 259.0 %reduce-scatter.30.cloned.1.call-done = f32[800,1600]{1,0:T(8,128)} async-done(((f32[6400,1600]{1,0:T(8,128)}), f32[800,1600]{1,0:T(8,128)}) %reduce-scatter.30.cloned.1.call-update) | async-done | bytes 5120016 | tf_op jit(solution)/shard_map/reduce_scatter | solution.py:146
  2004.0 6.8 copy.105
  2021.6 17.6 fusion.25
  2039.2 19.8 all-reduce.6.cloned.1.call-done
  2059.8 19.4 psum.8
  2079.8 18.7 reduce-scatter.34.cloned.1.call-done
  2102.2 86.1 %reduce-scatter.32.cloned.1.call-done = f32[1200,200]{1,0:T(8,128)} async-done(((f32[4800,200]{1,0:T(8,128)}), f32[1200,200]{1,0:T(8,128)}) %reduce-scatter.32.cloned.1.call-update) | async-done | bytes 960016
  2193.6 112.6 %reduce-scatter.36.cloned.1.call-done = f32[1600,200]{1,0:T(8,128)} async-done(((f32[6400,200]{1,0:T(8,128)}), f32[1600,200]{1,0:T(8,128)}) %reduce-scatter.36.cloned.1.call-update) | async-done | bytes 1280016
  2309.3 101.4 %reduce-scatter.38.cloned.1.call-done = f32[400,800]{1,0:T(8,128)} async-done(((f32[1600,800]{1,0:T(8,128)}), f32[400,800]{1,0:T(8,128)}) %reduce-scatter.38.cloned.1.call-update) | async-done | bytes 1280016
  (389 shorter events, 271.1 us)
Async XLA Ops:
  7.2 50.7 %all-gather.27.cloned.1.call-start = ((), (), s32[]{:S(2)}) async-start(), calls=%async_computation.21 | async-start | bytes 2560000 | tf_op jit(solution)/shard_map/all_gather | solution.py:125
  9.3 137.7 %all-gather.13.cloned.1.call-start = ((), (), s32[]{:S(2)}) async-start(), calls=%async_computation.10 | async-start | bytes 17510400 | tf_op jit(solution)/shard_map/all_gather | solution.py:131
  63.4 157.7 %all-gather.23.cloned.1.call-start = ((), (), s32[]{:S(2)}) async-start(), calls=%async_computation.15 | async-start | bytes 3584000 | tf_op jit(solution)/shard_map/all_gather | solution.py:128
  64.3 12.6 copy-start.1
  64.4 212.9 %all-gather.29.cloned.1.call-start = ((), (), s32[]{:S(2)}) async-start(), calls=%async_computation.22 | async-start | bytes 3328000 | tf_op jit(solution)/shard_map/all_gather | solution.py:127
  66.8 276.9 %all-gather.15.cloned.1.call-start = ((), (), s32[]{:S(2)}) async-start(), calls=%async_computation.11 | async-start | bytes 4096000 | tf_op jit(solution)/shard_map/all_gather | solution.py:226
  76.9 70.1 %copy-start.33 = (f32[1600]{0:T(1024)}, f32[1600]{0:T(1024)S(1)}, u32[]{:S(2)}) copy-start(f32[1600]{0:T(1024)S(1)} %get-tuple-element.306) | copy-start | bytes 19204
  76.9 84.0 %copy-start.28 = (f32[1600]{0:T(1024)}, f32[1600]{0:T(1024)S(1)}, u32[]{:S(2)}) copy-start(f32[1600]{0:T(1024)S(1)} %get-tuple-element.307) | copy-start | bytes 19204
  77.2 69.8 %copy-start.36 = (f32[384]{0:T(512)}, f32[384]{0:T(512)S(1)}, u32[]{:S(2)}) copy-start(f32[384]{0:T(512)S(1)} %broadcast_multiply_fusion.1) | copy-start | bytes 4612
  77.6 69.4 %copy-start.55 = (f32[384]{0:T(512)}, f32[384]{0:T(512)S(1)}, u32[]{:S(2)}) copy-start(f32[384]{0:T(512)S(1)} %fusion.31) | copy-start | bytes 4612
  77.6 69.4 %copy-start.38 = (f32[384]{0:T(512)}, f32[384]{0:T(512)S(1)}, u32[]{:S(2)}) copy-start(f32[384]{0:T(512)S(1)} %fusion.46) | copy-start | bytes 4612
  164.0 245.4 %all-gather.17.cloned.1.call-start = ((), (), s32[]{:S(2)}) async-start(), calls=%async_computation.12 | async-start | bytes 4096000 | tf_op jit(solution)/shard_map/all_gather | solution.py:225
  164.5 301.8 %all-gather.19.cloned.1.call-start = ((), (), s32[]{:S(2)}) async-start(), calls=%async_computation.13 | async-start | bytes 5990400 | tf_op jit(solution)/shard_map/all_gather | solution.py:132
  197.1 365.3 %all-gather.25.cloned.1.call-start = ((), (), s32[]{:S(2)}) async-start(), calls=%async_computation.16 | async-start | bytes 23961600 | tf_op jit(solution)/shard_map/all_gather | solution.py:134
  226.2 443.6 %all-gather.21.cloned.1.call-start = ((), (), s32[]{:S(2)}) async-start(), calls=%async_computation.14 | async-start | bytes 23040000 | tf_op jit(solution)/shard_map/all_gather | solution.py:133
  287.2 727.1 %reduce-scatter.26.cloned.1.call-start = ((), (), s32[]{:S(2)}) async-start(), calls=%async_computation.18 | async-start | bytes 8192000 | tf_op jit(solution)/shard_map/reduce_scatter | solution.py:268
  473.1 243.1 %copy-start.45 = (f32[384]{0:T(512)}, f32[384]{0:T(512)S(1)}, u32[]{:S(2)}) copy-start(f32[384]{0:T(512)S(1)} %broadcast_multiply_fusion) | copy-start | bytes 4612
  474.9 241.3 %copy-start.47 = (f32[384]{0:T(512)}, f32[384]{0:T(512)S(1)}, u32[]{:S(2)}) copy-start(f32[384]{0:T(512)S(1)} %fusion.47) | copy-start | bytes 4612
  474.9 195.0 %copy-start.4 = (f32[384,1600]{0,1:T(8,128)S(1)}, f32[384,1600]{0,1:T(8,128)}, u32[]{:S(2)}) copy-start(f32[384,1600]{0,1:T(8,128)} %copy-done.3) | copy-start | bytes 7372804
  474.9 195.0 %copy-start.41 = (f32[1600]{0:T(1024)S(1)}, f32[1600]{0:T(1024)}, u32[]{:S(2)}) copy-start(f32[1600]{0:T(1024)} %get-tuple-element.300) | copy-start | bytes 19204
  474.9 195.0 %copy-start.43 = (f32[1600]{0:T(1024)S(1)}, f32[1600]{0:T(1024)}, u32[]{:S(2)}) copy-start(f32[1600]{0:T(1024)} %get-tuple-element.302) | copy-start | bytes 19204
  718.6 8.2 copy-start.12
  899.1 233.0 %reduce-scatter.24.cloned.1.call-start = ((), (), s32[]{:S(2)}) async-start(), calls=%async_computation.17 | async-start | bytes 8192000 | tf_op jit(solution)/shard_map/reduce_scatter | solution.py:267
  906.6 323.1 %reduce-scatter.40.cloned.1.call-start = ((), (), s32[]{:S(2)}) async-start(), calls=%async_computation.28 | async-start | bytes 11980800
  914.0 508.4 %reduce-scatter.28.cloned.1.call-start = ((), (), s32[]{:S(2)}) async-start(), calls=%async_computation.19 | async-start | bytes 35020800 | tf_op jit(solution)/shard_map/reduce_scatter | solution.py:143
  917.9 216.7 %copy-start.2 = (bf16[384,1600]{0,1:T(8,128)(2,1)S(1)}, bf16[384,1600]{0,1:T(8,128)(2,1)}, u32[]{:S(2)}) copy-start(bf16[384,1600]{0,1:T(8,128)(2,1)} %param.21) | copy-start | bytes 3686404
  917.9 216.7 %copy-start.13 = (bf16[5,384,320]{1,2,0:T(8,128)(2,1)S(1)}, bf16[5,384,320]{1,2,0:T(8,128)(2,1)}, u32[]{:S(2)}) copy-start(bf16[5,384,320]{1,2,0:T(8,128)(2,1)} %get-tuple-element.116) | copy-start | bytes 3686404
  917.9 216.7 %copy-start.29 = (f32[1600]{0:T(1024)S(1)}, f32[1600]{0:T(1024)}, u32[]{:S(2)}) copy-start(f32[1600]{0:T(1024)} %copy-done.28) | copy-start | bytes 19204
  917.9 216.7 %copy-start.34 = (f32[1600]{0:T(1024)S(1)}, f32[1600]{0:T(1024)}, u32[]{:S(2)}) copy-start(f32[1600]{0:T(1024)} %copy-done.33) | copy-start | bytes 19204
  917.9 216.7 %copy-start.37 = (f32[384]{0:T(512)S(1)}, f32[384]{0:T(512)}, u32[]{:S(2)}) copy-start(f32[384]{0:T(512)} %copy-done.36) | copy-start | bytes 4612
  917.9 216.7 %copy-start.39 = (f32[384]{0:T(512)S(1)}, f32[384]{0:T(512)}, u32[]{:S(2)}) copy-start(f32[384]{0:T(512)} %copy-done.38) | copy-start | bytes 4612
  1155.6 582.4 %reduce-scatter.42.cloned.1.call-start = ((), (), s32[]{:S(2)}) async-start(), calls=%async_computation.29 | async-start | bytes 46080000
  1179.5 824.6 %reduce-scatter.30.cloned.1.call-start = ((), (), s32[]{:S(2)}) async-start(), calls=%async_computation.20 | async-start | bytes 47923200 | tf_op jit(solution)/shard_map/reduce_scatter | solution.py:146
  1203.8 855.2 %all-reduce.6.cloned.1.call-start = ((), (), s32[]{:S(2)}) async-start(), calls=%async_computation.27 | async-start | bytes 212992
  1206.4 14.9 copy-start.56
  1229.6 869.0 %reduce-scatter.34.cloned.1.call-start = ((), (), s32[]{:S(2)}) async-start(), calls=%async_computation.24 | async-start | bytes 2048000
  1232.7 955.6 %reduce-scatter.32.cloned.1.call-start = ((), (), s32[]{:S(2)}) async-start(), calls=%async_computation.23 | async-start | bytes 6144000
  1428.1 878.1 %reduce-scatter.36.cloned.1.call-start = ((), (), s32[]{:S(2)}) async-start(), calls=%async_computation.25 | async-start | bytes 8192000
  1744.5 666.3 %reduce-scatter.38.cloned.1.call-start = ((), (), s32[]{:S(2)}) async-start(), calls=%async_computation.26 | async-start | bytes 7168000
  2021.5 57.7 %copy-start.50 = (f32[12,200]{1,0:T(8,128)S(1)}, f32[12,200]{1,0:T(8,128)}, u32[]{:S(2)}) copy-start(f32[12,200]{1,0:T(8,128)} %param.27) | copy-start | bytes 28804
  2021.5 57.7 %copy-start.57 = (f32[12,200]{1,0:T(8,128)S(1)}, f32[12,200]{1,0:T(8,128)}, u32[]{:S(2)}) copy-start(f32[12,200]{1,0:T(8,128)} %param.32) | copy-start | bytes 28804
  2021.5 57.7 %copy-start.58 = (f32[12,200]{1,0:T(8,128)S(1)}, f32[12,200]{1,0:T(8,128)}, u32[]{:S(2)}) copy-start(f32[12,200]{1,0:T(8,128)} %param.37) | copy-start | bytes 28804
  2021.5 78.2 %copy-start.31 = (f32[200,400]{1,0:T(8,128)S(1)}, f32[200,400]{1,0:T(8,128)}, u32[]{:S(2)}) copy-start(f32[200,400]{1,0:T(8,128)} %param.24) | copy-start | bytes 960004
  2021.5 78.2 %copy-start.40 = (f32[200,400]{1,0:T(8,128)S(1)}, f32[200,400]{1,0:T(8,128)}, u32[]{:S(2)}) copy-start(f32[200,400]{1,0:T(8,128)} %param.29) | copy-start | bytes 960004
  2099.8 90.2 %copy-start.24 = (f32[200,1200]{1,0:T(8,128)S(1)}, f32[200,1200]{1,0:T(8,128)}, u32[]{:S(2)}) copy-start(f32[200,1200]{1,0:T(8,128)} %param.23) | copy-start | bytes 2880004
  2102.2 87.8 %copy-start.35 = (f32[200,1200]{1,0:T(8,128)S(1)}, f32[200,1200]{1,0:T(8,128)}, u32[]{:S(2)}) copy-start(f32[200,1200]{1,0:T(8,128)} %param.28) | copy-start | bytes 2880004
  2306.2 107.7 %copy-start.14 = (f32[800,400]{1,0:T(8,128)S(1)}, f32[800,400]{1,0:T(8,128)}, u32[]{:S(2)}) copy-start(f32[800,400]{1,0:T(8,128)} %copy.94) | copy-start | bytes 3840004
  2306.2 107.7 %copy-start.15 = (f32[800,400]{1,0:T(8,128)S(1)}, f32[800,400]{1,0:T(8,128)}, u32[]{:S(2)}) copy-start(f32[800,400]{1,0:T(8,128)} %copy.91) | copy-start | bytes 3840004
  (50 other events, 177.4 us)
Sparse Core Ops, SparseCore 0:
  10.2 47.6 all-gather.26
  63.5 83.4 all-gather.12
  149.1 71.8 all-gather.22
  223.1 54.1 all-gather.28
  279.3 64.3 all-gather.14
  345.6 63.7 all-gather.16
  411.8 39.6 all-gather.18
  453.4 108.9 all-gather.24
  564.3 105.5 all-gather.20
  899.2 114.9 reduce-scatter.25
  1016.6 115.5 reduce-scatter.23
  1135.6 87.4 reduce-scatter.39
  1226.8 195.4 reduce-scatter.27
  1426.2 311.7 reduce-scatter.41
  1742.0 261.9 reduce-scatter.29
  2007.5 51.4 all-reduce.5
  2061.3 37.2 reduce-scatter.33
  2100.7 87.4 reduce-scatter.31
  2190.7 115.4 reduce-scatter.35
  2308.5 102.2 reduce-scatter.37
where the time goes:
time: 2450 us; the launch traced here: 2440 us
  waiting for transfers between devices  1800 us (73%)
  matrix products  306 us (12%)
  local copies, waits for them, and re-layouts  151 us (6%)
  other arithmetic  106 us (4%)
  blocking collectives  59.8 us (2%)
    unnamed x27, waiting for transfers between devices  649 us
    reduce_scatter x1, waiting for transfers between devices, reduce_gradients(): lax.psum_scatter(matrices[3], 'shard', scatter_dimension=0, tiled=True)  259 us
    reduce_scatter x1, waiting for transfers between devices, reduce_gradients(): lax.psum_scatter(matrices[0], 'shard', scatter_dimension=0, tiled=True)  190 us
    reduce_scatter x1, waiting for transfers between devices, local(): lax.psum_scatter(grad_key[:PROMPT], 'ctx', scatter_dimension=0, tiled=True)  116 us
    reduce_scatter x1, waiting for transfers between devices, local(): lax.psum_scatter(grad_value[:PROMPT], 'ctx', scatter_dimension=0, tiled=T...  96.3 us
    all_gather x1, waiting for transfers between devices, gather_weights(): lax.all_gather(widened[2], 'shard', axis=0, tiled=True)  91 us
    all_gather x1, waiting for transfers between devices, gather_weights(): lax.all_gather(widened[3], 'shard', axis=0, tiled=True)  87.5 us
    dot_general x4, matrix products, contract_rows(): lax.dot_general(left, right, (((0,), (0,)), ((), ())), preferred_element_...  72.7 us
  transfers between devices with their start and end apart: 20, of which 18 were waited for; matrix products, arithmetic and copies ran while one was open for 12% of the time, Pallas kernels for 0%

commit v1 on v0

v1 whole, which is shorter than its diff:
```python
import functools
import math

import jax
import jax.numpy as jnp
from jax import lax
from jax.experimental import pallas as pl
from jax.experimental.pallas import tpu as pltpu
from jax.sharding import PartitionSpec as P

D = 1600
HD = 64
FF = 6400
BLK = 128
PROMPT = 1024
STEP = 10
TP = 4

NORM_EPS = 1e-05
BETA_ONE = 0.9
BETA_TWO = 0.999
ADAM_EPS = 1e-08
WEIGHT_DECAY = 0.1
SMALL_RATE = 0.2
MASKED = -1e30
MESH = pl.DeviceIdType.MESH
BF = jnp.bfloat16
F32 = jnp.float32
VMEM_BYTES = 60 * 1024 * 1024


def flip(index, mask):
    bit = 1
    while bit <= mask:
        if mask & bit:
            index = index + bit - 2 * bit * ((index // bit) % 2)
        bit *= 2
    return index


def spans(bits):
    tags = [0]
    for bit in bits:
        tags = tags + [t + bit for t in tags]
    return tags


def exchange_cost(us):
    return pl.CostEstimate(flops=0, bytes_accessed=us * 3_000_000, transcendentals=0)


def greet(peers):
    barrier = pltpu.get_barrier_semaphore()
    for peer in peers:
        pl.semaphore_signal(barrier, inc=1, device_id=peer, device_id_type=MESH)
    pl.semaphore_wait(barrier, len(peers))


def remote(src, dst, send, recv, peer):
    return pltpu.make_async_remote_copy(
        src_ref=src, dst_ref=dst, send_sem=send, recv_sem=recv, device_id=peer, device_id_type=MESH
    )


class Keep:
    def __init__(self, src, dst, room, sems):
        self.load = pltpu.make_async_copy(src, room, sems.at[0])
        self.store = pltpu.make_async_copy(room, dst, sems.at[1])
        self.load.start()

    def forward(self):
        self.load.wait()
        self.store.start()

    def finish(self):
        self.store.wait()


def add_into(target, other, rows):
    def step(i, carry):
        target[i] = (target[i].astype(F32) + other[i].astype(F32)).astype(BF)
        return carry

    lax.fori_loop(0, rows, step, 0)


def gather_kernel(ns, nc, *refs):
    srcs, column, dsts, columns, token = refs[:4], refs[4], refs[5:9], refs[9], refs[10]
    send, recv, send_z, recv_z, local_sem = refs[11:16]
    rooms, column_room = refs[16:20], refs[20]
    token[0] = jnp.int32(0)
    s, c = lax.axis_index("shard"), lax.axis_index("ctx")
    bits = [1 << k for k in range(1, ns.bit_length() - 1)]
    along = [(s, (c + j) % nc) for j in range(1, nc)]
    greet([(flip(s, b), c) for b in [1] + bits] + along)
    orders = [bits, bits, bits[::-1], bits[::-1]]

    def push(a, tag, bit):
        block = dsts[a].at[flip(s, tag)]
        got = tag + bit
        copy = remote(
            srcs[a] if tag == 0 else block, block, send.at[a, got], recv.at[a, got], (flip(s, bit), c)
        )
        copy.start()
        return copy

    def arrived(a, tag):
        block = dsts[a].at[flip(s, tag)]
        remote(block, block, send.at[a, tag], recv.at[a, tag], (s, c)).wait_recv()

    copies = []
    for k in range(len(bits)):
        for a in range(4):
            copies.append(push(a, 0, orders[a][k]))
    for a in range(4):
        copies.append(push(a, 0, 1))
    for j in range(1, nc):
        copy = remote(column, columns.at[c], send_z.at[j - 1], recv_z.at[j - 1], along[j - 1])
        copy.start()
        copies.append(copy)
    keep = [Keep(srcs[a], dsts[a].at[s], rooms[a], local_sem.at[a]) for a in range(4)]
    keep.append(Keep(column, columns.at[c], column_room, local_sem.at[4]))
    for own in keep:
        own.forward()
    for i in range(1, len(spans(bits))):
        for a in range(4):
            tag = spans(orders[a])[i]
            arrived(a, tag)
            last = max(k for k, b in enumerate(orders[a]) if tag & b)
            for b in orders[a][last + 1 :]:
                copies.append(push(a, tag, b))
            copies.append(push(a, tag, 1))
    for own in keep:
        own.finish()
    for a in range(4):
        for tag in spans(bits):
            arrived(a, tag + 1)
    for j in range(1, nc):
        block = columns.at[(c + nc - j) % nc]
        remote(block, block, send_z.at[j - 1], recv_z.at[j - 1], (s, c)).wait_recv()
    for copy in copies:
        copy.wait_send()


def gather_rows(blocks, column, ns, nc):
    any_spec = pl.BlockSpec(memory_space=pl.ANY)
    return pl.pallas_call(
        functools.partial(gather_kernel, ns, nc),
        out_shape=[jax.ShapeDtypeStruct((ns,) + b.shape, b.dtype) for b in blocks]
        + [jax.ShapeDtypeStruct((nc,) + column.shape, BF), jax.ShapeDtypeStruct((1,), jnp.int32)],
        in_specs=[any_spec] * 5,
        out_specs=[any_spec] * 5 + [pl.BlockSpec(memory_space=pltpu.SMEM)],
        scratch_shapes=[
            pltpu.SemaphoreType.DMA((4, ns)),
            pltpu.SemaphoreType.DMA((4, ns)),
            pltpu.SemaphoreType.DMA((nc - 1,)),
            pltpu.SemaphoreType.DMA((nc - 1,)),
            pltpu.SemaphoreType.DMA((5, 2)),
        ]
        + [pltpu.VMEM(b.shape, BF) for b in blocks]
        + [pltpu.VMEM(column.shape, BF)],
        compiler_params=pltpu.CompilerParams(collective_id=1, has_side_effects=True),
        cost_estimate=exchange_cost(95),
        name="gather_rows",
    )(*blocks, column)


def scatter_kernel(ns, n, *refs):
    grads, outs = refs[:n], refs[n : 2 * n]
    refs = refs[2 * n :]
    acc, got_core, got_late = refs[:n], refs[n : 2 * n], refs[2 * n : 3 * n]
    send_core, recv_core, send_late, recv_late, load_sem, out_sem = refs[3 * n :]
    s, c = lax.axis_index("shard"), lax.axis_index("ctx")
    bits = [1 << k for k in range(1, ns.bit_length() - 1)]
    nb = len(bits)
    greet([(flip(s, b), c) for b in [1] + bits])
    orders = [bits if a % 2 == 0 else bits[::-1] for a in range(n)]
    core_copies, loads, late = {}, {}, {}
    for i in range(ns // 2 - 1, -1, -1):
        for a in range(n):
            tag = spans(orders[a][::-1])[i]
            copy = remote(
                grads[a].at[flip(s, tag + 1)],
                got_core[a].at[tag // 2],
                send_core.at[a, tag // 2],
                recv_core.at[a, tag // 2],
                (flip(s, 1), c),
            )
            copy.start()
            core_copies[a, tag] = copy
            load = pltpu.make_async_copy(
                grads[a].at[flip(s, tag)], acc[a].at[tag // 2], load_sem.at[a, tag // 2]
            )
            load.start()
            loads[a, tag] = load
    def fold(a, tag, k):
        rows = acc[a].shape[1]
        if k == 0:
            loads[a, tag].wait()
            core_copies[a, tag].wait_recv()
            add_into(acc[a].at[tag // 2], got_core[a].at[tag // 2], rows)
        else:
            copy, slot = late[a, k - 1, tag]
            copy.wait_recv()
            add_into(acc[a].at[tag // 2], got_late[a].at[slot], rows)

    base = 0
    for k in range(nb):
        count = 2 ** (nb - 1 - k)
        for i in range(count - 1, -1, -1):
            for a in range(n):
                bit = orders[a][k]
                kept = spans(orders[a][k + 1 :][::-1])[i]
                fold(a, kept + bit, k)
                copy = remote(
                    acc[a].at[(kept + bit) // 2],
                    got_late[a].at[base + i],
                    send_late.at[a, base + i],
                    recv_late.at[a, base + i],
                    (flip(s, bit), c),
                )
                copy.start()
                late[a, k, kept] = (copy, base + i)
        for i in range(count - 1, -1, -1):
            for a in range(n):
                fold(a, spans(orders[a][k + 1 :][::-1])[i], k)
        base += count
    writes = []
    for a in range(n):
        fold(a, 0, nb)
        write = pltpu.make_async_copy(acc[a].at[0], outs[a], out_sem.at[a])
        write.start()
        writes.append(write)
    for copy in core_copies.values():
        copy.wait_send()
    for copy, _ in late.values():
        copy.wait_send()
    for write in writes:
        write.wait()


def scatter_rows(grads, ns):
    half = ns // 2
    n = len(grads)
    any_spec = pl.BlockSpec(memory_space=pl.ANY)
    return pl.pallas_call(
        functools.partial(scatter_kernel, ns, n),
        out_shape=[jax.ShapeDtypeStruct(g.shape[1:], BF) for g in grads],
        in_specs=[any_spec] * n,
        out_specs=[any_spec] * n,
        scratch_shapes=[pltpu.VMEM((half,) + g.shape[1:], BF) for g in grads]
        + [pltpu.VMEM((half,) + g.shape[1:], BF) for g in grads]
        + [pltpu.VMEM((half - 1,) + g.shape[1:], BF) for g in grads]
        + [
            pltpu.SemaphoreType.DMA((n, half)),
            pltpu.SemaphoreType.DMA((n, half)),
            pltpu.SemaphoreType.DMA((n, half - 1)),
            pltpu.SemaphoreType.DMA((n, half - 1)),
            pltpu.SemaphoreType.DMA((n, half)),
            pltpu.SemaphoreType.DMA((n,)),
        ],
        compiler_params=pltpu.CompilerParams(
            collective_id=2, has_side_effects=True, vmem_limit_bytes=VMEM_BYTES
        ),
        cost_estimate=exchange_cost(95),
        name="scatter_rows",
    )(*grads)


def quad_kernel(n, *refs):
    parts, passed, wide, passed_on = refs[:n], refs[n], refs[n + 1 : 2 * n + 1], refs[2 * n + 1]
    send, recv, local_sem = refs[2 * n + 2 : 2 * n + 5]
    rooms = refs[2 * n + 5 :]
    s, c = lax.axis_index("shard"), lax.axis_index("ctx")
    rank = s % TP
    greet([(flip(s, d), c) for d in (1, 2, 3)])
    copies = []
    keep = [Keep(passed, passed_on, rooms[n], local_sem.at[n])]
    for a in range(n):
        for d in (2, 3, 1):
            copy = remote(
                parts[a].at[flip(rank, d)], wide[a].at[rank], send.at[a, d], recv.at[a, d], (flip(s, d), c)
            )
            copy.start()
            copies.append(copy)
        keep.append(Keep(parts[a].at[rank], wide[a].at[rank], rooms[a], local_sem.at[a]))
    for own in keep:
        own.forward()
    for a in range(n):
        for d in (1, 2, 3):
            block = wide[a].at[flip(rank, d)]
            remote(block, block, send.at[a, d], recv.at[a, d], (s, c)).wait_recv()
    for own in keep:
        own.finish()
    for copy in copies:
        copy.wait_send()


def share_acts(acts, wide, send, recv, s, c, rank):
    copies = []

    def push(a, d, src):
        hop = 2 if d == 2 else 1
        copy = remote(
            src, wide[a].at[flip(rank, d - hop)], send.at[a, d], recv.at[a, d], (flip(s, hop), c)
        )
        copy.start()
        copies.append(copy)

    def arrived(a, d):
        block = wide[a].at[flip(rank, d)]
        remote(block, block, send.at[a, d], recv.at[a, d], (s, c)).wait_recv()

    for a in range(len(acts)):
        push(a, 2, acts[a])
        push(a, 1, acts[a])

    def finish():
        for a in range(len(acts)):
            arrived(a, 2)
            push(a, 3, wide[a].at[flip(rank, 2)])
        for a in range(len(acts)):
            arrived(a, 1)
            arrived(a, 3)
        for copy in copies:
            copy.wait_send()

    return finish


def share_quad(parts, passed, collective_id):
    any_spec = pl.BlockSpec(memory_space=pl.ANY)
    n = len(parts)
    return pl.pallas_call(
        functools.partial(quad_kernel, n),
        out_shape=[jax.ShapeDtypeStruct(p.shape, BF) for p in parts]
        + [jax.ShapeDtypeStruct(passed.shape, BF)],
        in_specs=[any_spec] * (n + 1),
        out_specs=[any_spec] * (n + 1),
        scratch_shapes=[
            pltpu.SemaphoreType.DMA((n, TP)),
            pltpu.SemaphoreType.DMA((n, TP)),
            pltpu.SemaphoreType.DMA((n + 1, 2)),
        ]
        + [pltpu.VMEM(p.shape[1:], BF) for p in parts]
        + [pltpu.VMEM(passed.shape, BF)],
        compiler_params=pltpu.CompilerParams(collective_id=collective_id, has_side_effects=True),
        cost_estimate=exchange_cost(30),
        name="share_quad",
    )(*parts, passed)


def share_kernel(ny, na, *refs):
    weight, acts, wide, wide_acts = refs[0], refs[1 : na + 1], refs[na + 1], refs[na + 2 : 2 * na + 2]
    send_far, recv_far, send_act, recv_act, local_sem = refs[2 * na + 2 : 2 * na + 7]
    rooms = refs[2 * na + 7 :]
    s, c = lax.axis_index("shard"), lax.axis_index("ctx")
    rank, y = s % TP, s // TP
    far = [(((y + j) % ny) * TP + rank, c) for j in range(1, ny)]
    greet([(flip(s, d), c) for d in (1, 2)] + far)
    finish = share_acts(acts, wide_acts, send_act, recv_act, s, c, rank)
    copies = []
    for j in range(1, ny):
        copy = remote(weight, wide.at[y], send_far.at[j - 1], recv_far.at[j - 1], far[j - 1])
        copy.start()
        copies.append(copy)
    keep = [Keep(weight, wide.at[y], rooms[na], local_sem.at[na])]
    for a in range(na):
        keep.append(Keep(acts[a], wide_acts[a].at[rank], rooms[a], local_sem.at[a]))
    for own in keep:
        own.forward()
    finish()
    for own in keep:
        own.finish()
    for j in range(1, ny):
        block = wide.at[(y + ny - j) % ny]
        remote(block, block, send_far.at[j - 1], recv_far.at[j - 1], (s, c)).wait_recv()
    for copy in copies:
        copy.wait_send()


def share_rows(weight, acts, ny):
    any_spec = pl.BlockSpec(memory_space=pl.ANY)
    na = len(acts)
    return pl.pallas_call(
        functools.partial(share_kernel, ny, na),
        out_shape=[jax.ShapeDtypeStruct((ny,) + weight.shape, BF)]
        + [jax.ShapeDtypeStruct((TP,) + act.shape, BF) for act in acts],
        in_specs=[any_spec] * (na + 1),
        out_specs=[any_spec] * (na + 1),
        scratch_shapes=[
            pltpu.SemaphoreType.DMA((ny - 1,)),
            pltpu.SemaphoreType.DMA((ny - 1,)),
            pltpu.SemaphoreType.DMA((na, TP)),
            pltpu.SemaphoreType.DMA((na, TP)),
            pltpu.SemaphoreType.DMA((na + 1, 2)),
        ]
        + [pltpu.VMEM(act.shape, BF) for act in acts]
        + [pltpu.VMEM(weight.shape, BF)],
        compiler_params=pltpu.CompilerParams(
            collective_id=3, has_side_effects=True, vmem_limit_bytes=VMEM_BYTES
        ),
        cost_estimate=exchange_cost(60),
        name="share_rows",
    )(weight, *acts)


def return_kernel(ny, pieces, *refs):
    grad, acts = refs[0], refs[1:3]
    out, act_outs = refs[3], refs[4:6]
    part, got_far, act_part, act_core, act_far = refs[6:11]
    send_far, recv_far, send_act, recv_act, load_sem, act_load, out_sem, act_sem = refs[11:]
    s, c = lax.axis_index("shard"), lax.axis_index("ctx")
    rank, y = s % TP, s // TP
    far = [(((y + j) % ny) * TP + rank, c) for j in range(1, ny)]
    greet([(flip(s, d), c) for d in (1, 2)] + far)
    act_rows = act_part.shape[2]
    rows = part.shape[1]
    act_loads, act_copies = {}, {}
    for a in range(2):
        for d in (2, 0):
            copy = remote(
                acts[a].at[flip(rank, d + 1)],
                act_core.at[a, d // 2],
                send_act.at[a, d // 2],
                recv_act.at[a, d // 2],
                (flip(s, 1), c),
            )
            copy.start()
            act_copies[a, d] = copy
            load = pltpu.make_async_copy(
                acts[a].at[flip(rank, d)], act_part.at[a, d // 2], act_load.at[a, d // 2]
            )
            load.start()
            act_loads[a, d] = load
    far_copies, loads = {}, {}
    for p in range(pieces):
        for j in range(1, ny):
            copy = remote(
                grad.at[(y + j) % ny, p],
                got_far.at[p, j - 1],
                send_far.at[p, j - 1],
                recv_far.at[p, j - 1],
                far[j - 1],
            )
            copy.start()
            far_copies[p, j] = copy
        load = pltpu.make_async_copy(grad.at[y, p], part.at[p], load_sem.at[p])
        load.start()
        loads[p] = load
    writes = []

    def finish_act(a):
        act_copies[a, 3].wait_recv()
        add_into(act_part.at[a, 0], act_far.at[a], act_rows)
        write = pltpu.make_async_copy(act_part.at[a, 0], act_outs[a], act_sem.at[a])
        write.start()
        writes.append(write)

    for a in range(2):
        for d in (2, 0):
            act_loads[a, d].wait()
            act_copies[a, d].wait_recv()
            add_into(act_part.at[a, d // 2], act_core.at[a, d // 2], act_rows)
            if d == 2:
                copy = remote(
                    act_part.at[a, 1], act_far.at[a], send_act.at[a, 2], recv_act.at[a, 2], (flip(s, 2), c)
                )
                copy.start()
                act_copies[a, 3] = copy
    for p in range(pieces):
        loads[p].wait()
        for j in range(1, ny):
            far_copies[p, j].wait_recv()
            add_into(part.at[p], got_far.at[p, j - 1], rows)
        write = pltpu.make_async_copy(part.at[p], out.at[p], out_sem.at[p])
        write.start()
        writes.append(write)
        if p == pieces // 2:
            finish_act(0)
    finish_act(1)
    for write in writes:
        write.wait()
    for group in (act_copies, far_copies):
        for copy in group.values():
            copy.wait_send()


def return_grads(grad, acts):
    ny, pieces = grad.shape[:2]
    block = grad.shape[2:]
    act = acts[0].shape[1:]
    any_spec = pl.BlockSpec(memory_space=pl.ANY)
    return pl.pallas_call(
        functools.partial(return_kernel, ny, pieces),
        out_shape=[jax.ShapeDtypeStruct(grad.shape[1:], BF)]
        + [jax.ShapeDtypeStruct(act, BF) for _ in acts],
        in_specs=[any_spec] * 3,
        out_specs=[any_spec] * 3,
        scratch_shapes=[
            pltpu.VMEM((pieces,) + block, BF),
            pltpu.VMEM((pieces, ny - 1) + block, BF),
            pltpu.VMEM((2, 2) + act, BF),
            pltpu.VMEM((2, 2) + act, BF),
            pltpu.VMEM((2,) + act, BF),
            pltpu.SemaphoreType.DMA((pieces, ny - 1)),
            pltpu.SemaphoreType.DMA((pieces, ny - 1)),
            pltpu.SemaphoreType.DMA((2, 3)),
            pltpu.SemaphoreType.DMA((2, 3)),
            pltpu.SemaphoreType.DMA((pieces,)),
            pltpu.SemaphoreType.DMA((2, 2)),
            pltpu.SemaphoreType.DMA((pieces,)),
            pltpu.SemaphoreType.DMA((2,)),
        ],
        compiler_params=pltpu.CompilerParams(
            collective_id=4, has_side_effects=True, vmem_limit_bytes=VMEM_BYTES
        ),
        cost_estimate=exchange_cost(70),
        name="return_grads",
    )(grad, *acts)


NN = (((1,), (0,)), ((), ()))
NT = (((1,), (1,)), ((), ()))
TN = (((0,), (0,)), ((), ()))


def mm(left, right, dims):
    return lax.dot_general(left, right, dims, preferred_element_type=F32)


def halves(rows):
    lane = lax.broadcasted_iota(jnp.int32, (rows, 2 * HD), 1)
    return lane < HD


def one_of(values, low, head):
    return jnp.where(low if head == 0 else jnp.logical_not(low), values, jnp.zeros_like(values))


def for_pairs(width, body):
    pairs = width // (2 * HD)

    def step(i, carry):
        body(pl.ds(pl.multiple_of(i * 2 * HD, 2 * HD), 2 * HD), 2 * i, 2)
        return carry

    lax.fori_loop(0, pairs, step, 0)
    if width % (2 * HD):
        body(pl.ds(pairs * 2 * HD, HD), 2 * pairs, 1)


def attend_kernel(q_ref, k_ref, v_ref, bias_ref, o_ref, lse_ref):
    rows, width = q_ref.shape
    keys = k_ref.shape[0]
    low = halves(keys)

    def body(cols, first, count):
        q = q_ref[:, cols]
        k = k_ref[:, cols]
        v = v_ref[:, cols]
        total = None
        for head in range(count):
            k_h = one_of(k, low, head) if count == 2 else k
            v_h = one_of(v, low, head) if count == 2 else v
            scores = mm(q, k_h, NT) + bias_ref[...]
            peak = jnp.max(scores, axis=1, keepdims=True)
            weights = jnp.exp(scores - peak)
            norm = jnp.sum(weights, axis=1, keepdims=True)
            part = mm(weights.astype(BF), v_h, NN) / norm
            total = part if total is None else total + part
            lse_ref[first + head] = peak + jnp.log(norm)
        o_ref[:, cols] = total.astype(BF)

    for_pairs(width, body)


def attend_forward(q, k, v, bias):
    heads = q.shape[1] // HD
    return pl.pallas_call(
        attend_kernel,
        out_shape=[
            jax.ShapeDtypeStruct(q.shape, BF),
            jax.ShapeDtypeStruct((heads, q.shape[0], 1), F32),
        ],
        in_specs=[pl.BlockSpec(memory_space=pltpu.VMEM)] * 4,
        out_specs=[pl.BlockSpec(memory_space=pltpu.VMEM)] * 2,
        compiler_params=pltpu.CompilerParams(vmem_limit_bytes=VMEM_BYTES),
        cost_estimate=pl.CostEstimate(
            flops=16 * q.shape[0] * k.shape[0] * q.shape[1],
            bytes_accessed=20_000_000,
            transcendentals=q.shape[0] * k.shape[0] * heads,
        ),
        name="attend_forward",
    )(q, k, v, bias)


def attend_back_kernel(q_ref, k_ref, v_ref, g_ref, lse_ref, bias_ref, _, dq_ref, dk_ref, dv_ref):
    rows, width = q_ref.shape
    keys = k_ref.shape[0]
    low_q = halves(rows)
    low_k = halves(keys)
    scale = 1.0 / math.sqrt(HD)

    def body(cols, first, count):
        q = q_ref[:, cols]
        k = k_ref[:, cols]
        v = v_ref[:, cols]
        g = g_ref[:, cols]
        dq = dk = dv = None
        for head in range(count):
            if count == 2:
                q_h, g_h = one_of(q, low_q, head), one_of(g, low_q, head)
                k_h = one_of(k, low_k, head)
            else:
                q_h, g_h, k_h = q, g, k
            scores = mm(k, q_h, NT) + bias_ref[...]
            probs = jnp.exp(scores - lse_ref[first + head])
            grad = mm(v, g_h, NT)
            both = probs * grad
            centre = jnp.sum(both, axis=0, keepdims=True)
            ds = (both - probs * centre).astype(BF)
            dq_h = mm(ds, k_h, TN)
            dk_h = mm(ds, q_h, NN)
            dv_h = mm(probs.astype(BF), g_h, NN)
            dq = dq_h if dq is None else dq + dq_h
            dk = dk_h if dk is None else dk + dk_h
            dv = dv_h if dv is None else dv + dv_h
        dq_ref[:, cols] = (dq * scale).astype(BF)
        dk_ref[:, cols] = dk.astype(BF)
        dv_ref[:, cols] = dv.astype(BF)

    for_pairs(width, body)


def attend_backward(q, k, v, g, lse, bias, ready):
    heads = q.shape[1] // HD
    return pl.pallas_call(
        attend_back_kernel,
        out_shape=[jax.ShapeDtypeStruct(x.shape, BF) for x in (q, k, v)],
        in_specs=[pl.BlockSpec(memory_space=pltpu.VMEM)] * 6 + [pl.BlockSpec(memory_space=pl.ANY)],
        out_specs=[pl.BlockSpec(memory_space=pltpu.VMEM)] * 3,
        compiler_params=pltpu.CompilerParams(vmem_limit_bytes=VMEM_BYTES),
        cost_estimate=pl.CostEstimate(
            flops=40 * q.shape[0] * k.shape[0] * q.shape[1],
            bytes_accessed=30_000_000,
            transcendentals=q.shape[0] * k.shape[0] * heads,
        ),
        name="attend_backward",
    )(q, k, v, g, lse, bias, ready)


def normed(values):
    mean = jnp.mean(values, axis=-1, keepdims=True)
    centred = values - mean
    spread = jnp.mean(centred * centred, axis=-1, keepdims=True)
    inverse = lax.rsqrt(spread + NORM_EPS)
    return centred * inverse, inverse


def norm_back(u, unit, inverse, gain):
    gu = gain * u
    grad = inverse * (
        gu - jnp.mean(gu, axis=-1, keepdims=True) - unit * jnp.mean(gu * unit, axis=-1, keepdims=True)
    )
    return grad, jnp.sum(u * unit, axis=0), jnp.sum(u, axis=0)


def adamw(master, first, second, gradient, rate, decay):
    first_new = BETA_ONE * first + (1.0 - BETA_ONE) * gradient
    second_new = BETA_TWO * second + (1.0 - BETA_TWO) * gradient * gradient
    fix_one = 1.0 - BETA_ONE**STEP
    fix_two = 1.0 - BETA_TWO**STEP
    update = first_new / fix_one / (jnp.sqrt(second_new / fix_two) + ADAM_EPS)
    master_new = master - rate * (update + decay * master)
    return (master_new, first_new, second_new, master_new.astype(BF))


def behind(token, value):
    return jnp.where(token[0] == 0, value, jnp.zeros_like(value))


def local(
    tokens,
    cotangent,
    master_qkv,
    master_out,
    master_fc,
    master_proj,
    master_small,
    first_qkv,
    first_out,
    first_fc,
    first_proj,
    first_small,
    second_qkv,
    second_out,
    second_fc,
    second_proj,
    second_small,
):
    ns, nc = lax.axis_size("shard"), lax.axis_size("ctx")
    s, c = lax.axis_index("shard"), lax.axis_index("ctx")
    ny = ns // TP
    rank = s % TP
    rows = tokens.shape[0]
    prompt_rows = PROMPT // nc
    kr = D // ns
    hs = FF // ns // TP
    hq = ns * hs
    hc = hq // nc
    pack = 8 if kr % 8 == 0 else 4
    packed = (kr // pack, pack, D)
    act_pack = (rows // 8, 8, D)
    far_groups = [[y * TP + r for y in range(ny)] for r in range(TP)]

    qc = master_qkv.shape[1]
    attn_block = jnp.concatenate([master_qkv.astype(BF), master_out.astype(BF)], axis=1)
    attn_z = lax.all_gather(attn_block, "ctx", axis=0)
    small_all = lax.all_gather(master_small.astype(BF), "shard", axis=0)
    small = small_all.transpose(1, 0, 2).reshape(master_small.shape[0], D).astype(F32)
    fc_parts = master_fc.astype(BF).reshape(kr, ns // nc, TP, hs).transpose(2, 0, 1, 3)
    proj_parts = master_proj.astype(BF).reshape(TP, hs, D // nc)
    fc_quad, proj_quad, prompt_own = share_quad(
        [fc_parts.reshape(TP, kr, hc), proj_parts], tokens[:prompt_rows], 5
    )
    prompt_tokens = lax.all_gather(prompt_own, "ctx", axis=0, tiled=True)
    fc_z = lax.all_gather(lax.optimization_barrier((attn_z, fc_quad))[1], "ctx", axis=0)

    qkv_rows = attn_z[:, :, :qc].transpose(1, 0, 2).reshape(kr, 3, D)
    out_rows = attn_z[:, :, qc:].transpose(1, 0, 2).reshape(packed)
    gathered = gather_rows(
        [qkv_rows[:, i].reshape(packed) for i in range(3)] + [out_rows], proj_quad, ns, nc
    )
    w_q, w_k, w_v, w_o = [w.reshape(D, D) for w in gathered[:4]]
    proj_z = gathered[4]
    fc_z = behind(gathered[5], fc_z).reshape(nc, TP, kr, hc)
    fc_rows = fc_z.transpose(1, 2, 0, 3).reshape((TP * packed[0],) + packed[1:2] + (hq,))
    proj_rows = proj_z.transpose(1, 2, 0, 3).reshape(TP * hs, D)
    proj_wide = lax.all_gather(
        proj_rows, "shard", axis=0, tiled=True, axis_index_groups=far_groups
    )

    own = tokens.astype(F32)
    unit_one, inverse_one = normed(own)
    all_rows = jnp.concatenate([prompt_tokens, tokens[prompt_rows:]], axis=0).astype(F32)
    unit_all = normed(all_rows)[0]
    act_all = (unit_all * small[0] + small[1]).astype(BF)
    act_one = jnp.concatenate(
        [lax.dynamic_slice_in_dim(act_all, c * prompt_rows, prompt_rows), act_all[PROMPT:]], axis=0
    )
    scale = 1.0 / math.sqrt(HD)
    q = (mm(act_one, w_q, NN) + small[4]).astype(BF) * BF(scale)
    k = mm(act_all, w_k, NN).astype(BF)
    v = (mm(act_all, w_v, NN) + small[5]).astype(BF)
    places = jnp.arange(rows, dtype=jnp.int32)
    in_prompt = places < prompt_rows
    later = places - prompt_rows
    pos_query = jnp.where(in_prompt, c * prompt_rows + places, PROMPT + later % BLK)
    seq_query = jnp.where(in_prompt, -1, later // BLK)
    cont_keys = jnp.arange(rows - prompt_rows, dtype=jnp.int32)
    pos_key = jnp.concatenate([jnp.arange(PROMPT, dtype=jnp.int32), PROMPT + cont_keys % BLK])
    seq_key = jnp.concatenate([jnp.full((PROMPT,), -1, jnp.int32), cont_keys // BLK])
    allowed = (pos_key[None, :] <= pos_query[:, None]) & (
        (seq_key[None, :] == -1) | (seq_key[None, :] == seq_query[:, None])
    )
    bias = jnp.where(allowed, 0.0, MASKED).astype(F32)
    attended, log_totals = attend_forward(q, k, v, bias)
    middle = own + mm(attended, w_o, NN) + small[6]
    unit_two, inverse_two = normed(middle)
    act_two = (unit_two * small[2] + small[3]).astype(BF)

    fc_wide, act_wide, cot_wide = share_rows(
        fc_rows, [act_two.reshape(act_pack), cotangent.reshape(act_pack)], ny
    )
    w_fc = fc_wide.reshape(D, hq)
    w_proj = proj_wide
    act_wide = act_wide.reshape(TP * rows, D)
    cot_wide = cot_wide.reshape(TP * rows, D)
    fc_bias = lax.dynamic_index_in_dim(
        small[7 : 7 + FF // D].reshape(ns, TP, hs), rank, axis=1, keepdims=False
    ).reshape(hq)
    hidden = mm(act_wide, w_fc, NN) + fc_bias
    cube = 0.7978845608028654 * (hidden + 0.044715 * hidden * hidden * hidden)
    bent = jnp.tanh(cube)
    act_three = (0.5 * hidden * (1.0 + bent)).astype(BF)
    slope = 0.5 * (1.0 + bent) + 0.5 * hidden * (1.0 - bent * bent) * 0.7978845608028654 * (
        1.0 + 3.0 * 0.044715 * hidden * hidden
    )
    grad_hidden = (mm(cot_wide, w_proj, NT) * slope).astype(BF)
    grad_proj = mm(act_three, cot_wide, TN).astype(BF)
    proj_far = lax.psum_scatter(
        grad_proj, "shard", scatter_dimension=0, tiled=True, axis_index_groups=far_groups
    )
    out_part = mm(act_three, w_proj, NN).astype(BF)
    mid_part = mm(grad_hidden, w_fc, NT).astype(BF)
    grad_fc = mm(act_wide, grad_hidden, TN).astype(BF)
    grad_fc_bias = jnp.sum(grad_hidden, axis=0, dtype=F32)
    fc_far, mid_sum, out_sum = return_grads(
        grad_fc.reshape((ny, TP) + packed),
        [mid_part.reshape((TP,) + act_pack), out_part.reshape((TP,) + act_pack)],
    )
    output = middle + out_sum.reshape(rows, D).astype(F32) + small[small.shape[0] - 1]
    proj_far = proj_far.reshape(TP * hs, nc, D // nc).transpose(1, 0, 2)
    proj_near = lax.psum_scatter(proj_far, "ctx", scatter_dimension=0)
    fc_far = fc_far.reshape(TP * kr, nc, hc).transpose(1, 0, 2)
    fc_near = lax.psum_scatter(fc_far, "ctx", scatter_dimension=0)

    grad_output = cotangent.astype(F32)
    grad_norm, gain_two, shift_two = norm_back(
        mid_sum.reshape(rows, D).astype(F32), unit_two, inverse_two, small[2]
    )
    grad_middle = grad_output + grad_norm
    grad_branch = grad_middle.astype(BF)
    grad_wo = mm(attended, grad_branch, TN).astype(BF)
    grad_attended = mm(grad_branch, w_o, NT).astype(BF)
    grad_q, grad_k, grad_v = attend_backward(
        q, k, v, grad_attended, log_totals.transpose(0, 2, 1), bias.T, proj_far
    )
    key_part = mm(grad_k, w_k, NT) + mm(grad_v, w_v, NT)
    prompt_sum = lax.psum_scatter(
        key_part[:PROMPT].astype(BF), "ctx", scatter_dimension=0, tiled=True
    )
    query_part = mm(grad_q, w_q, NT)
    grad_wq = mm(act_one, grad_q, TN).astype(BF)
    grad_wk = mm(act_all, grad_k, TN).astype(BF)
    grad_wv = mm(act_all, grad_v, TN).astype(BF)

    hidden_grads = lax.dynamic_update_index_in_dim(
        jnp.zeros((ns, TP, hs), F32), grad_fc_bias.reshape(ns, 1, hs), rank, axis=1
    )
    small_grads = jnp.concatenate(
        [
            jnp.stack(
                [
                    jnp.sum(key_part * unit_all, axis=0) + jnp.sum(query_part * unit_one, axis=0),
                    jnp.sum(key_part, axis=0) + jnp.sum(query_part, axis=0),
                    gain_two,
                    shift_two,
                    jnp.sum(grad_q, axis=0, dtype=F32),
                    jnp.sum(grad_v, axis=0, dtype=F32),
                    jnp.sum(grad_branch, axis=0, dtype=F32),
                ]
            ),
            hidden_grads.reshape(FF // D, D),
            jnp.sum(grad_output, axis=0)[None],
        ],
        axis=0,
    )
    n_small = small_grads.shape[0]
    small_parts = small_grads.reshape(n_small, ns, kr).transpose(1, 0, 2).reshape(ns, n_small * kr)
    small_parts = jnp.pad(small_parts, ((0, 0), (0, 8 * D - n_small * kr)))
    back_q, back_k, back_v, back_o, back_small = scatter_rows(
        [g.reshape((ns,) + packed) for g in (grad_wq, grad_wk, grad_wv, grad_wo)]
        + [small_parts.astype(BF).reshape(ns, 1, 8, D)],
        ns,
    )
    fc_back, proj_back, _ = share_quad(
        [fc_near.reshape(TP, kr, hc), proj_near.reshape(TP, hs, D // nc)], back_small, 6
    )
    qkv_back = jnp.concatenate([b.reshape(kr, D) for b in (back_q, back_k, back_v)], axis=1)
    attn_back = jnp.concatenate(
        [qkv_back.reshape(kr, nc, qc), back_o.reshape(kr, nc, D // nc)], axis=2
    ).transpose(1, 0, 2)
    wide_rows = attn_back.shape[2]
    small_back = back_small.reshape(8 * D)[: 8 * wide_rows].reshape(1, 8, wide_rows)
    grad_attn = lax.psum_scatter(
        jnp.concatenate([attn_back, jnp.broadcast_to(small_back, (nc, 8, wide_rows))], axis=1),
        "ctx",
        scatter_dimension=0,
    )
    small_own = grad_attn[kr:].reshape(-1)[: n_small * kr].reshape(n_small, kr).astype(F32)
    grad_act = query_part + jnp.concatenate(
        [prompt_sum.astype(F32), key_part[PROMPT:]], axis=0
    )
    grad_norm, _, _ = norm_back(grad_act, unit_one, inverse_one, small[0])
    grad_input = grad_middle + grad_norm

    gradients = (
        grad_attn[:kr, :qc].astype(F32),
        grad_attn[:kr, qc:].astype(F32),
        fc_back.reshape(TP, kr, ns // nc, hs).transpose(1, 2, 0, 3).reshape(kr, FF // nc).astype(F32),
        proj_back.reshape(TP * hs, D // nc).astype(F32),
        small_own,
    )
    masters = (master_qkv, master_out, master_fc, master_proj, master_small)
    firsts = (first_qkv, first_out, first_fc, first_proj, first_small)
    seconds = (second_qkv, second_out, second_fc, second_proj, second_small)
    rates = (D ** (-0.5), max(D // 256, 1) ** (-0.5), D ** (-0.5), FF ** (-0.5), SMALL_RATE)
    decays = (WEIGHT_DECAY, WEIGHT_DECAY, WEIGHT_DECAY, WEIGHT_DECAY, 0.0)
    results = [
        adamw(masters[i], firsts[i], seconds[i], gradients[i], rates[i], decays[i]) for i in range(5)
    ]
    return (output.astype(BF), grad_input) + tuple(results[i][j] for j in range(4) for i in range(5))


def solution(mesh):
    row_spec = P(("shard", "ctx"), None)
    weight_specs = (P("shard", "ctx"),) * 4 + (P(None, "shard"),)
    return jax.shard_map(
        local,
        mesh=mesh,
        in_specs=(row_spec, row_spec) + weight_specs * 3,
        out_specs=(row_spec, row_spec) + weight_specs * 4,
        check_vma=False,
    )
```

time: 2450 us -> 930 us (0.38)
  waiting for transfers between devices: 1800 us -> 34.9 us
  Pallas kernels: 0 us -> 466 us
  matrix products: 306 us -> 192 us
  blocking collectives: 59.8 us -> 9.47 us
  other arithmetic: 106 us -> 64 us
    reduce_scatter x4 -> x5, waiting for transfers between devices: 661 us -> 6.05 us  [the longest x1 6.04 us: local(): lax.psum_scatter(jnp.concatenate([attn_back, jnp.broadcast_to(small_back,...]
    unnamed x27 -> x9, waiting for transfers between devices: 649 us -> 0.15 us
    pallas_call x0 -> x8, Pallas kernels: none -> 466 us  [the longest x1 94.7 us: gather_rows(): pl.pallas_call(functools.partial(gather_kernel, ns, nc), out_shape=[jax.S...]
    all_gather x9 -> x4, waiting for transfers between devices: 487 us -> 28.7 us  [the longest x1 28.7 us: local(): attn_z = lax.all_gather(attn_block, 'ctx', axis=0)]
    dot_general x47 -> x18, matrix products: 306 us -> 192 us  [mm(): return lax.dot_general(left, right, dims, preferred_element_type=F32)]
    unnamed x144 -> x138, local copies, waits for them, and re-layouts: 68.6 us -> 24.9 us
    convert_element_type x12 -> x13, other arithmetic: 63.7 us -> 22.6 us  [the longest x5 14 us: adamw(): return (master_new, first_new, second_new, master_new.astype(BF))]
    reshape x5 -> x14, local copies, waits for them, and re-layouts: 0.11 us -> 40.3 us  [the longest x1 9.58 us: local(): fc_far = fc_far.reshape(TP * kr, nc, hc).transpose(1, 0, 2)]
  transfers between devices with their start and end apart: 20 -> 9, of which waited for: 18 -> 2; matrix products, arithmetic and copies ran while one was open for 12% -> 36% of each run, Pallas kernels for 0% -> 45%
where the time goes in v1:
time: 930 us; the launch traced here: 925 us
  Pallas kernels  466 us (50%)
  matrix products  192 us (21%)
  local copies, waits for them, and re-layouts  143 us (15%)
  other arithmetic  64 us (7%)
  waiting for transfers between devices  34.9 us (4%)
  between operations  15.7 us (2%)
  blocking collectives  9.47 us (1%)
    dot_general x18, matrix products, mm(): return lax.dot_general(left, right, dims, preferred_element_type=F32)  192 us
    pallas_call x1, Pallas kernels, gather_rows(): pl.pallas_call(functools.partial(gather_kernel, ns, nc), out_shape=[jax.S...  94.7 us
    pallas_call x1, Pallas kernels, scatter_rows(): pl.pallas_call(functools.partial(scatter_kernel, ns, n), out_shape=[jax.S...  94.2 us
    pallas_call x1, Pallas kernels, share_rows(): pl.pallas_call(functools.partial(share_kernel, ny, na), out_shape=[jax.Sh...  91 us
    pallas_call x1, Pallas kernels, return_grads(): pl.pallas_call(functools.partial(return_kernel, ny, pieces), out_shape=[j...  63.4 us
    pallas_call x1, Pallas kernels, attend_backward(): pl.pallas_call(attend_back_kernel, out_shape=[jax.ShapeDtypeStruct(x.shap...  46.1 us
    pallas_call x2, Pallas kernels, share_quad(): pl.pallas_call(functools.partial(quad_kernel, n), out_shape=[jax.ShapeDty...  42.8 us
    pallas_call x1, Pallas kernels, attend_forward(): pl.pallas_call(attend_kernel, out_shape=[jax.ShapeDtypeStruct(q.shape, BF...  33.9 us
  transfers between devices with their start and end apart: 9, of which 2 were waited for; matrix products, arithmetic and copies ran while one was open for 36% of the time, Pallas kernels for 45%

profile of v1, /device:TPU:0, one launch (start us, length us, event | category | flops | bytes accessed | tf_op | source)
XLA Modules:
  0.0 925.0 jit_solution(3653727656548500)
XLA Ops:
  18.0 22.2 %share_quad.2 = (bf16[4,200,400]{2,1,0:T(8,128)(2,1)}, bf16[4,200,400]{2,1,0:T(8,128)(2,1)}, bf16[256,1600]{1,0:T(8,128)(2,1)}) custom-call(bf16[4,200,400]{2,1,0:T(8,128)(2,1)} %reshape.366.refs_0_, bf16[4,200,400]{2,1,0:T(8,128)(2,1)} %bitcast.132, bf16[256,1600]{1,0:T(8,128)(2,1)} %slice.109.refs_2_), custom_call_target="tpu_custom_call" | custom-call | bytes 90000000 | tf_op jit(solution)/shard_map/share_quad/pallas_call | solution.py:334
  40.3 28.7 %all-gather.13.cloned.1.call-done = bf16[800,1600]{1,0:T(8,128)(2,1)} async-done(((bf16[200,1600]{1,0:T(8,128)(2,1)}), bf16[800,1600]{1,0:T(8,128)(2,1)}) %all-gather.13.cloned.1.call-update) | async-done | bytes 2560016 | tf_op jit(solution)/shard_map/all_gather | solution.py:719
  69.9 9.5 %all-gather.3 = bf16[8,12,200]{2,1,0:T(8,128)(2,1)S(1)} all-gather(bf16[1,12,200]{2,1,0:T(8,128)(2,1)S(1)} %convert_bitcast_fusion.2), channel_id=2, replica_groups=mesh['shard'=8,'ctx'=4] {'shard'}, dimensions={0}, use_global_device_ids=true | all-gather | bytes 43200 | tf_op jit(solution)/shard_map/all_gather | solution.py:720
  101.8 94.7 %gather_rows.1 = (bf16[8,25,8,1600]{3,2,1,0:T(8,128)(2,1)}, bf16[8,25,8,1600]{3,2,1,0:T(8,128)(2,1)}, bf16[8,25,8,1600]{3,2,1,0:T(8,128)(2,1)}, bf16[8,25,8,1600...) custom-call(bf16[25,8,1600]{2,1,0:T(8,128)(2,1)} %bitcast.139, bf16[25,8,1600]{2,1,0:T(8,128)(2,1)} %bitcast.138, ...), custom_call_target="tpu_custom_call" | custom-call | bytes 285000000 | tf_op jit(solution)/shard_map/gather_rows/pallas_call | solution.py:147
  196.5 6.3 copy.193
  202.7 6.9 reshape.379
  214.9 3.1 fusion.12
  218.2 9.1 convolution_convert_fusion.8.k_ref
  227.4 9.0 fusion.15.v_ref
  236.4 3.7 fusion.27.q_ref
  240.1 33.9 %attend_forward.1 = (bf16[384,1600]{1,0:T(8,128)(2,1)}, f32[25,384,1]{2,1,0:T(8,128)}) custom-call(bf16[384,1600]{1,0:T(8,128)(2,1)} %fusion.27.q_ref, bf16[1152,1600]{1,0:T(8,128)(2,1)} %convolution_convert_fusion.8.k_ref, bf16[1152,1600]{1,0:T(8,128)(2,1)} %fusion.15.v_ref, f32[384,1152]{1,0:T(8,128)} %and_select_fusion.1.bias_ref), custom_call_target="tpu_custom_call" | custom-call | flops 11324620800 | bytes 20000000 | tf_op jit(solution)/shard_map/attend_forward/pallas_call | solution.py:580
  274.0 4.0 reduce.16
  278.6 5.3 fusion.81
  291.7 4.2 reshape.374.refs_0_
  295.9 91.0 %share_rows.1 = (bf16[2,100,8,1600]{3,2,1,0:T(8,128)(2,1)}, bf16[4,48,8,1600]{3,2,1,0:T(8,128)(2,1)}, bf16[4,48,8,1600]{3,2,1,0:T(8,128)(2,1)}) custom-call(bf16[100,8,1600]{2,1,0:T(8,128)(2,1)} %reshape.374.refs_0_, bf16[48,8,1600]{2,1,0:T(8,128)(2,1)} %fusion.45.refs_1_, bf16[48,8,1600]{2,1,0:T(8,128)(2,1)} %bitcast.121), custom_call_target="tpu_custom_call" | custom-call | bytes 180000000 | tf_op jit(solution)/shard_map/share_rows/pallas_call | solution.py:385
  386.8 13.5 %fusion.83 = f32[1536,1600]{0,1:T(8,128)S(1)} fusion(bf16[1536,1600]{1,0:T(8,128)(2,1)} %bitcast.166, bf16[1600,1600]{1,0:T(8,128)(2,1)} %bitcast.164), kind=kOutput, calls=%fused_computation.179 | convolution fusion | flops 7864320000 | bytes 19865600 | tf_op jit(solution)/shard_map/dot_general | solution.py:529
  400.4 3.8 copy-done.51
  404.1 13.3 %convolution_convert_fusion.5 = bf16[1600,1600]{1,0:T(8,128)(2,1)} fusion(bf16[1536,1600]{1,0:T(8,128)(2,1)S(1)} %bitcast.169, f32[1536,1600]{0,1:T(8,128)S(1)} %fusion.83, f32[1600]{0:T(1024)S(1)} %add.344), kind=kOutput, calls=%fused_computation.29 | convolution fusion | flops 7891456000 | bytes 19872000 | tf_op jit(solution)/shard_map/dot_general | solution.py:529
  417.5 20.8 %convert_reduce_fusion = (bf16[1600]{0:T(1024)(128)(2,1)S(1)}, bf16[1536,1600]{0,1:T(8,128)(2,1)S(1)}) fusion(f32[1536,1600]{0,1:T(8,128)} %copy-done.51, f32[1600]{0:T(1024)S(1)} %add.344, bf16[1536,1600]{1,0:T(8,128)(2,1)} %bitcast.168, bf16[1600,1600]{1,0:T(8,128)(2,1)} %all-gather.11.cloned.1.call-done), kind=kOutput, calls=%fused_computation.9 | convolution fusion | flops 7918385664 | bytes 24790400 | tf_op jit(solution)/shard_map/dot_general | solution.py:529
  440.5 12.4 %convolution_convert_fusion = bf16[1536,1600]{0,1:T(8,128)(2,1)} fusion(bf16[1600,1600]{1,0:T(8,128)(2,1)} %bitcast.165, bf16[1536,1600]{0,1:T(8,128)(2,1)S(1)} %get-tuple-element.236), kind=kOutput, calls=%fused_computation.24 | convolution fusion | flops 7866777600 | bytes 14950400 | tf_op jit(solution)/shard_map/dot_general | solution.py:529
  452.9 7.6 copy.195
  460.5 17.0 %convolution_convert_fusion.6 = bf16[1536,1600]{0,1:T(8,128)(2,1)} fusion(bf16[1600,1600]{1,0:T(8,128)(2,1)} %all-gather.11.cloned.1.call-done, f32[1536,1600]{0,1:T(8,128)} %copy-done.51, f32[1600]{0:T(1024)S(1)} %add.344), kind=kOutput, calls=%fused_computation.30 | convolution fusion | flops 7891353600 | bytes 19872000 | tf_op jit(solution)/shard_map/dot_general | solution.py:529
  477.4 7.3 copy.196
  484.8 15.1 %convolution_convert_fusion.7 = bf16[1600,1600]{1,0:T(8,128)(2,1)} fusion(bf16[1536,1600]{1,0:T(8,128)(2,1)} %bitcast.167, bf16[1536,1600]{0,1:T(8,128)(2,1)} %copy-done.53), kind=kOutput, calls=%fused_computation.31 | convolution fusion | flops 7866880000 | bytes 14950400 | tf_op jit(solution)/shard_map/dot_general | solution.py:529
  499.9 63.4 %return_grads.1 = (bf16[4,25,8,1600]{3,2,1,0:T(8,128)(2,1)}, bf16[48,8,1600]{2,1,0:T(8,128)(2,1)}, bf16[48,8,1600]{2,1,0:T(8,128)(2,1)}) custom-call(bf16[2,4,25,8,1600]{4,3,2,1,0:T(8,128)(2,1)} %bitcast.129, bf16[4,48,8,1600]{3,2,1,0:T(8,128)(2,1)} %bitcast.114, bf16[4,48,8,1600]{3,2,1,0:T(8,128)(2,1)} %bitcast.115), custom_call_target="tpu_custom_call" | custom-call | bytes 210000000 | tf_op jit(solution)/shard_map/return_grads/pallas_call | solution.py:494
  565.0 4.0 fusion.38
  577.0 4.3 copy.198
  584.1 46.1 %attend_backward.1 = (bf16[384,1600]{1,0:T(8,128)(2,1)}, bf16[1152,1600]{1,0:T(8,128)(2,1)}, bf16[1152,1600]{1,0:T(8,128)(2,1)}) custom-call(bf16[384,1600]{1,0:T(8,128)(2,1)} %fusion.27.q_ref, bf16[1152,1600]{1,0:T(8,128)(2,1)} %convolution_convert_fusion.8.k_ref, bf16[1152,1600]{1,0:T(8,128)(2,1)} %fusion.15.v_ref, bf16[384,1600]{1,0:T(8,128)(2,1)} %copy.200.g_ref, ...), custom_call_target="tpu_custom_call" | custom-call | flops 28311552000 | bytes 30000000 | tf_op jit(solution)/shard_map/attend_backward/pallas_call | solution.py:638
  630.3 13.4 %fusion.84 = f32[1152,1600]{1,0:T(8,128)} fusion(bf16[1152,1600]{1,0:T(8,128)(2,1)} %get-tuple-element.68, bf16[1600,1600]{1,0:T(8,128)(2,1)} %bitcast.156), kind=kOutput, calls=%fused_computation.180 | convolution fusion | flops 5898240000 | bytes 16179200 | tf_op jit(solution)/shard_map/dot_general | solution.py:529
  643.7 14.1 %fusion.63 = (f32[1600]{0:T(1024)S(1)}, f32[1600]{0:T(1024)S(1)}, f32[1152,1600]{1,0:T(8,128)}) fusion(f32[1152]{0:T(1024)S(1)} %copy-done.46, f32[1152]{0:T(1024)S(1)} %copy-done.41, bf16[128,1600]{1,0:T(8,128)(2,1)S(1)} %copy-done.15, bf16[1024,1600]{1,0:T(8,128)(2,1)S(1)} %copy-done.5, f32[1152,1600]{1,0:T(8,128)} %fusion.84, ...), kind=kOutput, calls=%fused_computation.169 | convolution fusion | flops 5916668928 | bytes 27260416 | tf_op jit(solution)/shard_map/dot_general | solution.py:529
  657.8 5.0 slice.147
  662.9 9.6 %reshape.398 = bf16[800,4,400]{2,1,0:T(4,128)(2,1)S(1)} reshape(bf16[4,25,8,1600]{3,2,1,0:T(8,128)(2,1)} %get-tuple-element.75) | data formatting | bytes 5120000 | tf_op jit(solution)/shard_map/reshape | solution.py:806
  672.5 5.0 copy.207
  681.1 7.7 convolution_convert_fusion.1
  688.8 10.3 %convolution_convert_fusion.2 = bf16[1600,1600]{1,0:T(8,128)(2,1)} fusion(bf16[1152,1600]{1,0:T(8,128)(2,1)S(1)} %copy-done.12, bf16[1152,1600]{1,0:T(8,128)(2,1)S(1)} %copy-done.25), kind=kOutput, calls=%fused_computation.26 | convolution fusion | flops 5900800000 | bytes 12492800 | tf_op jit(solution)/shard_map/dot_general | solution.py:529
  700.4 7.1 fusion.82
  711.9 3.5 copy.203
  715.5 6.9 convolution_convert_fusion.4
  722.3 10.4 %convolution_convert_fusion.3 = bf16[1600,1600]{1,0:T(8,128)(2,1)} fusion(bf16[1152,1600]{1,0:T(8,128)(2,1)S(1)} %copy-done.13, bf16[1152,1600]{1,0:T(8,128)(2,1)S(1)} %copy-done.52), kind=kOutput, calls=%fused_computation.27 | convolution fusion | flops 5900800000 | bytes 12492800 | tf_op jit(solution)/shard_map/dot_general | solution.py:529
  738.6 94.2 %scatter_rows.1 = (bf16[25,8,1600]{2,1,0:T(8,128)(2,1)}, bf16[25,8,1600]{2,1,0:T(8,128)(2,1)}, bf16[25,8,1600]{2,1,0:T(8,128)(2,1)}, bf16[25,8,1600]{2,1,0:T(8,128)(2,1)}, bf16[1,8,1600]{2,1,0:T(8,128)(2,1)}) custom-call(bf16[8,25,8,1600]{3,2,1,0:T(8,128)(2,1)} %bitcast.127, bf16[8,25,8,1600]{3,2,1,0:T(8,128)(2,1)} %bitcast.128, ...), custom_call_target="tpu_custom_call" | custom-call | bytes 285000000 | tf_op jit(solution)/shard_map/scatter_rows/pallas_call | solution.py:246
  832.7 4.8 concatenate.60
  837.5 5.6 reshape.396
  843.1 3.9 reshape.397
  858.5 4.8 fusion.31
  863.3 3.2 copy.214
  866.5 20.6 %share_quad.3 = (bf16[4,200,400]{2,1,0:T(8,128)(2,1)}, bf16[4,200,400]{2,1,0:T(8,128)(2,1)}, bf16[1,8,1600]{2,1,0:T(8,128)(2,1)}) custom-call(bf16[4,200,400]{2,1,0:T(8,128)(2,1)} %bitcast.131, bf16[4,200,400]{2,1,0:T(8,128)(2,1)} %bitcast.140, bf16[1,8,1600]{2,1,0:T(8,128)(2,1)} %get-tuple-element.74.refs_2_), custom_call_target="tpu_custom_call" | custom-call | bytes 90000000 | tf_op jit(solution)/shard_map/share_quad/pallas_call | solution.py:334
  897.2 5.3 fusion.68
  905.5 6.0 reduce-scatter.10.cloned.1.call-done
  (276 shorter events, 108.1 us)
Async XLA Ops:
  7.2 61.8 %all-gather.13.cloned.1.call-start = ((), (), s32[]{:S(2)}) async-start(), calls=%async_computation.12 | async-start | bytes 3328000 | tf_op jit(solution)/shard_map/all_gather | solution.py:719
  10.6 199.7 %all-gather.9.cloned.1.call-start = ((), (), s32[]{:S(2)}) async-start(), calls=%async_computation.5 | async-start | bytes 4259840 | tf_op jit(solution)/shard_map/all_gather | solution.py:727
  17.0 261.7 %copy-start = (bf16[384,1600]{1,0:T(8,128)(2,1)}, bf16[384,1600]{1,0:T(8,128)(2,1)S(1)}, u32[]{:S(2)}) copy-start(bf16[384,1600]{1,0:T(8,128)(2,1)S(1)} %copy.177) | copy-start | bytes 3686404
  18.0 51.8 %copy-start.42 = (f32[12,200]{1,0:T(8,128)S(1)}, f32[12,200]{1,0:T(8,128)}, u32[]{:S(2)}) copy-start(f32[12,200]{1,0:T(8,128)} %param.23) | copy-start | bytes 28804
  18.0 63.0 %copy-start.22 = (bf16[384,1600]{0,1:T(8,128)(2,1)S(1)}, bf16[384,1600]{0,1:T(8,128)(2,1)}, u32[]{:S(2)}) copy-start(bf16[384,1600]{0,1:T(8,128)(2,1)} %param.18) | copy-start | bytes 3686404
  40.2 246.7 %all-gather.15.cloned.1.call-start = ((), (), s32[]{:S(2)}) async-start(), calls=%async_computation.13 | async-start | bytes 4096000 | tf_op jit(solution)/shard_map/all_gather | solution.py:728
  69.0 348.5 %all-gather.11.cloned.1.call-start = ((), (), s32[]{:S(2)}) async-start(), calls=%async_computation.6 | async-start | bytes 7987200 | tf_op jit(solution)/shard_map/all_gather | solution.py:740
  80.6 134.3 %copy-start.38 = (f32[1600]{0:T(1024)}, f32[1600]{0:T(1024)S(1)}, u32[]{:S(2)}) copy-start(f32[1600]{0:T(1024)S(1)} %mul.348) | copy-start | bytes 19204
  83.3 4.1 copy-start.26
  210.3 366.6 %reduce-scatter.6.cloned.1.call-start = ((), (), s32[]{:S(2)}) async-start(), calls=%async_computation.7 | async-start | bytes 7987200 | tf_op jit(solution)/shard_map/reduce_scatter | solution.py:792
  213.7 4.3 copy-start.40
  213.7 4.5 slice-start.4
  218.0 9.3 %copy-start.11 = (bf16[1152,1600]{1,0:T(8,128)(2,1)}, bf16[1152,1600]{1,0:T(8,128)(2,1)S(1)}, u32[]{:S(2)}) copy-start(bf16[1152,1600]{1,0:T(8,128)(2,1)S(1)} %fusion.12) | copy-start | bytes 11059204
  218.1 18.3 %copy-start.36 = (bf16[128,1600]{1,0:T(8,128)(2,1)}, bf16[128,1600]{1,0:T(8,128)(2,1)S(1)}, u32[]{:S(2)}) copy-start(bf16[128,1600]{1,0:T(8,128)(2,1)S(1)} %slice.113) | copy-start | bytes 1228804
  218.1 9.2 slice-start.2
  218.2 18.2 %copy-start.34 = (bf16[256,1600]{1,0:T(8,128)(2,1)}, bf16[256,1600]{1,0:T(8,128)(2,1)S(1)}, u32[]{:S(2)}) copy-start(bf16[256,1600]{1,0:T(8,128)(2,1)S(1)} %constant_dynamic-slice_fusion) | copy-start | bytes 2457604
  218.2 9.1 slice-start.3
  218.2 18.2 %slice-start = ((s8[5324800]{0:T(1024)(128)(4,1)}), s8[4194304]{0:T(1024)(128)(4,1)S(1)}, s32[]{:S(2)}) async-start(s8[5324800]{0:T(1024)(128)(4,1)} %bitcast.149), calls=%async_computation.14 | async-start | bytes 8388608
  227.4 9.1 slice-start.1
  274.0 4.6 copy-start.50
  386.8 17.3 %copy-start.49 = (bf16[4,48,8,1600]{3,2,1,0:T(8,128)(2,1)S(1)}, bf16[4,48,8,1600]{3,2,1,0:T(8,128)(2,1)}, u32[]{:S(2)}) copy-start(bf16[4,48,8,1600]{3,2,1,0:T(8,128)(2,1)} %get-tuple-element.61) | copy-start | bytes 14745604
  417.5 315.2 %reduce-scatter.8.cloned.1.call-start = ((), (), s32[]{:S(2)}) async-start(), calls=%async_computation.8 | async-start | bytes 4259840 | tf_op jit(solution)/shard_map/reduce_scatter | solution.py:821
  499.9 65.1 %copy-start.3 = (f32[384,1600]{1,0:T(8,128)S(1)}, f32[384,1600]{1,0:T(8,128)}, u32[]{:S(2)}) copy-start(f32[384,1600]{1,0:T(8,128)} %copy-done.2) | copy-start | bytes 7372804
  499.9 65.1 %copy-start.44 = (f32[1600]{0:T(1024)S(1)}, f32[1600]{0:T(1024)}, u32[]{:S(2)}) copy-start(f32[1600]{0:T(1024)} %add.352) | copy-start | bytes 19204
  565.0 4.1 copy-start.6
  565.0 4.1 copy-start.8
  565.0 6.6 slice-start.6
  630.2 13.4 %copy-start.5 = (bf16[1024,1600]{1,0:T(8,128)(2,1)S(1)}, bf16[1024,1600]{1,0:T(8,128)(2,1)}, u32[]{:S(2)}) copy-start(bf16[1024,1600]{1,0:T(8,128)(2,1)} %all-gather.9.cloned.1.call-done) | copy-start | bytes 9830404
  630.2 13.4 %copy-start.15 = (bf16[128,1600]{1,0:T(8,128)(2,1)S(1)}, bf16[128,1600]{1,0:T(8,128)(2,1)}, u32[]{:S(2)}) copy-start(bf16[128,1600]{1,0:T(8,128)(2,1)} %slice.110) | copy-start | bytes 1228804
  630.2 13.4 %copy-start.24 = (bf16[1152,1600]{1,0:T(8,128)(2,1)S(1)}, bf16[1152,1600]{1,0:T(8,128)(2,1)}, u32[]{:S(2)}) copy-start(bf16[1152,1600]{1,0:T(8,128)(2,1)} %get-tuple-element.69) | copy-start | bytes 11059204
  630.3 13.4 %copy-start.41 = (f32[1152]{0:T(1024)S(1)}, f32[1152]{0:T(1024)}, u32[]{:S(2)}) copy-start(f32[1152]{0:T(1024)} %copy-done.40) | copy-start | bytes 13828
  630.3 13.4 %copy-start.46 = (f32[1152]{0:T(1024)S(1)}, f32[1152]{0:T(1024)}, u32[]{:S(2)}) copy-start(f32[1152]{0:T(1024)} %copy-done.45) | copy-start | bytes 13828
  662.8 193.4 %reduce-scatter.12.cloned.1.call-start = ((), (), s32[]{:S(2)}) async-start(), calls=%async_computation.10 | async-start | bytes 3584000 | tf_op jit(solution)/shard_map/reduce_scatter | solution.py:807
  677.5 189.0 %reduce-scatter.14.cloned.1.call-start = ((), (), s32[]{:S(2)}) async-start(), calls=%async_computation.11 | async-start | bytes 4096000 | tf_op jit(solution)/shard_map/reduce_scatter | solution.py:805
  681.1 7.7 copy-start.12
  681.1 7.7 copy-start.25
  699.1 212.4 %reduce-scatter.10.cloned.1.call-start = ((), (), s32[]{:S(2)}) async-start(), calls=%async_computation.9 | async-start | bytes 3461120 | tf_op jit(solution)/shard_map/reduce_scatter | solution.py:867
  715.4 6.9 copy-start.13
  715.5 6.9 copy-start.52
  722.3 11.8 %copy-start.39 = (f32[1600]{0:T(1024)S(1)}, f32[1600]{0:T(1024)}, u32[]{:S(2)}) copy-start(f32[1600]{0:T(1024)} %copy-done.38) | copy-start | bytes 19204
  897.2 5.4 copy-start.19
  897.2 5.4 copy-start.20
  897.2 5.4 copy-start.28
  897.2 5.4 copy-start.29
  902.6 9.9 %copy-start.27 = (f32[200,400]{1,0:T(8,128)S(1)}, f32[200,400]{1,0:T(8,128)}, u32[]{:S(2)}) copy-start(f32[200,400]{1,0:T(8,128)} %param.20) | copy-start | bytes 960004
  902.6 12.6 %copy-start.33 = (f32[200,1200]{1,0:T(8,128)S(1)}, f32[200,1200]{1,0:T(8,128)}, u32[]{:S(2)}) copy-start(f32[200,1200]{1,0:T(8,128)} %param.29) | copy-start | bytes 2880004
  905.5 9.7 %copy-start.23 = (f32[200,1200]{1,0:T(8,128)S(1)}, f32[200,1200]{1,0:T(8,128)}, u32[]{:S(2)}) copy-start(f32[200,1200]{1,0:T(8,128)} %param.19) | copy-start | bytes 2880004
  905.5 9.7 %copy-start.32 = (f32[200,1200]{1,0:T(8,128)S(1)}, f32[200,1200]{1,0:T(8,128)}, u32[]{:S(2)}) copy-start(f32[200,1200]{1,0:T(8,128)} %param.24) | copy-start | bytes 2880004
  (23 other events, 55.0 us)
Sparse Core Ops, SparseCore 0:
  10.8 58.1 all-gather.12
  70.5 117.0 all-gather.8
  189.3 70.5 all-gather.14
  261.2 98.5 all-gather.10
  417.6 69.7 reduce-scatter.5
  662.9 67.7 reduce-scatter.7
  733.1 56.3 reduce-scatter.11
  791.9 62.1 reduce-scatter.13
  856.5 54.9 reduce-scatter.9

commit v2 on v1

v2 whole, which is shorter than its diff:
```python
import functools
import math

import jax
import jax.numpy as jnp
from jax import lax
from jax.experimental import pallas as pl
from jax.experimental.pallas import tpu as pltpu
from jax.sharding import PartitionSpec as P

D = 1600
HD = 64
FF = 6400
BLK = 128
PROMPT = 1024
STEP = 10
TP = 4

NORM_EPS = 1e-05
BETA_ONE = 0.9
BETA_TWO = 0.999
ADAM_EPS = 1e-08
WEIGHT_DECAY = 0.1
SMALL_RATE = 0.2
MASKED = -1e30
MESH = pl.DeviceIdType.MESH
BF = jnp.bfloat16
F32 = jnp.float32
VMEM_BYTES = 60 * 1024 * 1024


def flip(index, mask):
    bit = 1
    while bit <= mask:
        if mask & bit:
            index = index + bit - 2 * bit * ((index // bit) % 2)
        bit *= 2
    return index


def spans(bits):
    tags = [0]
    for bit in bits:
        tags = tags + [t + bit for t in tags]
    return tags


def exchange_cost(us):
    return pl.CostEstimate(flops=0, bytes_accessed=us * 3_000_000, transcendentals=0)


def greet(peers):
    barrier = pltpu.get_barrier_semaphore()
    for peer in peers:
        pl.semaphore_signal(barrier, inc=1, device_id=peer, device_id_type=MESH)
    pl.semaphore_wait(barrier, len(peers))


def remote(src, dst, send, recv, peer):
    return pltpu.make_async_remote_copy(
        src_ref=src, dst_ref=dst, send_sem=send, recv_sem=recv, device_id=peer, device_id_type=MESH
    )


class Keep:
    def __init__(self, src, dst, room, sems):
        self.load = pltpu.make_async_copy(src, room, sems.at[0])
        self.store = pltpu.make_async_copy(room, dst, sems.at[1])
        self.load.start()

    def forward(self):
        self.load.wait()
        self.store.start()

    def finish(self):
        self.store.wait()


def add_into(target, other, rows):
    def step(i, carry):
        target[i] = (target[i].astype(F32) + other[i].astype(F32)).astype(BF)
        return carry

    lax.fori_loop(0, rows, step, 0)


def gather_kernel(ns, *refs):
    srcs, dsts, token = refs[:4], refs[4:8], refs[8]
    send, recv, local_sem = refs[9:12]
    rooms = refs[12:]
    token[0] = jnp.int32(0)
    s, c = lax.axis_index("shard"), lax.axis_index("ctx")
    bits = [1 << k for k in range(1, ns.bit_length() - 1)]
    greet([(flip(s, b), c) for b in [1] + bits])
    orders = [bits, bits, bits[::-1], bits[::-1]]

    def push(a, tag, bit):
        block = dsts[a].at[flip(s, tag)]
        got = tag + bit
        copy = remote(
            srcs[a] if tag == 0 else block, block, send.at[a, got], recv.at[a, got], (flip(s, bit), c)
        )
        copy.start()
        return copy

    def arrived(a, tag):
        block = dsts[a].at[flip(s, tag)]
        remote(block, block, send.at[a, tag], recv.at[a, tag], (s, c)).wait_recv()

    copies = []
    for k in range(len(bits)):
        for a in range(4):
            copies.append(push(a, 0, orders[a][k]))
    for a in range(4):
        copies.append(push(a, 0, 1))
    keep = [Keep(srcs[a], dsts[a].at[s], rooms[a], local_sem.at[a]) for a in range(4)]
    for own in keep:
        own.forward()
    for i in range(1, len(spans(bits))):
        for a in range(4):
            tag = spans(orders[a])[i]
            arrived(a, tag)
            last = max(k for k, b in enumerate(orders[a]) if tag & b)
            for b in orders[a][last + 1 :]:
                copies.append(push(a, tag, b))
            copies.append(push(a, tag, 1))
    for own in keep:
        own.finish()
    for a in range(4):
        for tag in spans(bits):
            arrived(a, tag + 1)
    for copy in copies:
        copy.wait_send()


def gather_rows(blocks, ns):
    any_spec = pl.BlockSpec(memory_space=pl.ANY)
    return pl.pallas_call(
        functools.partial(gather_kernel, ns),
        out_shape=[jax.ShapeDtypeStruct((ns,) + b.shape, b.dtype) for b in blocks]
        + [jax.ShapeDtypeStruct((1,), jnp.int32)],
        in_specs=[any_spec] * 4,
        out_specs=[any_spec] * 4 + [pl.BlockSpec(memory_space=pltpu.SMEM)],
        scratch_shapes=[
            pltpu.SemaphoreType.DMA((4, ns)),
            pltpu.SemaphoreType.DMA((4, ns)),
            pltpu.SemaphoreType.DMA((4, 2)),
        ]
        + [pltpu.VMEM(b.shape, BF) for b in blocks],
        compiler_params=pltpu.CompilerParams(collective_id=1, has_side_effects=True),
        cost_estimate=exchange_cost(95),
        name="gather_rows",
    )(*blocks)


def scatter_kernel(ns, n, *refs):
    grads, outs = refs[:n], refs[n : 2 * n]
    refs = refs[2 * n :]
    acc, got_core, got_late = refs[:n], refs[n : 2 * n], refs[2 * n : 3 * n]
    send_core, recv_core, send_late, recv_late, load_sem, out_sem = refs[3 * n :]
    s, c = lax.axis_index("shard"), lax.axis_index("ctx")
    bits = [1 << k for k in range(1, ns.bit_length() - 1)]
    nb = len(bits)
    greet([(flip(s, b), c) for b in [1] + bits])
    orders = [bits if a % 2 == 0 else bits[::-1] for a in range(n)]
    core_copies, loads, late = {}, {}, {}
    for i in range(ns // 2 - 1, -1, -1):
        for a in range(n):
            tag = spans(orders[a][::-1])[i]
            copy = remote(
                grads[a].at[flip(s, tag + 1)],
                got_core[a].at[tag // 2],
                send_core.at[a, tag // 2],
                recv_core.at[a, tag // 2],
                (flip(s, 1), c),
            )
            copy.start()
            core_copies[a, tag] = copy
            load = pltpu.make_async_copy(
                grads[a].at[flip(s, tag)], acc[a].at[tag // 2], load_sem.at[a, tag // 2]
            )
            load.start()
            loads[a, tag] = load
    def fold(a, tag, k):
        rows = acc[a].shape[1]
        if k == 0:
            loads[a, tag].wait()
            core_copies[a, tag].wait_recv()
            add_into(acc[a].at[tag // 2], got_core[a].at[tag // 2], rows)
        else:
            copy, slot = late[a, k - 1, tag]
            copy.wait_recv()
            add_into(acc[a].at[tag // 2], got_late[a].at[slot], rows)

    base = 0
    for k in range(nb):
        count = 2 ** (nb - 1 - k)
        for i in range(count - 1, -1, -1):
            for a in range(n):
                bit = orders[a][k]
                kept = spans(orders[a][k + 1 :][::-1])[i]
                fold(a, kept + bit, k)
                copy = remote(
                    acc[a].at[(kept + bit) // 2],
                    got_late[a].at[base + i],
                    send_late.at[a, base + i],
                    recv_late.at[a, base + i],
                    (flip(s, bit), c),
                )
                copy.start()
                late[a, k, kept] = (copy, base + i)
        for i in range(count - 1, -1, -1):
            for a in range(n):
                fold(a, spans(orders[a][k + 1 :][::-1])[i], k)
        base += count
    writes = []
    for a in range(n):
        fold(a, 0, nb)
        write = pltpu.make_async_copy(acc[a].at[0], outs[a], out_sem.at[a])
        write.start()
        writes.append(write)
    for copy in core_copies.values():
        copy.wait_send()
    for copy, _ in late.values():
        copy.wait_send()
    for write in writes:
        write.wait()


def scatter_rows(grads, ns):
    half = ns // 2
    n = len(grads)
    any_spec = pl.BlockSpec(memory_space=pl.ANY)
    return pl.pallas_call(
        functools.partial(scatter_kernel, ns, n),
        out_shape=[jax.ShapeDtypeStruct(g.shape[1:], BF) for g in grads],
        in_specs=[any_spec] * n,
        out_specs=[any_spec] * n,
        scratch_shapes=[pltpu.VMEM((half,) + g.shape[1:], BF) for g in grads]
        + [pltpu.VMEM((half,) + g.shape[1:], BF) for g in grads]
        + [pltpu.VMEM((half - 1,) + g.shape[1:], BF) for g in grads]
        + [
            pltpu.SemaphoreType.DMA((n, half)),
            pltpu.SemaphoreType.DMA((n, half)),
            pltpu.SemaphoreType.DMA((n, half - 1)),
            pltpu.SemaphoreType.DMA((n, half - 1)),
            pltpu.SemaphoreType.DMA((n, half)),
            pltpu.SemaphoreType.DMA((n,)),
        ],
        compiler_params=pltpu.CompilerParams(
            collective_id=2, has_side_effects=True, vmem_limit_bytes=VMEM_BYTES
        ),
        cost_estimate=exchange_cost(95),
        name="scatter_rows",
    )(*grads)


class Parts:
    def __init__(self, parts, wide, send, recv, rooms, local_sem, s, c, rank):
        self.copies, self.keep, self.arrivals = [], [], []
        for a in range(len(parts)):
            for d in (2, 3, 1):
                copy = remote(
                    parts[a].at[flip(rank, d)],
                    wide[a].at[rank],
                    send.at[a, d],
                    recv.at[a, d],
                    (flip(s, d), c),
                )
                copy.start()
                self.copies.append(copy)
                block = wide[a].at[flip(rank, d)]
                self.arrivals.append(remote(block, block, send.at[a, d], recv.at[a, d], (s, c)))
            self.keep.append(Keep(parts[a].at[rank], wide[a].at[rank], rooms[a], local_sem.at[a]))

    def forward(self):
        for own in self.keep:
            own.forward()

    def finish(self):
        for arrival in self.arrivals:
            arrival.wait_recv()
        for own in self.keep:
            own.finish()
        for copy in self.copies:
            copy.wait_send()


class Share:
    def __init__(self, act, wide, send, recv, room, local_sem, s, c, rank):
        self.wide, self.send, self.recv, self.at, self.rank = wide, send, recv, (s, c), rank
        self.copies = []
        self.push(2, act)
        self.push(1, act)
        self.keep = Keep(act, wide.at[rank], room, local_sem)

    def push(self, d, src):
        s, c = self.at
        hop = 2 if d == 2 else 1
        copy = remote(
            src,
            self.wide.at[flip(self.rank, d - hop)],
            self.send.at[d],
            self.recv.at[d],
            (flip(s, hop), c),
        )
        copy.start()
        self.copies.append(copy)

    def arrived(self, d):
        block = self.wide.at[flip(self.rank, d)]
        remote(block, block, self.send.at[d], self.recv.at[d], self.at).wait_recv()

    def forward(self):
        self.keep.forward()
        self.arrived(2)
        self.push(3, self.wide.at[flip(self.rank, 2)])

    def finish(self):
        self.arrived(1)
        self.arrived(3)
        self.keep.finish()
        for copy in self.copies:
            copy.wait_send()


class Far:
    def __init__(self, weight, wide, send, recv, room, local_sem, s, c, ny):
        y = s // TP
        far = far_peers(s, c, ny)
        self.arrivals, self.copies = [], []
        for j in range(1, ny):
            copy = remote(weight, wide.at[y], send.at[j - 1], recv.at[j - 1], far[j - 1])
            copy.start()
            self.copies.append(copy)
            block = wide.at[(y + ny - j) % ny]
            self.arrivals.append(remote(block, block, send.at[j - 1], recv.at[j - 1], (s, c)))
        self.keep = Keep(weight, wide.at[y], room, local_sem)

    def forward(self):
        self.keep.forward()

    def finish(self):
        for arrival in self.arrivals:
            arrival.wait_recv()
        self.keep.finish()
        for copy in self.copies:
            copy.wait_send()


def far_peers(s, c, ny):
    return [((s // TP + j) % ny * TP + s % TP, c) for j in range(1, ny)]


class RowSum:
    def __init__(self, parts, out, part, core, far, send, recv, local_sem, s, c, rank):
        self.out, self.part, self.core, self.far, self.at = out, part, core, far, (s, c)
        self.send, self.recv, self.local_sem = send, recv, local_sem
        self.copies, self.loads = {}, {}
        for d in (2, 0):
            copy = remote(
                parts.at[flip(rank, d + 1)],
                core.at[d // 2],
                send.at[d // 2],
                recv.at[d // 2],
                (flip(s, 1), c),
            )
            copy.start()
            self.copies[d] = copy
            self.loads[d] = pltpu.make_async_copy(
                parts.at[flip(rank, d)], part.at[d // 2], local_sem.at[d // 2]
            )
            self.loads[d].start()

    def forward(self):
        s, c = self.at
        rows = self.part.shape[1]
        for d in (2, 0):
            self.loads[d].wait()
            self.copies[d].wait_recv()
            add_into(self.part.at[d // 2], self.core.at[d // 2], rows)
            if d == 2:
                copy = remote(
                    self.part.at[1], self.far, self.send.at[2], self.recv.at[2], (flip(s, 2), c)
                )
                copy.start()
                self.copies[3] = copy

    def finish(self):
        self.copies[3].wait_recv()
        add_into(self.part.at[0], self.far, self.part.shape[1])
        write = pltpu.make_async_copy(self.part.at[0], self.out, self.local_sem.at[2])
        write.start()
        for copy in self.copies.values():
            copy.wait_send()
        write.wait()


def quad_here():
    s, c = lax.axis_index("shard"), lax.axis_index("ctx")
    return s, c, s % TP


def first_kernel(ns, *refs):
    parts, small, passed, wide, all_small, passed_on = refs[:2], *refs[2:4], refs[4:6], *refs[6:8]
    send, recv, send_small, recv_small, local_sem = refs[8:13]
    rooms, small_room, passed_room = refs[13:15], *refs[15:]
    s, c, rank = quad_here()
    others = [((s + j) % ns, c) for j in range(1, ns)]
    greet(others)
    copies = []
    for j in range(1, ns):
        copy = remote(
            small, all_small.at[s], send_small.at[j - 1], recv_small.at[j - 1], others[j - 1]
        )
        copy.start()
        copies.append(copy)
    two = Parts(parts, wide, send, recv, rooms, local_sem, s, c, rank)
    own = Keep(small, all_small.at[s], small_room, local_sem.at[2])
    kept = Keep(passed, passed_on, passed_room, local_sem.at[3])
    own.forward()
    kept.forward()
    two.forward()
    for j in range(1, ns):
        block = all_small.at[(s + ns - j) % ns]
        remote(block, block, send_small.at[j - 1], recv_small.at[j - 1], (s, c)).wait_recv()
    two.finish()
    own.finish()
    kept.finish()
    for copy in copies:
        copy.wait_send()


def first_exchange(parts, small, passed, ns):
    any_spec = pl.BlockSpec(memory_space=pl.ANY)
    return pl.pallas_call(
        functools.partial(first_kernel, ns),
        out_shape=[jax.ShapeDtypeStruct(p.shape, BF) for p in parts]
        + [
            jax.ShapeDtypeStruct((ns,) + small.shape, BF),
            jax.ShapeDtypeStruct(passed.shape, BF),
        ],
        in_specs=[any_spec] * 4,
        out_specs=[any_spec] * 4,
        scratch_shapes=[
            pltpu.SemaphoreType.DMA((2, TP)),
            pltpu.SemaphoreType.DMA((2, TP)),
            pltpu.SemaphoreType.DMA((ns - 1,)),
            pltpu.SemaphoreType.DMA((ns - 1,)),
            pltpu.SemaphoreType.DMA((4, 2)),
        ]
        + [pltpu.VMEM(p.shape[1:], BF) for p in parts]
        + [pltpu.VMEM(x.shape, BF) for x in (small, passed)],
        compiler_params=pltpu.CompilerParams(collective_id=5, has_side_effects=True),
        cost_estimate=exchange_cost(25),
        name="first_exchange",
    )(*parts, small, passed)


def share_kernel(ny, weight, act, wide, wide_act, *refs):
    send_far, recv_far, send, recv, local_sem, room, act_room = refs
    s, c, rank = quad_here()
    greet([(flip(s, d), c) for d in (1, 2)] + far_peers(s, c, ny))
    far = Far(weight, wide, send_far, recv_far, room, local_sem.at[1], s, c, ny)
    rows = Share(act, wide_act, send, recv, act_room, local_sem.at[0], s, c, rank)
    far.forward()
    rows.forward()
    rows.finish()
    far.finish()


def share_scratch(weight, act, ny):
    return [
        pltpu.SemaphoreType.DMA((ny - 1,)),
        pltpu.SemaphoreType.DMA((ny - 1,)),
        pltpu.SemaphoreType.DMA((TP,)),
        pltpu.SemaphoreType.DMA((TP,)),
        pltpu.SemaphoreType.DMA((2, 2)),
        pltpu.VMEM(weight.shape, BF),
        pltpu.VMEM(act.shape, BF),
    ]


def share_rows(weight, act, ny):
    any_spec = pl.BlockSpec(memory_space=pl.ANY)
    return pl.pallas_call(
        functools.partial(share_kernel, ny),
        out_shape=[
            jax.ShapeDtypeStruct((ny,) + weight.shape, BF),
            jax.ShapeDtypeStruct((TP,) + act.shape, BF),
        ],
        in_specs=[any_spec] * 2,
        out_specs=[any_spec] * 2,
        scratch_shapes=share_scratch(weight, act, ny),
        compiler_params=pltpu.CompilerParams(
            collective_id=3, has_side_effects=True, vmem_limit_bytes=VMEM_BYTES
        ),
        cost_estimate=exchange_cost(60),
        name="share_rows",
    )(weight, act)


def sum_scratch(act):
    return [
        pltpu.VMEM((2,) + act, BF),
        pltpu.VMEM((2,) + act, BF),
        pltpu.VMEM(act, BF),
        pltpu.SemaphoreType.DMA((3,)),
        pltpu.SemaphoreType.DMA((3,)),
        pltpu.SemaphoreType.DMA((3,)),
    ]


def add_rows(target, other):
    def step(i, carry):
        rows = pl.ds(pl.multiple_of(i * 16, 16), 16)
        target[rows] = (target[rows].astype(F32) + other[rows].astype(F32)).astype(BF)
        return carry

    lax.fori_loop(0, target.shape[0] // 16, step, 0)


def middle_kernel(*refs):
    grad_hbm, fc_hbm, act_hbm, proj_hbm, in_hbm = refs[:5]
    sum_out, out_out, fc_out = refs[5:8]
    grad, w_fc, act, w_proj, act_in, out_part, grad_fc = refs[8:15]
    parts, core, far = refs[15:18]
    send, recv, load_sem, out_sem = refs[18:]
    s, c, rank = quad_here()
    loads = [
        pltpu.make_async_copy(src, dst, load_sem.at[i])
        for i, (src, dst) in enumerate(
            (
                (grad_hbm, grad),
                (fc_hbm, w_fc),
                (act_hbm, act),
                (proj_hbm, w_proj),
                (in_hbm, act_in),
            )
        )
    ]
    for load in loads:
        load.start()
    greet([(flip(s, d), c) for d in (1, 2)])
    rows = far.shape[0]
    loads[0].wait()
    loads[1].wait()

    def part(d):
        block = grad[pl.ds(pl.multiple_of(flip(rank, d) * rows, rows), rows), :]
        parts[d] = mm(block, w_fc[...], NT).astype(BF)

    copies = {}
    for d in (3, 1):
        part(d)
        copy = remote(
            parts.at[d], core.at[d // 2], send.at[d // 2], recv.at[d // 2], (flip(s, 1), c)
        )
        copy.start()
        copies[d] = copy
    part(2)
    copies[3].wait_recv()
    add_rows(parts.at[2], core.at[1])
    across = remote(parts.at[2], far, send.at[2], recv.at[2], (flip(s, 2), c))
    across.start()
    part(0)
    copies[1].wait_recv()
    add_rows(parts.at[0], core.at[0])
    loads[2].wait()
    loads[3].wait()
    step_rows = 256 if act.shape[0] % 256 == 0 else 128

    def out_step(i, carry):
        at = pl.ds(pl.multiple_of(i * step_rows, step_rows), step_rows)
        out_part[at, :] = mm(act[at, :], w_proj[...], NN).astype(BF)
        return carry

    lax.fori_loop(0, act.shape[0] // step_rows, out_step, 0)
    writes = [pltpu.make_async_copy(out_part, out_out, out_sem.at[0])]
    writes[0].start()
    loads[4].wait()
    width = act_in.shape[1]

    def fc_step(i, carry):
        at = pl.ds(pl.multiple_of(i * 256, 256), 256)
        grad_fc[at, :] = mm(act_in[:, at], grad[...], TN).astype(BF)
        return carry

    lax.fori_loop(0, width // 256, fc_step, 0)
    if width % 256:
        at = pl.ds(width // 256 * 256, width % 256)
        grad_fc[at, :] = mm(act_in[:, at], grad[...], TN).astype(BF)
    writes.append(pltpu.make_async_copy(grad_fc, fc_out, out_sem.at[1]))
    writes[1].start()
    across.wait_recv()
    add_rows(parts.at[0], far)
    writes.append(pltpu.make_async_copy(parts.at[0], sum_out, out_sem.at[2]))
    writes[2].start()
    for copy in copies.values():
        copy.wait_send()
    across.wait_send()
    for write in writes:
        write.wait()


def middle_rows(grad, w_fc, act, w_proj, act_in):
    any_spec = pl.BlockSpec(memory_space=pl.ANY)
    rows = grad.shape[0] // TP
    width = act_in.shape[1]
    return pl.pallas_call(
        middle_kernel,
        out_shape=[
            jax.ShapeDtypeStruct((rows, width), BF),
            jax.ShapeDtypeStruct((TP * rows, w_proj.shape[1]), BF),
            jax.ShapeDtypeStruct((width, grad.shape[1]), BF),
        ],
        in_specs=[any_spec] * 5,
        out_specs=[any_spec] * 3,
        scratch_shapes=[pltpu.VMEM(x.shape, BF) for x in (grad, w_fc, act, w_proj, act_in)]
        + [
            pltpu.VMEM((TP * rows, w_proj.shape[1]), BF),
            pltpu.VMEM((width, grad.shape[1]), BF),
            pltpu.VMEM((TP, rows, width), BF),
            pltpu.VMEM((2, rows, width), BF),
            pltpu.VMEM((rows, width), BF),
            pltpu.SemaphoreType.DMA((3,)),
            pltpu.SemaphoreType.DMA((3,)),
            pltpu.SemaphoreType.DMA((5,)),
            pltpu.SemaphoreType.DMA((3,)),
        ],
        compiler_params=pltpu.CompilerParams(
            collective_id=4, has_side_effects=True, vmem_limit_bytes=VMEM_BYTES
        ),
        cost_estimate=exchange_cost(50),
        name="middle_rows",
    )(grad, w_fc, act, w_proj, act_in)


def last_kernel(*refs):
    parts, wide = refs[:2], refs[3:5]
    send, recv, local_sem = refs[5:8]
    s, c, rank = quad_here()
    greet([(flip(s, d), c) for d in (1, 2, 3)])
    two = Parts(parts, wide, send, recv, refs[8:], local_sem, s, c, rank)
    two.forward()
    two.finish()


def last_exchange(parts, ready):
    any_spec = pl.BlockSpec(memory_space=pl.ANY)
    return pl.pallas_call(
        last_kernel,
        out_shape=[jax.ShapeDtypeStruct(p.shape, BF) for p in parts],
        in_specs=[any_spec] * 3,
        out_specs=[any_spec] * 2,
        scratch_shapes=[
            pltpu.SemaphoreType.DMA((2, TP)),
            pltpu.SemaphoreType.DMA((2, TP)),
            pltpu.SemaphoreType.DMA((2, 2)),
        ]
        + [pltpu.VMEM(p.shape[1:], BF) for p in parts],
        compiler_params=pltpu.CompilerParams(collective_id=6, has_side_effects=True),
        cost_estimate=exchange_cost(20),
        name="last_exchange",
    )(*parts, ready)


NN = (((1,), (0,)), ((), ()))
NT = (((1,), (1,)), ((), ()))
TN = (((0,), (0,)), ((), ()))


def mm(left, right, dims):
    return lax.dot_general(left, right, dims, preferred_element_type=F32)


def halves(rows):
    lane = lax.broadcasted_iota(jnp.int32, (rows, 2 * HD), 1)
    return lane < HD


def one_of(values, low, head):
    return jnp.where(low if head == 0 else jnp.logical_not(low), values, jnp.zeros_like(values))


def for_pairs(width, body, between):
    pairs = width // (2 * HD)

    def step(i, carry):
        body(pl.ds(pl.multiple_of(i * 2 * HD, 2 * HD), 2 * HD), 2 * i, 2)
        return carry

    start = 0
    for n, extra in enumerate(between):
        stop = pairs * (n + 1) // (len(between) + 1)
        lax.fori_loop(start, stop, step, 0)
        extra()
        start = stop
    lax.fori_loop(start, pairs, step, 0)
    if width % (2 * HD):
        body(pl.ds(pairs * 2 * HD, HD), 2 * pairs, 1)


def attend_kernel(ny, *refs):
    q_ref, k_ref, v_ref, bias_ref, weight, act = refs[:6]
    o_ref, lse_ref, wide, wide_act, token = refs[6:11]
    send_far, recv_far, send_act, recv_act, local_sem, room, act_room = refs[11:]
    token[0] = jnp.int32(0)
    width = q_ref.shape[1]
    low = halves(k_ref.shape[0])
    s, c, rank = quad_here()
    greet([(flip(s, d), c) for d in (1, 2)] + far_peers(s, c, ny))
    far = Far(weight, wide, send_far, recv_far, room, local_sem.at[1], s, c, ny)
    rows = Share(act, wide_act, send_act, recv_act, act_room, local_sem.at[0], s, c, rank)

    def body(cols, first, count):
        q = q_ref[:, cols]
        k = k_ref[:, cols]
        v = v_ref[:, cols]
        total = None
        for head in range(count):
            k_h = one_of(k, low, head) if count == 2 else k
            v_h = one_of(v, low, head) if count == 2 else v
            scores = mm(q, k_h, NT) + bias_ref[...]
            peak = jnp.max(scores, axis=1, keepdims=True)
            weights = jnp.exp(scores - peak)
            norm = jnp.sum(weights, axis=1, keepdims=True)
            part = mm(weights.astype(BF), v_h, NN) / norm
            total = part if total is None else total + part
            lse_ref[first + head] = peak + jnp.log(norm)
        o_ref[:, cols] = total.astype(BF)

    for_pairs(width, body, [far.forward, lambda: None, lambda: None])
    rows.forward()
    rows.finish()
    far.finish()


def attend_forward(q, k, v, bias, weight, act, ny):
    heads = q.shape[1] // HD
    vmem = pl.BlockSpec(memory_space=pltpu.VMEM)
    any_spec = pl.BlockSpec(memory_space=pl.ANY)
    return pl.pallas_call(
        functools.partial(attend_kernel, ny),
        out_shape=[
            jax.ShapeDtypeStruct(q.shape, BF),
            jax.ShapeDtypeStruct((heads, q.shape[0], 1), F32),
            jax.ShapeDtypeStruct((ny,) + weight.shape, BF),
            jax.ShapeDtypeStruct((TP,) + act.shape, BF),
            jax.ShapeDtypeStruct((1,), jnp.int32),
        ],
        in_specs=[vmem] * 4 + [any_spec] * 2,
        out_specs=[vmem] * 2 + [any_spec] * 2 + [pl.BlockSpec(memory_space=pltpu.SMEM)],
        scratch_shapes=share_scratch(weight, act, ny),
        compiler_params=pltpu.CompilerParams(
            collective_id=7, has_side_effects=True, vmem_limit_bytes=VMEM_BYTES
        ),
        cost_estimate=exchange_cost(60),
        name="attend_forward",
    )(q, k, v, bias, weight, act)


def attend_back_kernel(*refs):
    q_ref, k_ref, v_ref, g_ref, lse_ref, bias_ref, _, parts = refs[:8]
    dq_ref, dk_ref, dv_ref, out = refs[8:12]
    width = q_ref.shape[1]
    low_q = halves(q_ref.shape[0])
    low_k = halves(k_ref.shape[0])
    scale = 1.0 / math.sqrt(HD)
    s, c, rank = quad_here()
    greet([(flip(s, d), c) for d in (1, 2)])
    rows = RowSum(parts, out, *refs[12:], s, c, rank)

    def body(cols, first, count):
        q = q_ref[:, cols]
        k = k_ref[:, cols]
        v = v_ref[:, cols]
        g = g_ref[:, cols]
        dq = dk = dv = None
        for head in range(count):
            if count == 2:
                q_h, g_h = one_of(q, low_q, head), one_of(g, low_q, head)
                k_h = one_of(k, low_k, head)
            else:
                q_h, g_h, k_h = q, g, k
            scores = mm(k, q_h, NT) + bias_ref[...]
            probs = jnp.exp(scores - lse_ref[first + head])
            grad = mm(v, g_h, NT)
            both = probs * grad
            centre = jnp.sum(both, axis=0, keepdims=True)
            ds = (both - probs * centre).astype(BF)
            dq_h = mm(ds, k_h, TN)
            dk_h = mm(ds, q_h, NN)
            dv_h = mm(probs.astype(BF), g_h, NN)
            dq = dq_h if dq is None else dq + dq_h
            dk = dk_h if dk is None else dk + dk_h
            dv = dv_h if dv is None else dv + dv_h
        dq_ref[:, cols] = (dq * scale).astype(BF)
        dk_ref[:, cols] = dk.astype(BF)
        dv_ref[:, cols] = dv.astype(BF)

    for_pairs(width, body, [rows.forward, lambda: None, lambda: None])
    rows.finish()


def attend_backward(q, k, v, g, lse, bias, ready, parts):
    vmem = pl.BlockSpec(memory_space=pltpu.VMEM)
    any_spec = pl.BlockSpec(memory_space=pl.ANY)
    act = parts.shape[1:]
    return pl.pallas_call(
        attend_back_kernel,
        out_shape=[jax.ShapeDtypeStruct(x.shape, BF) for x in (q, k, v)]
        + [jax.ShapeDtypeStruct(act, BF)],
        in_specs=[vmem] * 6 + [any_spec] * 2,
        out_specs=[vmem] * 3 + [any_spec],
        scratch_shapes=sum_scratch(act),
        compiler_params=pltpu.CompilerParams(
            collective_id=8, has_side_effects=True, vmem_limit_bytes=VMEM_BYTES
        ),
        cost_estimate=exchange_cost(47),
        name="attend_backward",
    )(q, k, v, g, lse, bias, ready, parts)


def normed(values):
    mean = jnp.mean(values, axis=-1, keepdims=True)
    centred = values - mean
    spread = jnp.mean(centred * centred, axis=-1, keepdims=True)
    inverse = lax.rsqrt(spread + NORM_EPS)
    return centred * inverse, inverse


def norm_back(u, unit, inverse, gain):
    gu = gain * u
    grad = inverse * (
        gu - jnp.mean(gu, axis=-1, keepdims=True) - unit * jnp.mean(gu * unit, axis=-1, keepdims=True)
    )
    return grad, jnp.sum(u * unit, axis=0), jnp.sum(u, axis=0)


def adamw(master, first, second, gradient, rate, decay):
    first_new = BETA_ONE * first + (1.0 - BETA_ONE) * gradient
    second_new = BETA_TWO * second + (1.0 - BETA_TWO) * gradient * gradient
    fix_one = 1.0 - BETA_ONE**STEP
    fix_two = 1.0 - BETA_TWO**STEP
    update = first_new / fix_one / (jnp.sqrt(second_new / fix_two) + ADAM_EPS)
    master_new = master - rate * (update + decay * master)
    return (master_new, first_new, second_new, master_new.astype(BF))


def cuts(start, stop, width):
    found = []
    while start < stop:
        block, low = divmod(start, width)
        high = min(width, low + stop - start)
        found.append((block, low, high))
        start += high - low
    return found


def after(first, later):
    return lax.optimization_barrier((first, later))[1]


def behind(token, value):
    return jnp.where(token[0] == 0, value, jnp.zeros_like(value))


def local(
    tokens,
    cotangent,
    master_qkv,
    master_out,
    master_fc,
    master_proj,
    master_small,
    first_qkv,
    first_out,
    first_fc,
    first_proj,
    first_small,
    second_qkv,
    second_out,
    second_fc,
    second_proj,
    second_small,
):
    ns, nc = lax.axis_size("shard"), lax.axis_size("ctx")
    s, c = lax.axis_index("shard"), lax.axis_index("ctx")
    ny = ns // TP
    rank = s % TP
    rows = tokens.shape[0]
    prompt_rows = PROMPT // nc
    kr = D // ns
    hs = FF // ns // TP
    hq = ns * hs
    hc = hq // nc
    oc = D // nc
    pack = 8 if kr % 8 == 0 else 4
    packed = (kr // pack, pack, D)
    act_pack = (rows // 8, 8, D)
    far_groups = [[y * TP + r for y in range(ny)] for r in range(TP)]

    qc = master_qkv.shape[1]
    attn_block = jnp.concatenate([master_qkv.astype(BF), master_out.astype(BF)], axis=1)
    attn_z = lax.all_gather(attn_block, "ctx", axis=0)
    fc_parts = master_fc.astype(BF).reshape(kr, ns // nc, TP, hs).transpose(2, 0, 1, 3)
    proj_parts = master_proj.astype(BF).reshape(TP, hs, D // nc)
    fc_quad, proj_quad, small_all, prompt_own = first_exchange(
        [fc_parts.reshape(TP, kr, hc), proj_parts],
        master_small.astype(BF),
        tokens[:prompt_rows],
        ns,
    )
    small = small_all.transpose(1, 0, 2).reshape(master_small.shape[0], D).astype(F32)
    prompt_tokens = lax.all_gather(prompt_own, "ctx", axis=0, tiled=True)
    fc_z = lax.all_gather(after(attn_z, fc_quad), "ctx", axis=0)
    proj_z = lax.all_gather(after(attn_z, proj_quad), "ctx", axis=0)

    qkv_rows = [
        jnp.concatenate(
            [attn_z[b, :, low:high] for b, low, high in cuts(i * D, (i + 1) * D, qc)], axis=1
        )
        for i in range(3)
    ]
    out_rows = jnp.concatenate([attn_z[b, :, qc:] for b in range(nc)], axis=1)
    gathered = gather_rows([w.reshape(packed) for w in qkv_rows + [out_rows]], ns)
    w_q, w_k, w_v, w_o = [w.reshape(D, D) for w in gathered[:4]]
    fc_z = behind(gathered[4], fc_z).reshape(nc, TP * kr, hc)
    fc_rows = jnp.concatenate([fc_z[b] for b in range(nc)], axis=1)

    own = tokens.astype(F32)
    unit_one, inverse_one = normed(own)
    all_rows = jnp.concatenate([prompt_tokens, tokens[prompt_rows:]], axis=0).astype(F32)
    unit_all = normed(all_rows)[0]
    act_all = (unit_all * small[0] + small[1]).astype(BF)
    act_one = jnp.concatenate(
        [lax.dynamic_slice_in_dim(act_all, c * prompt_rows, prompt_rows), act_all[PROMPT:]], axis=0
    )
    scale = 1.0 / math.sqrt(HD)
    q = (mm(act_one, w_q, NN) + small[4]).astype(BF) * BF(scale)
    k = mm(act_all, w_k, NN).astype(BF)
    v = (mm(act_all, w_v, NN) + small[5]).astype(BF)
    places = jnp.arange(rows, dtype=jnp.int32)
    in_prompt = places < prompt_rows
    later = places - prompt_rows
    pos_query = jnp.where(in_prompt, c * prompt_rows + places, PROMPT + later % BLK)
    seq_query = jnp.where(in_prompt, -1, later // BLK)
    cont_keys = jnp.arange(rows - prompt_rows, dtype=jnp.int32)
    pos_key = jnp.concatenate([jnp.arange(PROMPT, dtype=jnp.int32), PROMPT + cont_keys % BLK])
    seq_key = jnp.concatenate([jnp.full((PROMPT,), -1, jnp.int32), cont_keys // BLK])
    allowed = (pos_key[None, :] <= pos_query[:, None]) & (
        (seq_key[None, :] == -1) | (seq_key[None, :] == seq_query[:, None])
    )
    bias = jnp.where(allowed, 0.0, MASKED).astype(F32)
    attended, log_totals, w_fc, cot_wide, token = attend_forward(
        q, k, v, bias, fc_rows.reshape(TP * packed[0], pack, hq), cotangent.reshape(act_pack), ny
    )
    middle = own + mm(attended, w_o, NN) + small[6]
    unit_two, inverse_two = normed(middle)
    act_two = (unit_two * small[2] + small[3]).astype(BF)

    proj_z = behind(token, proj_z).reshape(nc, TP * hs, oc)
    proj_rows = jnp.concatenate([proj_z[b] for b in range(nc)], axis=1)
    pack_hs = 8 if hs % 8 == 0 else 4
    w_proj, act_wide = share_rows(
        proj_rows.reshape(TP * hs // pack_hs, pack_hs, D), act_two.reshape(act_pack), ny
    )
    w_fc = w_fc.reshape(D, hq)
    w_proj = w_proj.reshape(hq, D)
    act_wide = act_wide.reshape(TP * rows, D)
    cot_wide = cot_wide.reshape(TP * rows, D)
    fc_bias = lax.dynamic_index_in_dim(
        small[7 : 7 + FF // D].reshape(ns, TP, hs), rank, axis=1, keepdims=False
    ).reshape(hq)
    hidden = mm(act_wide, w_fc, NN) + fc_bias
    cube = 0.7978845608028654 * (hidden + 0.044715 * hidden * hidden * hidden)
    bent = jnp.tanh(cube)
    act_three = (0.5 * hidden * (1.0 + bent)).astype(BF)
    slope = 0.5 * (1.0 + bent) + 0.5 * hidden * (1.0 - bent * bent) * 0.7978845608028654 * (
        1.0 + 3.0 * 0.044715 * hidden * hidden
    )
    grad_hidden = (mm(cot_wide, w_proj, NT) * slope).astype(BF)
    grad_proj = mm(act_three, cot_wide, TN).astype(BF)
    proj_far = lax.psum_scatter(
        grad_proj, "shard", scatter_dimension=0, tiled=True, axis_index_groups=far_groups
    )
    mid_sum, out_part, grad_fc = middle_rows(grad_hidden, w_fc, act_three, w_proj, act_wide)
    grad_fc_bias = jnp.sum(grad_hidden, axis=0, dtype=F32)
    fc_far = lax.psum_scatter(
        grad_fc, "shard", scatter_dimension=0, tiled=True, axis_index_groups=far_groups
    )
    proj_far = proj_far.reshape(TP * hs, nc, D // nc).transpose(1, 0, 2)
    proj_near = lax.psum_scatter(proj_far, "ctx", scatter_dimension=0)
    fc_far = fc_far.reshape(TP * kr, nc, hc).transpose(1, 0, 2)
    fc_near = lax.psum_scatter(fc_far, "ctx", scatter_dimension=0)

    grad_output = cotangent.astype(F32)
    grad_norm, gain_two, shift_two = norm_back(
        mid_sum.astype(F32), unit_two, inverse_two, small[2]
    )
    grad_middle = grad_output + grad_norm
    grad_branch = grad_middle.astype(BF)
    grad_wo = mm(attended, grad_branch, TN).astype(BF)
    grad_attended = mm(grad_branch, w_o, NT).astype(BF)
    grad_q, grad_k, grad_v, out_sum = attend_backward(
        q, k, v, grad_attended, log_totals.transpose(0, 2, 1), bias.T, proj_far,
        out_part.reshape((TP,) + act_pack),
    )
    output = middle + out_sum.reshape(rows, D).astype(F32) + small[small.shape[0] - 1]
    key_part = mm(grad_k, w_k, NT) + mm(grad_v, w_v, NT)
    prompt_sum = lax.psum_scatter(
        key_part[:PROMPT].astype(BF), "ctx", scatter_dimension=0, tiled=True
    )
    query_part = mm(grad_q, w_q, NT)
    grad_wq = mm(act_one, grad_q, TN).astype(BF)
    grad_wk = mm(act_all, grad_k, TN).astype(BF)
    grad_wv = mm(act_all, grad_v, TN).astype(BF)

    hidden_grads = lax.dynamic_update_index_in_dim(
        jnp.zeros((ns, TP, hs), F32), grad_fc_bias.reshape(ns, 1, hs), rank, axis=1
    )
    small_grads = jnp.concatenate(
        [
            jnp.stack(
                [
                    jnp.sum(key_part * unit_all, axis=0) + jnp.sum(query_part * unit_one, axis=0),
                    jnp.sum(key_part, axis=0) + jnp.sum(query_part, axis=0),
                    gain_two,
                    shift_two,
                    jnp.sum(grad_q, axis=0, dtype=F32),
                    jnp.sum(grad_v, axis=0, dtype=F32),
                    jnp.sum(grad_branch, axis=0, dtype=F32),
                ]
            ),
            hidden_grads.reshape(FF // D, D),
            jnp.sum(grad_output, axis=0)[None],
        ],
        axis=0,
    )
    n_small = small_grads.shape[0]
    small_parts = small_grads.reshape(n_small, ns, kr).transpose(1, 0, 2).reshape(ns, n_small * kr)
    small_parts = jnp.pad(small_parts, ((0, 0), (0, 8 * D - n_small * kr)))
    back_q, back_k, back_v, back_o, back_small = scatter_rows(
        [g.reshape((ns,) + packed) for g in (grad_wq, grad_wk, grad_wv, grad_wo)]
        + [small_parts.astype(BF).reshape(ns, 1, 8, D)],
        ns,
    )
    fc_back, proj_back = last_exchange(
        [fc_near.reshape(TP, kr, hc), proj_near.reshape(TP, hs, D // nc)], back_small
    )
    qkv_back = [b.reshape(kr, D) for b in (back_q, back_k, back_v)]
    back_o = back_o.reshape(kr, D)
    attn_back = jnp.stack(
        [
            jnp.concatenate(
                [qkv_back[i][:, low:high] for i, low, high in cuts(b * qc, (b + 1) * qc, D)]
                + [back_o[:, b * oc : (b + 1) * oc]],
                axis=1,
            )
            for b in range(nc)
        ]
    )
    wide_rows = attn_back.shape[2]
    small_back = back_small.reshape(8 * D)[: 8 * wide_rows].reshape(1, 8, wide_rows)
    grad_attn = lax.psum_scatter(
        jnp.concatenate([attn_back, jnp.broadcast_to(small_back, (nc, 8, wide_rows))], axis=1),
        "ctx",
        scatter_dimension=0,
    )
    small_own = grad_attn[kr:].reshape(-1)[: n_small * kr].reshape(n_small, kr).astype(F32)
    grad_act = query_part + jnp.concatenate(
        [prompt_sum.astype(F32), key_part[PROMPT:]], axis=0
    )
    grad_norm, _, _ = norm_back(grad_act, unit_one, inverse_one, small[0])
    grad_input = grad_middle + grad_norm

    gradients = (
        grad_attn[:kr, :qc].astype(F32),
        grad_attn[:kr, qc:].astype(F32),
        fc_back.reshape(TP, kr, ns // nc, hs).transpose(1, 2, 0, 3).reshape(kr, FF // nc).astype(F32),
        proj_back.reshape(TP * hs, D // nc).astype(F32),
        small_own,
    )
    masters = (master_qkv, master_out, master_fc, master_proj, master_small)
    firsts = (first_qkv, first_out, first_fc, first_proj, first_small)
    seconds = (second_qkv, second_out, second_fc, second_proj, second_small)
    rates = (D ** (-0.5), max(D // 256, 1) ** (-0.5), D ** (-0.5), FF ** (-0.5), SMALL_RATE)
    decays = (WEIGHT_DECAY, WEIGHT_DECAY, WEIGHT_DECAY, WEIGHT_DECAY, 0.0)
    results = [
        adamw(masters[i], firsts[i], seconds[i], gradients[i], rates[i], decays[i]) for i in range(5)
    ]
    return (output.astype(BF), grad_input) + tuple(results[i][j] for j in range(4) for i in range(5))


def solution(mesh):
    row_spec = P(("shard", "ctx"), None)
    weight_specs = (P("shard", "ctx"),) * 4 + (P(None, "shard"),)
    return jax.shard_map(
        local,
        mesh=mesh,
        in_specs=(row_spec, row_spec) + weight_specs * 3,
        out_specs=(row_spec, row_spec) + weight_specs * 4,
        check_vma=False,
    )
```

time: 930 us -> 832 us (0.89)
  local copies, waits for them, and re-layouts: 143 us -> 93.2 us
  matrix products: 192 us -> 154 us
  Pallas kernels: 466 us -> 454 us
  blocking collectives: 9.47 us -> 0 us
    dot_general x18 -> x15, matrix products: 192 us -> 154 us  [mm(): return lax.dot_general(left, right, dims, preferred_element_type=F32)]
    reshape x6 -> x0, local copies, waits for them, and re-layouts: 33 us -> none  [the longest x1 9.58 us: local(): fc_far = fc_far.reshape(TP * kr, nc, hc).transpose(1, 0, 2)]
    pallas_call x6, Pallas kernels: 326 us -> 310 us  [the longest x1 94.3 us: gather_rows(): pl.pallas_call(functools.partial(gather_kernel, ns), out_shape=[jax.Shape...]
    convert_element_type x2 -> x0, local copies, waits for them, and re-layouts: 14.9 us -> none  [the longest x1 7.58 us: local(): mid_part = mm(grad_hidden, w_fc, NT).astype(BF)]
    transpose x2 -> x0, local copies, waits for them, and re-layouts: 11.3 us -> none  [the longest x1 6.26 us: local(): proj_rows = proj_z.transpose(1, 2, 0, 3).reshape(TP * hs, D)]
    concatenate x2 -> x8, local copies, waits for them, and re-layouts: 6.62 us -> 17.1 us  [the longest x1 5.74 us: local(): proj_rows = jnp.concatenate([proj_z[b] for b in range(nc)], axis=1)]
    all_gather x1 -> x0, blocking collectives: 9.47 us -> none  [local(): small_all = lax.all_gather(master_small.astype(BF), 'shard', axis=0)]
    unnamed x138 -> x132, local copies, waits for them, and re-layouts: 24.9 us -> 15.8 us
  transfers between devices with their start and end apart: 9 -> 10, of which waited for: 2 -> 3; matrix products, arithmetic and copies ran while one was open for 36% -> 31% of each run, Pallas kernels for 45% -> 48%
where the time goes in v2:
time: 832 us; the launch traced here: 825 us
  Pallas kernels  454 us (55%)
  matrix products  154 us (19%)
  local copies, waits for them, and re-layouts  93.2 us (11%)
  other arithmetic  73.1 us (9%)
  waiting for transfers between devices  33.6 us (4%)
  between operations  16.9 us (2%)
    dot_general x15, matrix products, mm(): return lax.dot_general(left, right, dims, preferred_element_type=F32)  154 us
    pallas_call x1, Pallas kernels, scatter_rows(): pl.pallas_call(functools.partial(scatter_kernel, ns, n), out_shape=[jax.S...  94.4 us
    pallas_call x1, Pallas kernels, gather_rows(): pl.pallas_call(functools.partial(gather_kernel, ns), out_shape=[jax.Shape...  94.3 us
    pallas_call x1, Pallas kernels, attend_forward(): pl.pallas_call(functools.partial(attend_kernel, ny), out_shape=[jax.Shape...  67.6 us
    pallas_call x1, Pallas kernels, share_rows(): pl.pallas_call(functools.partial(share_kernel, ny), out_shape=[jax.ShapeD...  59.8 us
    pallas_call x1, Pallas kernels, attend_backward(): pl.pallas_call(attend_back_kernel, out_shape=[jax.ShapeDtypeStruct(x.shap...  50.3 us
    pallas_call x1, Pallas kernels, middle_rows(): pl.pallas_call(middle_kernel, out_shape=[jax.ShapeDtypeStruct((rows, widt...  43 us
    all_gather x1, waiting for transfers between devices, local(): attn_z = lax.all_gather(attn_block, 'ctx', axis=0)  26.4 us
  transfers between devices with their start and end apart: 10, of which 3 were waited for; matrix products, arithmetic and copies ran while one was open for 31% of the time, Pallas kernels for 48%

profile of v2, /device:TPU:0, one launch (start us, length us, event | category | flops | bytes accessed | tf_op | source)
XLA Modules:
  0.0 825.4 jit_solution(12500972067780597951)
XLA Ops:
  18.6 23.9 %first_exchange.1 = (bf16[4,200,400]{2,1,0:T(8,128)(2,1)}, bf16[4,200,400]{2,1,0:T(8,128)(2,1)}, bf16[8,12,200]{2,1,0:T(8,128)(2,1)}, bf16[256,1600]{1,0:T(8,128)(2,1)}) custom-call(bf16[4,200,400]{2,1,0:T(8,128)(2,1)} %reshape.396.refs_0_, bf16[4,200,400]{2,1,0:T(8,128)(2,1)} %bitcast.131, bf16[12,200]{1,0:T(8,128)(2,1)} %convert_element_type.149.refs_2_, ...), custom_call_target="tpu_custom_call" | custom-call | bytes 75000000 | tf_op jit(solution)/shard_map/first_exchange/pallas_call | solution.py:436
  42.6 26.4 %all-gather.10.cloned.1.call-done = bf16[800,1600]{1,0:T(8,128)(2,1)} async-done(((bf16[200,1600]{1,0:T(8,128)(2,1)}), bf16[800,1600]{1,0:T(8,128)(2,1)}) %all-gather.10.cloned.1.call-update) | async-done | bytes 2560016 | tf_op jit(solution)/shard_map/all_gather | solution.py:906
  81.0 94.3 %gather_rows.1 = (bf16[8,25,8,1600]{3,2,1,0:T(8,128)(2,1)}, bf16[8,25,8,1600]{3,2,1,0:T(8,128)(2,1)}, bf16[8,25,8,1600]{3,2,1,0:T(8,128)(2,1)}, bf16[8,25,8,1600]{3,2,1,0:T(8,128)(2,1)}, s32[1]{0:T(128)}) custom-call(bf16[25,8,1600]{2,1,0:T(8,128)(2,1)} %get-tuple-element.249.refs_0_, bf16[25,8,1600]{2,1,0:T(8,128)(2,1)} %pad_maximum_fusion.7.refs_1_, ...), custom_call_target="tpu_custom_call" | custom-call | bytes 285000000 | tf_op jit(solution)/shard_map/gather_rows/pallas_call | solution.py:138
  176.0 2.7 convert_reduce_fusion.1
  180.3 2.6 fusion.12
  183.0 9.3 %convolution_convert_fusion.5.refs_1_ = bf16[1152,1600]{1,0:T(8,128)(2,1)} fusion(bf16[1152,1600]{1,0:T(8,128)(2,1)S(1)} %fusion.12, bf16[1600,1600]{1,0:T(8,128)(2,1)S(1)} %bitcast.163), kind=kOutput, calls=%fused_computation.29 | convolution fusion | flops 5900083200 | bytes 12492800 | tf_op jit(solution)/shard_map/dot_general | solution.py:674
  192.4 3.7 fusion.26.refs_0_
  196.2 9.3 %fusion.15.refs_2_ = bf16[1152,1600]{1,0:T(8,128)(2,1)} fusion(bf16[1152,1600]{1,0:T(8,128)(2,1)S(1)} %fusion.12, bf16[1600,1600]{1,0:T(8,128)(2,1)S(1)} %bitcast.159, f32[1600]{0:T(1024)S(1)} %add.325), kind=kOutput, calls=%fused_computation.23 | convolution fusion | flops 5901926400 | bytes 12499200 | tf_op jit(solution)/shard_map/dot_general | solution.py:674
  207.9 4.0 concatenate.135.refs_4_
  211.9 67.6 %attend_forward.1 = (bf16[384,1600]{1,0:T(8,128)(2,1)}, f32[25,384,1]{2,1,0:T(8,128)}, bf16[2,100,8,1600]{3,2,1,0:T(8,128)(2,1)}, bf16[4,48,8,1600]{3,2,1,0:T(8,128)(2,1)}, s32[1]{0:T(128)}) custom-call(bf16[384,1600]{1,0:T(8,128)(2,1)} %fusion.26.refs_0_, bf16[1152,1600]{1,0:T(8,128)(2,1)} %convolution_convert_fusion.5.refs_1_, ...), custom_call_target="tpu_custom_call" | custom-call | bytes 180000000 | tf_op jit(solution)/shard_map/attend_forward/pallas_call | solution.py:743
  284.9 5.3 fusion.82
  292.2 5.7 concatenate.140.weight
  298.0 59.8 %share_rows.1 = (bf16[2,100,8,1600]{3,2,1,0:T(8,128)(2,1)}, bf16[4,48,8,1600]{3,2,1,0:T(8,128)(2,1)}) custom-call(bf16[100,8,1600]{2,1,0:T(8,128)(2,1)} %concatenate.140.weight, bf16[48,8,1600]{2,1,0:T(8,128)(2,1)} %fusion.43.act), custom_call_target="tpu_custom_call" | custom-call | bytes 180000000 | tf_op jit(solution)/shard_map/share_rows/pallas_call | solution.py:486
  357.8 15.5 %multiply_convert_fusion = (bf16[1536,1600]{1,0:T(8,128)(2,1)S(1)}, f32[1536,1600]{1,0:T(8,128)}) fusion(f32[1600]{0:T(1024)S(1)} %add.346, bf16[1536,1600]{1,0:T(8,128)(2,1)} %bitcast.121, bf16[1600,1600]{1,0:T(8,128)(2,1)} %bitcast.115), kind=kOutput, calls=%fused_computation.10 | convolution fusion | flops 7888896000 | bytes 24787200 | tf_op jit(solution)/shard_map/dot_general | solution.py:674
  375.5 14.4 %convolution_convert_fusion.4 = bf16[1600,1600]{1,0:T(8,128)(2,1)} fusion(bf16[1536,1600]{1,0:T(8,128)(2,1)S(1)} %get-tuple-element.240.refs_2_, bf16[1536,1600]{1,0:T(8,128)(2,1)} %bitcast.166), kind=kOutput, calls=%fused_computation.28 | convolution fusion | flops 7866880000 | bytes 14950400 | tf_op jit(solution)/shard_map/dot_general | solution.py:674
  389.9 20.2 %convert_reduce_fusion = (bf16[1600]{0:T(1024)(128)(2,1)S(1)}, bf16[1536,1600]{1,0:T(8,128)(2,1)}) fusion(f32[1536,1600]{1,0:T(8,128)} %get-tuple-element.241, f32[1600]{0:T(1024)S(1)} %add.346, bf16[1536,1600]{1,0:T(8,128)(2,1)} %bitcast.167, bf16[1600,1600]{1,0:T(8,128)(2,1)} %bitcast.118), kind=kOutput, calls=%fused_computation.9 | convolution fusion | flops 7918385664 | bytes 24790400 | tf_op jit(solution)/shard_map/dot_general | solution.py:674
  410.2 43.0 %middle_rows.1 = (bf16[384,1600]{1,0:T(8,128)(2,1)}, bf16[1536,1600]{1,0:T(8,128)(2,1)}, bf16[1600,1600]{1,0:T(8,128)(2,1)}) custom-call(bf16[1536,1600]{1,0:T(8,128)(2,1)} %get-tuple-element.246.refs_0_, bf16[1600,1600]{1,0:T(8,128)(2,1)} %bitcast.116, bf16[1536,1600]{1,0:T(8,128)(2,1)} %copy-done.18, bf16[1600,1600]{1,0:T(8,128)(2,1)} %bitcast.119, ...), custom_call_target="tpu_custom_call" | custom-call | bytes 150000000 | tf_op jit(solution)/shard_map/middle_rows/pallas_call | solution.py:610
  453.3 2.7 and_select_fusion.refs_5_
  456.0 3.7 reduce.13
  460.4 2.5 fusion.37
  465.7 6.6 convolution_convert_fusion.6
  474.8 5.3 copy.138
  480.0 4.7 copy.139
  484.7 50.3 %attend_backward.1 = (bf16[384,1600]{1,0:T(8,128)(2,1)}, bf16[1152,1600]{1,0:T(8,128)(2,1)}, bf16[1152,1600]{1,0:T(8,128)(2,1)}, bf16[48,8,1600]{2,1,0:T(8,128)(2,1)}) custom-call(bf16[384,1600]{1,0:T(8,128)(2,1)} %fusion.26.refs_0_, bf16[1152,1600]{1,0:T(8,128)(2,1)} %convolution_convert_fusion.5.refs_1_, bf16[1152,1600]{1,0:T(8,128)(2,1)} %fusion.15.refs_2_, ...), custom_call_target="tpu_custom_call" | custom-call | bytes 141000000 | tf_op jit(solution)/shard_map/attend_backward/pallas_call | solution.py:810
  535.1 13.1 %fusion.84 = f32[1152,1600]{1,0:T(8,128)} fusion(bf16[1152,1600]{1,0:T(8,128)(2,1)} %get-tuple-element.76, bf16[1600,1600]{1,0:T(8,128)(2,1)} %bitcast.160), kind=kOutput, calls=%fused_computation.189 | convolution fusion | flops 5898240000 | bytes 16179200 | tf_op jit(solution)/shard_map/dot_general | solution.py:674
  548.2 15.1 %fusion.61 = (f32[1600]{0:T(1024)S(1)}, f32[1600]{0:T(1024)S(1)}, f32[1152,1600]{1,0:T(8,128)}) fusion(f32[1152]{0:T(1024)S(1)} %copy-done.48, f32[1152]{0:T(1024)S(1)} %copy-done.42, bf16[128,1600]{1,0:T(8,128)(2,1)S(1)} %copy-done.11, bf16[1024,1600]{1,0:T(8,128)(2,1)S(1)} %copy-done.5, f32[1152,1600]{1,0:T(8,128)} %fusion.84, ...), kind=kOutput, calls=%fused_computation.176 | convolution fusion | flops 5916668928 | bytes 27260416 | tf_op jit(solution)/shard_map/dot_general | solution.py:674
  563.3 5.0 slice.288
  568.5 5.2 copy.146
  579.8 7.7 convolution_convert_fusion
  587.5 5.4 convolution_convert_fusion.3
  593.0 4.6 fusion.83
  597.6 10.3 %convolution_convert_fusion.1 = bf16[1600,1600]{1,0:T(8,128)(2,1)} fusion(bf16[1152,1600]{1,0:T(8,128)(2,1)S(1)} %copy-done.9, bf16[1152,1600]{1,0:T(8,128)(2,1)S(1)} %copy-done.21), kind=kOutput, calls=%fused_computation.25 | convolution fusion | flops 5900800000 | bytes 12492800 | tf_op jit(solution)/shard_map/dot_general | solution.py:674
  609.5 2.8 reduce.2
  613.8 3.4 copy.143
  617.2 13.1 %convolution_convert_fusion.2 = bf16[1600,1600]{1,0:T(8,128)(2,1)} fusion(bf16[1152,1600]{1,0:T(8,128)(2,1)} %copy-done.8, bf16[1152,1600]{1,0:T(8,128)(2,1)} %get-tuple-element.76), kind=kOutput, calls=%fused_computation.26 | convolution fusion | flops 5900800000 | bytes 12492800 | tf_op jit(solution)/shard_map/dot_general | solution.py:674
  633.1 3.7 fusion.62
  638.1 94.4 %scatter_rows.1 = (bf16[25,8,1600]{2,1,0:T(8,128)(2,1)}, bf16[25,8,1600]{2,1,0:T(8,128)(2,1)}, bf16[25,8,1600]{2,1,0:T(8,128)(2,1)}, bf16[25,8,1600]{2,1,0:T(8,128)(2,1)}, bf16[1,8,1600]{2,1,0:T(8,128)(2,1)}) custom-call(bf16[8,25,8,1600]{3,2,1,0:T(8,128)(2,1)} %bitcast.113, bf16[8,25,8,1600]{3,2,1,0:T(8,128)(2,1)} %bitcast.117, ...), custom_call_target="tpu_custom_call" | custom-call | bytes 285000000 | tf_op jit(solution)/shard_map/scatter_rows/pallas_call | solution.py:234
  751.1 2.6 fusion.40
  753.7 2.6 copy.152
  758.6 4.7 fusion.30
  763.3 3.2 copy.153
  766.6 20.9 %last_exchange.1 = (bf16[4,200,400]{2,1,0:T(8,128)(2,1)}, bf16[4,200,400]{2,1,0:T(8,128)(2,1)}) custom-call(bf16[4,200,400]{2,1,0:T(8,128)(2,1)} %bitcast.126, bf16[4,200,400]{2,1,0:T(8,128)(2,1)} %bitcast.140, bf16[1,8,1600]{2,1,0:T(8,128)(2,1)} %get-tuple-element.82.refs_2_), custom_call_target="tpu_custom_call" | custom-call | bytes 60000000 | tf_op jit(solution)/shard_map/last_exchange/pallas_call | solution.py:651
  787.4 3.1 reshape.426
  791.6 2.8 reshape.424
  797.6 5.3 fusion.66
  802.9 2.9 fusion.68
  805.9 5.7 reduce-scatter.11.cloned.1.call-done
  812.5 2.8 fusion.70
  (269 shorter events, 84.0 us)
Async XLA Ops:
  7.2 4.1 copy-start.14
  7.2 61.8 %all-gather.10.cloned.1.call-start = ((), (), s32[]{:S(2)}) async-start(), calls=%async_computation.13 | async-start | bytes 3328000 | tf_op jit(solution)/shard_map/all_gather | solution.py:906
  10.7 165.4 %all-gather.8.cloned.1.call-start = ((), (), s32[]{:S(2)}) async-start(), calls=%async_computation.6 | async-start | bytes 4259840 | tf_op jit(solution)/shard_map/all_gather | solution.py:916
  17.6 51.5 %copy-start = (bf16[384,1600]{1,0:T(8,128)(2,1)}, bf16[384,1600]{1,0:T(8,128)(2,1)S(1)}, u32[]{:S(2)}) copy-start(bf16[384,1600]{1,0:T(8,128)(2,1)S(1)} %copy.124) | copy-start | bytes 3686404
  18.6 52.0 %copy-start.19 = (bf16[384,1600]{0,1:T(8,128)(2,1)S(1)}, bf16[384,1600]{0,1:T(8,128)(2,1)}, u32[]{:S(2)}) copy-start(bf16[384,1600]{0,1:T(8,128)(2,1)} %param.18) | copy-start | bytes 3686404
  42.5 26.6 %copy-start.43 = (bf16[8,12,200]{2,1,0:T(8,128)(2,1)S(1)}, bf16[8,12,200]{2,1,0:T(8,128)(2,1)}, u32[]{:S(2)}) copy-start(bf16[8,12,200]{2,1,0:T(8,128)(2,1)} %get-tuple-element.55) | copy-start | bytes 115204
  42.6 162.9 %all-gather.12.cloned.1.call-start = ((), (), s32[]{:S(2)}) async-start(), calls=%async_computation.14 | async-start | bytes 4096000 | tf_op jit(solution)/shard_map/all_gather | solution.py:917
  69.0 211.1 %all-gather.14.cloned.1.call-start = ((), (), s32[]{:S(2)}) async-start(), calls=%async_computation.15 | async-start | bytes 4096000 | tf_op jit(solution)/shard_map/all_gather | solution.py:918
  69.1 111.1 %copy-start.10 = (bf16[128,1600]{1,0:T(8,128)(2,1)}, bf16[128,1600]{1,0:T(8,128)(2,1)S(1)}, u32[]{:S(2)}) copy-start(bf16[128,1600]{1,0:T(8,128)(2,1)S(1)} %slice.218) | copy-start | bytes 1228804
  70.2 110.1 %copy-start.39 = (f32[1600]{0:T(1024)}, f32[1600]{0:T(1024)S(1)}, u32[]{:S(2)}) copy-start(f32[1600]{0:T(1024)S(1)} %mul.343) | copy-start | bytes 19204
  77.8 397.0 %reduce-scatter.7.cloned.1.call-start = ((), (), s32[]{:S(2)}) async-start(), calls=%async_computation.7 | async-start | bytes 7987200 | tf_op jit(solution)/shard_map/reduce_scatter | solution.py:985
  176.0 6.9 slice-start.6
  179.1 3.8 copy-start.41
  180.3 12.1 %slice-start = ((s8[5324800]{0:T(1024)(128)(4,1)}), s8[1130496]{0:T(1024)(128)(4,1)S(1)}, s32[]{:S(2)}) async-start(s8[5324800]{0:T(1024)(128)(4,1)} %bitcast.150), calls=%async_computation.16 | async-start | bytes 2260992
  182.9 13.2 %copy-start.8 = (bf16[1152,1600]{1,0:T(8,128)(2,1)}, bf16[1152,1600]{1,0:T(8,128)(2,1)S(1)}, u32[]{:S(2)}) copy-start(bf16[1152,1600]{1,0:T(8,128)(2,1)S(1)} %fusion.12) | copy-start | bytes 11059204
  182.9 9.4 %slice-start.1 = ((s8[5324800]{0:T(1024)(128)(4,1)}), s8[4194304]{0:T(1024)(128)(4,1)S(1)}, s32[]{:S(2)}) async-start(s8[5324800]{0:T(1024)(128)(4,1)} %bitcast.150), calls=%async_computation.17 | async-start | bytes 8388608
  192.3 3.9 copy-start.32
  192.3 3.9 slice-start.4
  192.3 3.8 copy-start.36
  192.4 3.8 slice-start.5
  389.9 178.6 %reduce-scatter.13.cloned.1.call-start = ((), (), s32[]{:S(2)}) async-start(), calls=%async_computation.10 | async-start | bytes 7987200 | tf_op jit(solution)/shard_map/reduce_scatter | solution.py:990
  453.2 178.3 %reduce-scatter.9.cloned.1.call-start = ((), (), s32[]{:S(2)}) async-start(), calls=%async_computation.8 | async-start | bytes 4259840 | tf_op jit(solution)/shard_map/reduce_scatter | solution.py:1012
  535.1 13.2 %copy-start.5 = (bf16[1024,1600]{1,0:T(8,128)(2,1)S(1)}, bf16[1024,1600]{1,0:T(8,128)(2,1)}, u32[]{:S(2)}) copy-start(bf16[1024,1600]{1,0:T(8,128)(2,1)} %all-gather.8.cloned.1.call-done) | copy-start | bytes 9830404
  535.1 13.2 %copy-start.11 = (bf16[128,1600]{1,0:T(8,128)(2,1)S(1)}, bf16[128,1600]{1,0:T(8,128)(2,1)}, u32[]{:S(2)}) copy-start(bf16[128,1600]{1,0:T(8,128)(2,1)} %copy-done.10) | copy-start | bytes 1228804
  535.1 13.2 %copy-start.42 = (f32[1152]{0:T(1024)S(1)}, f32[1152]{0:T(1024)}, u32[]{:S(2)}) copy-start(f32[1152]{0:T(1024)} %copy-done.41) | copy-start | bytes 13828
  535.1 13.1 %copy-start.48 = (f32[1152]{0:T(1024)S(1)}, f32[1152]{0:T(1024)}, u32[]{:S(2)}) copy-start(f32[1152]{0:T(1024)} %copy-done.47) | copy-start | bytes 13828
  568.4 187.9 %reduce-scatter.15.cloned.1.call-start = ((), (), s32[]{:S(2)}) async-start(), calls=%async_computation.11 | async-start | bytes 3584000 | tf_op jit(solution)/shard_map/reduce_scatter | solution.py:996
  573.8 192.8 %reduce-scatter.17.cloned.1.call-start = ((), (), s32[]{:S(2)}) async-start(), calls=%async_computation.12 | async-start | bytes 4096000 | tf_op jit(solution)/shard_map/reduce_scatter | solution.py:994
  579.8 7.7 copy-start.27
  579.8 7.7 copy-start.33
  579.8 7.7 copy-start.37
  579.8 13.2 %slice-start.2 = ((s8[5324800]{0:T(1024)(128)(4,1)}), s8[4194304]{0:T(1024)(128)(4,1)S(1)}, s32[]{:S(2)}) async-start(s8[5324800]{0:T(1024)(128)(4,1)} %bitcast.153), calls=%async_computation.18 | async-start | bytes 8388608
  587.5 5.5 slice-start.3
  593.0 4.6 copy-start.9
  593.0 4.6 copy-start.21
  608.0 203.6 %reduce-scatter.11.cloned.1.call-start = ((), (), s32[]{:S(2)}) async-start(), calls=%async_computation.9 | async-start | bytes 3461120 | tf_op jit(solution)/shard_map/reduce_scatter | solution.py:1066
  732.6 7.4 copy-start.31
  732.6 8.4 %copy-start.35 = (bf16[25,8,1600]{2,1,0:T(8,128)(2,1)S(1)}, bf16[25,8,1600]{2,1,0:T(8,128)(2,1)}, u32[]{:S(2)}) copy-start(bf16[25,8,1600]{2,1,0:T(8,128)(2,1)} %get-tuple-element.80) | copy-start | bytes 1920004
  742.0 6.3 copy-start.38
  753.7 4.9 copy-start.3
  797.5 5.4 copy-start.15
  797.5 5.4 copy-start.16
  797.5 5.4 copy-start.25
  797.5 5.4 copy-start.26
  802.9 9.5 %copy-start.24 = (f32[200,400]{1,0:T(8,128)S(1)}, f32[200,400]{1,0:T(8,128)}, u32[]{:S(2)}) copy-start(f32[200,400]{1,0:T(8,128)} %param.20) | copy-start | bytes 960004
  802.9 12.3 %copy-start.30 = (f32[200,1200]{1,0:T(8,128)S(1)}, f32[200,1200]{1,0:T(8,128)}, u32[]{:S(2)}) copy-start(f32[200,1200]{1,0:T(8,128)} %param.29) | copy-start | bytes 2880004
  805.9 9.4 %copy-start.20 = (f32[200,1200]{1,0:T(8,128)S(1)}, f32[200,1200]{1,0:T(8,128)}, u32[]{:S(2)}) copy-start(f32[200,1200]{1,0:T(8,128)} %param.19) | copy-start | bytes 2880004
  805.9 9.4 %copy-start.29 = (f32[200,1200]{1,0:T(8,128)S(1)}, f32[200,1200]{1,0:T(8,128)}, u32[]{:S(2)}) copy-start(f32[200,1200]{1,0:T(8,128)} %param.24) | copy-start | bytes 2880004
  (22 other events, 54.0 us)
Sparse Core Ops, SparseCore 0:
  10.8 58.1 all-gather.9
  70.6 66.5 all-gather.7
  138.8 64.2 all-gather.11
  204.5 64.2 all-gather.13
  390.0 64.9 reduce-scatter.6
  457.2 66.5 reduce-scatter.12
  568.5 62.9 reduce-scatter.8
  633.9 56.2 reduce-scatter.14
  692.5 62.1 reduce-scatter.16
  756.9 54.6 reduce-scatter.10

commit v3 on v2

--- a/solution.py
+++ b/solution.py
@@ -457,18 +457,6 @@
     )(*parts, small, passed)
 
 
-def share_kernel(ny, weight, act, wide, wide_act, *refs):
-    send_far, recv_far, send, recv, local_sem, room, act_room = refs
-    s, c, rank = quad_here()
-    greet([(flip(s, d), c) for d in (1, 2)] + far_peers(s, c, ny))
-    far = Far(weight, wide, send_far, recv_far, room, local_sem.at[1], s, c, ny)
-    rows = Share(act, wide_act, send, recv, act_room, local_sem.at[0], s, c, rank)
-    far.forward()
-    rows.forward()
-    rows.finish()
-    far.finish()
-
-
 def share_scratch(weight, act, ny):
     return [
         pltpu.SemaphoreType.DMA((ny - 1,)),
@@ -481,23 +469,131 @@
     ]
 
 
-def share_rows(weight, act, ny):
+def hidden_kernel(ny, weight, act, fc_hbm, cot_hbm, bias, wide, act_out, g_out, slope_out, proj_out, *refs):
+    acts, w_fc, cot, bent, slope, grad_proj = refs[:6]
+    send_far, recv_far, send, recv, far_sem, load_sem, out_sem, room = refs[6:]
+    s, c, rank = quad_here()
+    rows = acts.shape[1]
+    loads = [
+        pltpu.make_async_copy(src, dst, load_sem.at[i])
+        for i, (src, dst) in enumerate(((act, acts.at[rank]), (fc_hbm, w_fc), (cot_hbm, cot)))
+    ]
+    for load in loads:
+        load.start()
+    greet([(flip(s, d), c) for d in (1, 2)] + far_peers(s, c, ny))
+    far = Far(weight, wide, send_far, recv_far, room, far_sem, s, c, ny)
+    loads[0].wait()
+    copies = []
+
+    def push(d):
+        hop = 2 if d == 2 else 1
+        block = acts.at[flip(rank, d - hop)]
+        copy = remote(block, block, send.at[d], recv.at[d], (flip(s, hop), c))
+        copy.start()
+        copies.append(copy)
+
+    def arrived(d):
+        block = acts.at[flip(rank, d)]
+        remote(block, block, send.at[d], recv.at[d], (s, c)).wait_recv()
+
+    push(2)
+    push(1)
+    loads[1].wait()
+    far.forward()
+
+    def hidden(d):
+        block = flip(rank, d)
+
+        def step(i, carry):
+            at = pl.ds(pl.multiple_of(i * 128, 128), 128)
+            h = mm(acts[block, at, :], w_fc[...], NN) + bias[...]
+            tanh = jnp.tanh(0.7978845608028654 * (h + 0.044715 * h * h * h))
+            to = pl.ds(pl.multiple_of(block * rows + i * 128, 128), 128)
+            bent[to, :] = (0.5 * h * (1.0 + tanh)).astype(BF)
+            slope[to, :] = 0.5 * (1.0 + tanh) + 0.5 * h * (
+                1.0 - tanh * tanh
+            ) * 0.7978845608028654 * (1.0 + 3.0 * 0.044715 * h * h)
+            return carry
+
+        lax.fori_loop(0, rows // 128, step, 0)
+
+    hidden(0)
+    arrived(1)
+    hidden(1)
+    arrived(2)
+    push(3)
+    hidden(2)
+    arrived(3)
+    writes = [
+        pltpu.make_async_copy(acts.at[t], act_out.at[t], out_sem.at[t]) for t in range(TP)
+    ]
+    for write in writes:
+        write.start()
+    hidden(3)
+    more = [
+        pltpu.make_async_copy(bent, g_out, out_sem.at[TP]),
+        pltpu.make_async_copy(slope, slope_out, out_sem.at[TP + 1]),
+    ]
+    for write in more:
+        write.start()
+    loads[2].wait()
+    width = bent.shape[1]
+
+    def proj_step(i, carry):
+        at = pl.ds(pl.multiple_of(i * 256, 256), 256)
+        grad_proj[at, :] = mm(bent[:, at], cot[...], TN).astype(BF)
+        return carry
+
+    lax.fori_loop(0, width // 256, proj_step, 0)
+    if width % 256:
+        at = pl.ds(width // 256 * 256, width % 256)
+        grad_proj[at, :] = mm(bent[:, at], cot[...], TN).astype(BF)
+    more.append(pltpu.make_async_copy(grad_proj, proj_out, out_sem.at[TP + 2]))
+    more[-1].start()
+    far.finish()
+    for copy in copies:
+        copy.wait_send()
+    for write in writes + more:
+        write.wait()
+
+
+def hidden_rows(weight, act, w_fc, cot, bias, ny):
     any_spec = pl.BlockSpec(memory_space=pl.ANY)
+    rows, width = act.shape
+    hq = w_fc.shape[1]
     return pl.pallas_call(
-        functools.partial(share_kernel, ny),
+        functools.partial(hidden_kernel, ny),
         out_shape=[
             jax.ShapeDtypeStruct((ny,) + weight.shape, BF),
-            jax.ShapeDtypeStruct((TP,) + act.shape, BF),
+            jax.ShapeDtypeStruct((TP, rows, width), BF),
+            jax.ShapeDtypeStruct((TP * rows, hq), BF),
+            jax.ShapeDtypeStruct((TP * rows, hq), F32),
+            jax.ShapeDtypeStruct((hq, cot.shape[1]), BF),
         ],
-        in_specs=[any_spec] * 2,
-        out_specs=[any_spec] * 2,
-        scratch_shapes=share_scratch(weight, act, ny),
+        in_specs=[any_spec] * 4 + [pl.BlockSpec(memory_space=pltpu.VMEM)],
+        out_specs=[any_spec] * 5,
+        scratch_shapes=[
+            pltpu.VMEM((TP, rows, width), BF),
+            pltpu.VMEM(w_fc.shape, BF),
+            pltpu.VMEM(cot.shape, BF),
+            pltpu.VMEM((TP * rows, hq), BF),
+            pltpu.VMEM((TP * rows, hq), F32),
+            pltpu.VMEM((hq, cot.shape[1]), BF),
+            pltpu.SemaphoreType.DMA((ny - 1,)),
+            pltpu.SemaphoreType.DMA((ny - 1,)),
+            pltpu.SemaphoreType.DMA((TP,)),
+            pltpu.SemaphoreType.DMA((TP,)),
+            pltpu.SemaphoreType.DMA((2,)),
+            pltpu.SemaphoreType.DMA((3,)),
+            pltpu.SemaphoreType.DMA((TP + 3,)),
+            pltpu.VMEM(weight.shape, BF),
+        ],
         compiler_params=pltpu.CompilerParams(
             collective_id=3, has_side_effects=True, vmem_limit_bytes=VMEM_BYTES
         ),
         cost_estimate=exchange_cost(60),
-        name="share_rows",
-    )(weight, act)
+        name="hidden_rows",
+    )(weight, act, w_fc, cot, bias)
 
 
 def sum_scratch(act):
@@ -963,28 +1059,20 @@
     proj_z = behind(token, proj_z).reshape(nc, TP * hs, oc)
     proj_rows = jnp.concatenate([proj_z[b] for b in range(nc)], axis=1)
     pack_hs = 8 if hs % 8 == 0 else 4
-    w_proj, act_wide = share_rows(
-        proj_rows.reshape(TP * hs // pack_hs, pack_hs, D), act_two.reshape(act_pack), ny
-    )
     w_fc = w_fc.reshape(D, hq)
-    w_proj = w_proj.reshape(hq, D)
-    act_wide = act_wide.reshape(TP * rows, D)
     cot_wide = cot_wide.reshape(TP * rows, D)
     fc_bias = lax.dynamic_index_in_dim(
         small[7 : 7 + FF // D].reshape(ns, TP, hs), rank, axis=1, keepdims=False
-    ).reshape(hq)
-    hidden = mm(act_wide, w_fc, NN) + fc_bias
-    cube = 0.7978845608028654 * (hidden + 0.044715 * hidden * hidden * hidden)
-    bent = jnp.tanh(cube)
-    act_three = (0.5 * hidden * (1.0 + bent)).astype(BF)
-    slope = 0.5 * (1.0 + bent) + 0.5 * hidden * (1.0 - bent * bent) * 0.7978845608028654 * (
-        1.0 + 3.0 * 0.044715 * hidden * hidden
-    )
-    grad_hidden = (mm(cot_wide, w_proj, NT) * slope).astype(BF)
-    grad_proj = mm(act_three, cot_wide, TN).astype(BF)
+    ).reshape(1, hq)
+    w_proj, act_wide, act_three, slope, grad_proj = hidden_rows(
+        proj_rows.reshape(TP * hs // pack_hs, pack_hs, D), act_two, w_fc, cot_wide, fc_bias, ny
+    )
+    w_proj = w_proj.reshape(hq, D)
+    act_wide = act_wide.reshape(TP * rows, D)
     proj_far = lax.psum_scatter(
         grad_proj, "shard", scatter_dimension=0, tiled=True, axis_index_groups=far_groups
     )
+    grad_hidden = (mm(cot_wide, w_proj, NT) * slope).astype(BF)
     mid_sum, out_part, grad_fc = middle_rows(grad_hidden, w_fc, act_three, w_proj, act_wide)
     grad_fc_bias = jnp.sum(grad_hidden, axis=0, dtype=F32)
     fc_far = lax.psum_scatter(

time: 832 us -> 801 us (0.963)
  matrix products: 154 us -> 123 us
    dot_general x15 -> x13, matrix products: 154 us -> 123 us  [mm(): return lax.dot_general(left, right, dims, preferred_element_type=F32)]
  transfers between devices with their start and end apart: 10 -> 10, of which waited for: 3 -> 3; matrix products, arithmetic and copies ran while one was open for 31% -> 33% of each run, Pallas kernels for 48% -> 50%
where the time goes in v3:
time: 801 us; the launch traced here: 794 us
  Pallas kernels  454 us (57%)
  matrix products  123 us (15%)
  local copies, waits for them, and re-layouts  94.1 us (12%)
  other arithmetic  72.9 us (9%)
  waiting for transfers between devices  32.9 us (4%)
  between operations  16.9 us (2%)
    dot_general x13, matrix products, mm(): return lax.dot_general(left, right, dims, preferred_element_type=F32)  123 us
    pallas_call x1, Pallas kernels, scatter_rows(): pl.pallas_call(functools.partial(scatter_kernel, ns, n), out_shape=[jax.S...  94.5 us
    pallas_call x1, Pallas kernels, gather_rows(): pl.pallas_call(functools.partial(gather_kernel, ns), out_shape=[jax.Shape...  94.3 us
    pallas_call x1, Pallas kernels, attend_forward(): pl.pallas_call(functools.partial(attend_kernel, ny), out_shape=[jax.Shape...  67.4 us
    pallas_call x1, Pallas kernels, hidden_rows(): pl.pallas_call(functools.partial(hidden_kernel, ny), out_shape=[jax.Shape...  60.7 us
    pallas_call x1, Pallas kernels, attend_backward(): pl.pallas_call(attend_back_kernel, out_shape=[jax.ShapeDtypeStruct(x.shap...  50.6 us
    pallas_call x1, Pallas kernels, middle_rows(): pl.pallas_call(middle_kernel, out_shape=[jax.ShapeDtypeStruct((rows, widt...  42.1 us
    all_gather x1, waiting for transfers between devices, local(): attn_z = lax.all_gather(attn_block, 'ctx', axis=0)  26.4 us
  transfers between devices with their start and end apart: 10, of which 3 were waited for; matrix products, arithmetic and copies ran while one was open for 33% of the time, Pallas kernels for 50%

profile of v3, /device:TPU:0, one launch (start us, length us, event | category | flops | bytes accessed | tf_op | source)
XLA Modules:
  0.0 794.3 jit_solution(18298263716618228276)
XLA Ops:
  18.6 23.9 %first_exchange.1 = (bf16[4,200,400]{2,1,0:T(8,128)(2,1)}, bf16[4,200,400]{2,1,0:T(8,128)(2,1)}, bf16[8,12,200]{2,1,0:T(8,128)(2,1)}, bf16[256,1600]{1,0:T(8,128)(2,1)}) custom-call(bf16[4,200,400]{2,1,0:T(8,128)(2,1)} %reshape.395.refs_0_, bf16[4,200,400]{2,1,0:T(8,128)(2,1)} %bitcast.126, bf16[12,200]{1,0:T(8,128)(2,1)} %convert_element_type.143.refs_2_, ...), custom_call_target="tpu_custom_call" | custom-call | bytes 75000000 | tf_op jit(solution)/shard_map/first_exchange/pallas_call | solution.py:436
  42.6 26.4 %all-gather.10.cloned.1.call-done = bf16[800,1600]{1,0:T(8,128)(2,1)} async-done(((bf16[200,1600]{1,0:T(8,128)(2,1)}), bf16[800,1600]{1,0:T(8,128)(2,1)}) %all-gather.10.cloned.1.call-update) | async-done | bytes 2560016 | tf_op jit(solution)/shard_map/all_gather | solution.py:1002
  81.6 94.3 %gather_rows.1 = (bf16[8,25,8,1600]{3,2,1,0:T(8,128)(2,1)}, bf16[8,25,8,1600]{3,2,1,0:T(8,128)(2,1)}, bf16[8,25,8,1600]{3,2,1,0:T(8,128)(2,1)}, bf16[8,25,8,1600]{3,2,1,0:T(8,128)(2,1)}, s32[1]{0:T(128)}) custom-call(bf16[25,8,1600]{2,1,0:T(8,128)(2,1)} %get-tuple-element.251.refs_0_, bf16[25,8,1600]{2,1,0:T(8,128)(2,1)} %pad_maximum_fusion.7.refs_1_, ...), custom_call_target="tpu_custom_call" | custom-call | bytes 285000000 | tf_op jit(solution)/shard_map/gather_rows/pallas_call | solution.py:138
  176.6 2.8 convert_reduce_fusion.1
  180.9 2.6 fusion.5
  183.5 9.3 %convolution_convert_fusion.4.refs_1_ = bf16[1152,1600]{1,0:T(8,128)(2,1)} fusion(bf16[1152,1600]{1,0:T(8,128)(2,1)S(1)} %fusion.5, bf16[1600,1600]{1,0:T(8,128)(2,1)S(1)} %bitcast.158), kind=kOutput, calls=%fused_computation.19 | convolution fusion | flops 5900083200 | bytes 12492800 | tf_op jit(solution)/shard_map/dot_general | solution.py:770
  192.9 3.8 fusion.19.refs_0_
  196.7 9.5 %fusion.8.refs_2_ = bf16[1152,1600]{1,0:T(8,128)(2,1)} fusion(bf16[1152,1600]{1,0:T(8,128)(2,1)S(1)} %fusion.5, bf16[1600,1600]{1,0:T(8,128)(2,1)S(1)} %bitcast.154, f32[1600]{0:T(1024)S(1)} %add.302), kind=kOutput, calls=%fused_computation.14 | convolution fusion | flops 5901926400 | bytes 12499200 | tf_op jit(solution)/shard_map/dot_general | solution.py:770
  209.5 5.3 concatenate.135.refs_4_
  214.7 67.4 %attend_forward.1 = (bf16[384,1600]{1,0:T(8,128)(2,1)}, f32[25,384,1]{2,1,0:T(8,128)}, bf16[2,100,8,1600]{3,2,1,0:T(8,128)(2,1)}, bf16[4,48,8,1600]{3,2,1,0:T(8,128)(2,1)}, s32[1]{0:T(128)}) custom-call(bf16[384,1600]{1,0:T(8,128)(2,1)} %fusion.19.refs_0_, bf16[1152,1600]{1,0:T(8,128)(2,1)} %convolution_convert_fusion.4.refs_1_, ...), custom_call_target="tpu_custom_call" | custom-call | bytes 180000000 | tf_op jit(solution)/shard_map/attend_forward/pallas_call | solution.py:839
  287.8 5.3 fusion.74
  295.2 5.9 concatenate.140.weight
  301.1 60.7 %hidden_rows.1 = (bf16[2,100,8,1600]{3,2,1,0:T(8,128)(2,1)}, bf16[4,384,1600]{2,1,0:T(8,128)(2,1)}, bf16[1536,1600]{1,0:T(8,128)(2,1)}, f32[1536,1600]{1,0:T(8,128)}, bf16[1600,1600]{1,0:T(8,128)(2,1)}) custom-call(bf16[100,8,1600]{2,1,0:T(8,128)(2,1)} %concatenate.140.weight, bf16[384,1600]{1,0:T(8,128)(2,1)} %add_convert_fusion.act, ...), custom_call_target="tpu_custom_call" | custom-call | bytes 180000000 | tf_op jit(solution)/shard_map/hidden_rows/pallas_call | solution.py:564
  361.8 17.8 %convert_reduce_fusion = (bf16[1600]{0:T(1024)(128)(2,1)S(1)}, bf16[1536,1600]{1,0:T(8,128)(2,1)}) fusion(f32[1536,1600]{1,0:T(8,128)} %get-tuple-element.73, bf16[1536,1600]{1,0:T(8,128)(2,1)} %bitcast.116, bf16[1600,1600]{1,0:T(8,128)(2,1)} %bitcast.112), kind=kOutput, calls=%fused_computation | convolution fusion | flops 7874148864 | bytes 24784000 | tf_op jit(solution)/shard_map/dot_general | solution.py:770
  379.6 42.1 %middle_rows.1 = (bf16[384,1600]{1,0:T(8,128)(2,1)}, bf16[1536,1600]{1,0:T(8,128)(2,1)}, bf16[1600,1600]{1,0:T(8,128)(2,1)}) custom-call(bf16[1536,1600]{1,0:T(8,128)(2,1)} %get-tuple-element.250.refs_0_, bf16[1600,1600]{1,0:T(8,128)(2,1)} %bitcast.103, bf16[1536,1600]{1,0:T(8,128)(2,1)} %get-tuple-element.74.refs_2_, bf16[1600,1600]{1,0:T(8,128)(2,1)} %bitcast.113, ...), custom_call_target="tpu_custom_call" | custom-call | bytes 150000000 | tf_op jit(solution)/shard_map/middle_rows/pallas_call | solution.py:706
  421.8 2.5 and_select_fusion.refs_5_
  424.4 3.8 reduce.13
  428.8 2.5 fusion.30
  434.1 7.3 convolution_convert_fusion.5
  441.4 2.5 copy.136.refs_3_
  443.9 5.3 copy.134
  449.2 4.6 copy.135
  453.8 50.6 %attend_backward.1 = (bf16[384,1600]{1,0:T(8,128)(2,1)}, bf16[1152,1600]{1,0:T(8,128)(2,1)}, bf16[1152,1600]{1,0:T(8,128)(2,1)}, bf16[48,8,1600]{2,1,0:T(8,128)(2,1)}) custom-call(bf16[384,1600]{1,0:T(8,128)(2,1)} %fusion.19.refs_0_, bf16[1152,1600]{1,0:T(8,128)(2,1)} %convolution_convert_fusion.4.refs_1_, bf16[1152,1600]{1,0:T(8,128)(2,1)} %fusion.8.refs_2_, ...), custom_call_target="tpu_custom_call" | custom-call | bytes 141000000 | tf_op jit(solution)/shard_map/attend_backward/pallas_call | solution.py:906
  504.4 13.4 %fusion.76 = f32[1152,1600]{1,0:T(8,128)} fusion(bf16[1152,1600]{1,0:T(8,128)(2,1)} %get-tuple-element.82, bf16[1600,1600]{1,0:T(8,128)(2,1)} %bitcast.155), kind=kOutput, calls=%fused_computation.178 | convolution fusion | flops 5898240000 | bytes 16179200 | tf_op jit(solution)/shard_map/dot_general | solution.py:770
  517.8 15.1 %fusion.53 = (f32[1600]{0:T(1024)S(1)}, f32[1600]{0:T(1024)S(1)}, f32[1152,1600]{1,0:T(8,128)}) fusion(f32[1152]{0:T(1024)S(1)} %add_rsqrt_fusion, f32[1152]{0:T(1024)S(1)} %broadcast_multiply_fusion, bf16[128,1600]{1,0:T(8,128)(2,1)S(1)} %slice.218, bf16[1024,1600]{1,0:T(8,128)(2,1)S(1)} %copy-done.5, f32[1152,1600]{1,0:T(8,128)} %fusion.76, ...), kind=kOutput, calls=%fused_computation.165 | convolution fusion | flops 5916668928 | bytes 27260416 | tf_op jit(solution)/shard_map/dot_general | solution.py:770
  532.9 5.0 slice.288
  538.1 5.3 copy.142
  549.2 7.7 convolution_convert_fusion
  556.9 5.5 convolution_convert_fusion.3
  562.3 4.6 fusion.75
  566.9 10.3 %convolution_convert_fusion.1 = bf16[1600,1600]{1,0:T(8,128)(2,1)} fusion(bf16[1152,1600]{1,0:T(8,128)(2,1)S(1)} %copy-done.9, bf16[1152,1600]{1,0:T(8,128)(2,1)S(1)} %copy-done.18), kind=kOutput, calls=%fused_computation.16 | convolution fusion | flops 5900800000 | bytes 12492800 | tf_op jit(solution)/shard_map/dot_general | solution.py:770
  578.9 2.8 reduce.2
  583.1 3.5 copy.139
  586.7 13.0 %convolution_convert_fusion.2 = bf16[1600,1600]{1,0:T(8,128)(2,1)} fusion(bf16[1152,1600]{1,0:T(8,128)(2,1)} %copy-done.8, bf16[1152,1600]{1,0:T(8,128)(2,1)} %get-tuple-element.82), kind=kOutput, calls=%fused_computation.17 | convolution fusion | flops 5900800000 | bytes 12492800 | tf_op jit(solution)/shard_map/dot_general | solution.py:770
  601.9 3.8 fusion.54
  606.9 94.5 %scatter_rows.1 = (bf16[25,8,1600]{2,1,0:T(8,128)(2,1)}, bf16[25,8,1600]{2,1,0:T(8,128)(2,1)}, bf16[25,8,1600]{2,1,0:T(8,128)(2,1)}, bf16[25,8,1600]{2,1,0:T(8,128)(2,1)}, bf16[1,8,1600]{2,1,0:T(8,128)(2,1)}) custom-call(bf16[8,25,8,1600]{3,2,1,0:T(8,128)(2,1)} %bitcast.109, bf16[8,25,8,1600]{3,2,1,0:T(8,128)(2,1)} %bitcast.111, ...), custom_call_target="tpu_custom_call" | custom-call | bytes 285000000 | tf_op jit(solution)/shard_map/scatter_rows/pallas_call | solution.py:234
  719.8 2.6 fusion.33
  722.5 2.6 copy.148
  727.4 4.7 fusion.23
  732.1 3.2 copy.149
  735.4 20.9 %last_exchange.1 = (bf16[4,200,400]{2,1,0:T(8,128)(2,1)}, bf16[4,200,400]{2,1,0:T(8,128)(2,1)}) custom-call(bf16[4,200,400]{2,1,0:T(8,128)(2,1)} %bitcast.121, bf16[4,200,400]{2,1,0:T(8,128)(2,1)} %bitcast.135, bf16[1,8,1600]{2,1,0:T(8,128)(2,1)} %get-tuple-element.88.refs_2_), custom_call_target="tpu_custom_call" | custom-call | bytes 60000000 | tf_op jit(solution)/shard_map/last_exchange/pallas_call | solution.py:747
  756.2 3.1 reshape.425
  760.4 2.8 reshape.423
  766.4 5.3 fusion.58
  771.8 2.9 fusion.60
  774.7 5.7 reduce-scatter.11.cloned.1.call-done
  781.2 2.8 fusion.62
  784.1 2.3 fusion.65
  (249 shorter events, 77.9 us)
Async XLA Ops:
  7.2 3.5 copy-start.37
  7.2 4.1 copy-start.12
  7.2 61.8 %all-gather.10.cloned.1.call-start = ((), (), s32[]{:S(2)}) async-start(), calls=%async_computation.13 | async-start | bytes 3328000 | tf_op jit(solution)/shard_map/all_gather | solution.py:1002
  10.7 165.9 %all-gather.8.cloned.1.call-start = ((), (), s32[]{:S(2)}) async-start(), calls=%async_computation.6 | async-start | bytes 4259840 | tf_op jit(solution)/shard_map/all_gather | solution.py:1012
  11.4 3.3 copy-start.10
  17.6 51.5 %copy-start = (bf16[384,1600]{1,0:T(8,128)(2,1)}, bf16[384,1600]{1,0:T(8,128)(2,1)S(1)}, u32[]{:S(2)}) copy-start(bf16[384,1600]{1,0:T(8,128)(2,1)S(1)} %copy.121) | copy-start | bytes 3686404
  18.6 52.6 %copy-start.16 = (bf16[384,1600]{0,1:T(8,128)(2,1)S(1)}, bf16[384,1600]{0,1:T(8,128)(2,1)}, u32[]{:S(2)}) copy-start(bf16[384,1600]{0,1:T(8,128)(2,1)} %param.18) | copy-start | bytes 3686404
  42.5 26.6 %copy-start.36 = (bf16[8,12,200]{2,1,0:T(8,128)(2,1)S(1)}, bf16[8,12,200]{2,1,0:T(8,128)(2,1)}, u32[]{:S(2)}) copy-start(bf16[8,12,200]{2,1,0:T(8,128)(2,1)} %get-tuple-element.58) | copy-start | bytes 115204
  42.6 163.6 %all-gather.12.cloned.1.call-start = ((), (), s32[]{:S(2)}) async-start(), calls=%async_computation.14 | async-start | bytes 4096000 | tf_op jit(solution)/shard_map/all_gather | solution.py:1013
  69.0 213.8 %all-gather.14.cloned.1.call-start = ((), (), s32[]{:S(2)}) async-start(), calls=%async_computation.15 | async-start | bytes 4096000 | tf_op jit(solution)/shard_map/all_gather | solution.py:1014
  70.8 110.1 %copy-start.34 = (f32[1600]{0:T(1024)}, f32[1600]{0:T(1024)S(1)}, u32[]{:S(2)}) copy-start(f32[1600]{0:T(1024)S(1)} %mul.297) | copy-start | bytes 19204
  78.4 365.5 %reduce-scatter.7.cloned.1.call-start = ((), (), s32[]{:S(2)}) async-start(), calls=%async_computation.7 | async-start | bytes 7987200 | tf_op jit(solution)/shard_map/reduce_scatter | solution.py:1072
  176.6 3.1 copy-start.4
  176.6 6.9 slice-start.6
  180.9 12.0 %slice-start = ((s8[5324800]{0:T(1024)(128)(4,1)}), s8[1130496]{0:T(1024)(128)(4,1)S(1)}, s32[]{:S(2)}) async-start(s8[5324800]{0:T(1024)(128)(4,1)} %bitcast.145), calls=%async_computation.16 | async-start | bytes 2260992
  183.4 13.2 %copy-start.8 = (bf16[1152,1600]{1,0:T(8,128)(2,1)}, bf16[1152,1600]{1,0:T(8,128)(2,1)S(1)}, u32[]{:S(2)}) copy-start(bf16[1152,1600]{1,0:T(8,128)(2,1)S(1)} %fusion.5) | copy-start | bytes 11059204
  183.5 9.4 %slice-start.1 = ((s8[5324800]{0:T(1024)(128)(4,1)}), s8[4194304]{0:T(1024)(128)(4,1)S(1)}, s32[]{:S(2)}) async-start(s8[5324800]{0:T(1024)(128)(4,1)} %bitcast.145), calls=%async_computation.17 | async-start | bytes 8388608
  192.8 3.9 copy-start.29
  192.8 3.9 slice-start.4
  192.9 3.8 slice-start.5
  285.0 2.9 copy-start.42
  361.8 176.3 %reduce-scatter.13.cloned.1.call-start = ((), (), s32[]{:S(2)}) async-start(), calls=%async_computation.10 | async-start | bytes 7987200 | tf_op jit(solution)/shard_map/reduce_scatter | solution.py:1078
  421.8 178.5 %reduce-scatter.9.cloned.1.call-start = ((), (), s32[]{:S(2)}) async-start(), calls=%async_computation.8 | async-start | bytes 4259840 | tf_op jit(solution)/shard_map/reduce_scatter | solution.py:1100
  428.2 3.2 copy-start.6
  428.2 3.2 copy-start.15
  504.4 13.4 %copy-start.5 = (bf16[1024,1600]{1,0:T(8,128)(2,1)S(1)}, bf16[1024,1600]{1,0:T(8,128)(2,1)}, u32[]{:S(2)}) copy-start(bf16[1024,1600]{1,0:T(8,128)(2,1)} %all-gather.8.cloned.1.call-done) | copy-start | bytes 9830404
  538.0 187.1 %reduce-scatter.15.cloned.1.call-start = ((), (), s32[]{:S(2)}) async-start(), calls=%async_computation.11 | async-start | bytes 3584000 | tf_op jit(solution)/shard_map/reduce_scatter | solution.py:1084
  543.3 192.0 %reduce-scatter.17.cloned.1.call-start = ((), (), s32[]{:S(2)}) async-start(), calls=%async_computation.12 | async-start | bytes 4096000 | tf_op jit(solution)/shard_map/reduce_scatter | solution.py:1082
  549.1 7.7 copy-start.24
  549.1 7.7 copy-start.30
  549.1 13.2 %slice-start.2 = ((s8[5324800]{0:T(1024)(128)(4,1)}), s8[4194304]{0:T(1024)(128)(4,1)S(1)}, s32[]{:S(2)}) async-start(s8[5324800]{0:T(1024)(128)(4,1)} %bitcast.148), calls=%async_computation.18 | async-start | bytes 8388608
  556.9 5.5 slice-start.3
  562.3 4.6 copy-start.9
  562.3 4.6 copy-start.18
  577.3 203.1 %reduce-scatter.11.cloned.1.call-start = ((), (), s32[]{:S(2)}) async-start(), calls=%async_computation.9 | async-start | bytes 3461120 | tf_op jit(solution)/shard_map/reduce_scatter | solution.py:1154
  701.4 7.4 copy-start.28
  701.4 8.4 %copy-start.32 = (bf16[25,8,1600]{2,1,0:T(8,128)(2,1)S(1)}, bf16[25,8,1600]{2,1,0:T(8,128)(2,1)}, u32[]{:S(2)}) copy-start(bf16[25,8,1600]{2,1,0:T(8,128)(2,1)} %get-tuple-element.86) | copy-start | bytes 1920004
  710.8 6.3 copy-start.33
  722.5 4.9 copy-start.3
  763.3 3.1 copy-start.11
  766.3 5.4 copy-start.13
  766.4 5.4 copy-start.14
  766.4 5.4 copy-start.22
  766.4 5.4 copy-start.23
  771.7 9.5 %copy-start.21 = (f32[200,400]{1,0:T(8,128)S(1)}, f32[200,400]{1,0:T(8,128)}, u32[]{:S(2)}) copy-start(f32[200,400]{1,0:T(8,128)} %param.20) | copy-start | bytes 960004
  771.7 12.3 %copy-start.27 = (f32[200,1200]{1,0:T(8,128)S(1)}, f32[200,1200]{1,0:T(8,128)}, u32[]{:S(2)}) copy-start(f32[200,1200]{1,0:T(8,128)} %param.29) | copy-start | bytes 2880004
  774.7 9.3 %copy-start.17 = (f32[200,1200]{1,0:T(8,128)S(1)}, f32[200,1200]{1,0:T(8,128)}, u32[]{:S(2)}) copy-start(f32[200,1200]{1,0:T(8,128)} %param.19) | copy-start | bytes 2880004
  774.7 9.3 %copy-start.26 = (f32[200,1200]{1,0:T(8,128)S(1)}, f32[200,1200]{1,0:T(8,128)}, u32[]{:S(2)}) copy-start(f32[200,1200]{1,0:T(8,128)} %param.24) | copy-start | bytes 2880004
  (13 other events, 26.7 us)
Sparse Core Ops, SparseCore 0:
  10.8 58.1 all-gather.9
  70.6 66.5 all-gather.7
  138.8 64.2 all-gather.11
  204.5 64.2 all-gather.13
  361.9 64.5 reduce-scatter.6
  428.7 66.5 reduce-scatter.12
  538.1 62.1 reduce-scatter.8
  602.6 56.3 reduce-scatter.14
  661.3 62.1 reduce-scatter.16
  725.6 54.6 reduce-scatter.10
